TPU v7x, 32 devices: a whole 2x2x4 slice. The times are simulated.
32 devices in a mesh: rows: 8 (over z, x), segment: 2 (over y), chan: 2 (over core).
Axes of the slice: x: 2, y: 2, z: 4, core: 2. Of those that a mesh axis runs over, the one named last changes fastest.
Arguments:
- features: bfloat16 [4, 8, 384, 128], P(None, 'rows', 'chan'), may hold values from -6 to 6
- caches: bfloat16 [2, 2, 2, 8, 384, 128], P('segment', None, None, 'rows', 'chan'), may hold values from -4 to 4
- conv_weights: bfloat16 [2, 2, 384, 3, 3, 3, 384], P('segment', None, 'chan'), may hold values from -0.0625 to 0.0625
- conv_bias: float32 [2, 2, 384], P('segment'), may hold values from -3 to 3
- norm_gain: float32 [2, 2, 384], P('segment'), may hold values from 0.25 to 1.75
Outputs:
- section_outputs: bfloat16 [2, 4, 8, 384, 128], P('segment', None, 'rows', 'chan')
- next_caches: bfloat16 [2, 2, 2, 8, 384, 128], P('segment', None, None, 'rows', 'chan')
All inputs are finite; a program needn't handle non-finite values.
Results may differ from a plain program's by a relative error of at most 0.0057.
Values may be sent and summed in bfloat16 or wider, within the bound.
No kernel may reach another device: no remote copies, remote signals or barrier semaphores. Data moves between devices by JAX's collectives and lax.ppermute only.
A program may use at most 64 MiB of HBM per device.

v0:
```python
import jax
import jax.numpy as jnp
from jax import lax
from jax.sharding import PartitionSpec as P


def padded_2(shard, sides, width):
    for axis, dim in sides:
        devices, length = (lax.axis_size(axis), shard.shape[dim])
        up = [(i, (i + 1) % devices) for i in range(devices - 1)]
        down = [(j, i) for i, j in up]
        last = lax.slice_in_dim(shard, length - width, length, axis=dim)
        first = lax.slice_in_dim(shard, 0, width, axis=dim)
        before = lax.ppermute(last, axis, up)
        after = lax.ppermute(first, axis, down)
        shard = jnp.concatenate([before, shard, after], axis=dim)
    return shard


def passed_along(shard, axis, by):
    devices = lax.axis_size(axis)
    pairs = [(i, i + by) for i in range(devices) if 0 <= i + by < devices]
    return lax.ppermute(shard, axis, pairs)


def normed_silu(source, gain):
    values = source.astype(jnp.float32)
    scale = lax.rsqrt(jnp.mean(values * values, axis=2, keepdims=True) + 1e-06)
    return jax.nn.silu(gain[:, None] * values * scale).astype(jnp.bfloat16)


def conv_input(source, gain):
    widened = lax.all_gather(source, "chan", axis=2, tiled=True)
    activated = normed_silu(widened, gain)
    return padded_2(activated, (("rows", 1),), 1)


def local_conv(window, kernel, offset):
    frame_count = window.shape[0] - 2
    row_count = window.shape[1] - 2
    col_count = window.shape[3]
    padded = jnp.pad(window, ((0, 0), (0, 0), (0, 0), (1, 1)))
    total = jnp.zeros((frame_count, row_count, kernel.shape[0], col_count), jnp.float32)
    for time_tap in range(3):
        for row_tap in range(3):
            for col_tap in range(3):
                shifted = padded[
                    time_tap : time_tap + frame_count,
                    row_tap : row_tap + row_count,
                    :,
                    col_tap : col_tap + col_count,
                ]
                tap_kernel = kernel[:, time_tap, row_tap, col_tap, :]
                total = total + jnp.einsum(
                    "oi,friw->frow", tap_kernel, shifted, preferred_element_type=jnp.float32
                )
    return total + offset[:, None]


def residual_block(block_input, cache_tails, kernels, offsets, gains):
    first_window = jnp.concatenate([cache_tails[0], conv_input(block_input, gains[0])], axis=0)
    middle = local_conv(first_window, kernels[0], offsets[0]).astype(jnp.bfloat16)
    second_window = jnp.concatenate([cache_tails[1], conv_input(middle, gains[1])], axis=0)
    product = local_conv(second_window, kernels[1], offsets[1])
    result = (block_input.astype(jnp.float32) + product).astype(jnp.bfloat16)
    return (result, [first_window[-2:], second_window[-2:]])


def shards(features, caches, conv_weights, conv_bias, norm_gain):
    segment_index = lax.axis_index("segment")
    segment_total = lax.axis_size("segment")
    chan_index = lax.axis_index("chan")
    width_dev = features.shape[2]
    kernels = conv_weights[0]
    offsets = lax.dynamic_slice_in_dim(conv_bias[0], chan_index * width_dev, width_dev, 1)
    gains = norm_gain[0]
    rimmed_cache = padded_2(caches[0], (("rows", 2),), 1)
    widened_cache = lax.all_gather(rimmed_cache, "chan", axis=3, tiled=True)
    cache_tails = [widened_cache[0], widened_cache[1]]
    group_frames = features.shape[0]
    group_count = features.shape[0] // group_frames
    period_total = group_count + segment_total - 1
    received = jnp.zeros_like(features)
    results = []
    for period in range(period_total):
        offset_now = period - segment_index
        active = jnp.logical_and(offset_now >= 0, offset_now < group_count)
        if period < group_count:
            local_frames = features
        else:
            local_frames = jnp.zeros_like(features)
        block_input = jnp.where(segment_index == 0, local_frames, received)
        result, new_tails = residual_block(block_input, cache_tails, kernels, offsets, gains)
        cache_tails = [
            jnp.where(active, fresh, older) for fresh, older in zip(new_tails, cache_tails)
        ]
        results.append(result)
        if period < period_total - 1:
            received = passed_along(result, "segment", 1)
    stacked = jnp.stack(results)
    mine = lax.dynamic_slice_in_dim(stacked, segment_index, group_count, 0)
    section_out = mine.reshape(features.shape)
    tails_all = jnp.stack(cache_tails)[:, :, 1:-1]
    tails_own = lax.dynamic_slice_in_dim(tails_all, chan_index * width_dev, width_dev, 3)
    return (section_out[None], tails_own[None])


def solution(mesh):
    in_specs = (
        P(None, "rows", "chan", None),
        P("segment", None, None, "rows", "chan", None),
        P("segment", None, "chan", None, None, None, None),
        P("segment", None, None),
        P("segment", None, None),
    )
    out_specs = (
        P("segment", None, "rows", "chan", None),
        P("segment", None, None, "rows", "chan", None),
    )
    return jax.shard_map(shards, mesh=mesh, in_specs=in_specs, out_specs=out_specs, check_vma=False)
```

profile of v0, /device:TPU:28, one launch (start us, length us, event | category | flops | bytes accessed | tf_op | source)
XLA Modules:
  0.0 185.2 jit_solution(354702324216350870)
XLA Ops:
  7.2 3.4 %collective-permute-start = (bf16[2,2,1,192,128]{4,3,1,2,0:T(8,128)(2,1)}, bf16[2,2,1,192,128]{4,3,1,2,0:T(8,128)(2,1)S(1)}, u32[]{:S(2)}, u32[]{:S(2)}) collective-permute-start(bf16[2,2,1,192,128]{4,3,1,2,0:T(8,128)(2,1)} %bitcast.1077), channel_id=1, source_target_pairs={{0,4},{4,8},{8,12},{12,16},{16,20},{20,24},{24,28},{1,5},{5,9},{9,... | collective-permute-start | bytes 589832 | tf_op jit(solution)/shard_map/ppermute | solution.py:14
  10.6 3.3 %collective-permute-start.1 = (bf16[2,2,1,192,128]{4,3,1,2,0:T(8,128)(2,1)}, bf16[2,2,1,192,128]{4,3,1,2,0:T(8,128)(2,1)S(1)}, u32[]{:S(2)}, u32[]{:S(2)}) collective-permute-start(bf16[2,2,1,192,128]{4,3,1,2,0:T(8,128)(2,1)} %bitcast.1078), channel_id=1, source_target_pairs={{4,0},{8,4},{12,8},{16,12},{20,16},{24,20},{28,24},{5,1},{9,5},{13... | collective-permute-start | bytes 589832 | tf_op jit(solution)/shard_map/ppermute | solution.py:15
  15.6 2.1 %all_gather.16 = bf16[4,1,384,128]{3,2,0,1:T(8,128)(2,1)S(1)} all-gather(bf16[4,1,192,128]{3,2,0,1:T(8,128)(2,1)S(1)} %bitcast_select_fusion), channel_id=1, replica_groups=mesh['rows'=8,'segment'=2,'chan'=2] {'chan'}, dimensions={2}, use_global_device_ids=true | all-gather | bytes 589824 | tf_op jit(solution)/shard_map/all_gather | solution.py:33
  18.6 2.5 %collective-permute-done.1 = bf16[2,2,1,192,128]{4,3,1,2,0:T(8,128)(2,1)S(1)} collective-permute-done((bf16[2,2,1,192,128]{4,3,1,2,0:T(8,128)(2,1)}, bf16[2,2,1,192,128]{4,3,1,2,0:T(8,128)(2,1)S(1)}, u32[]{:S(2)}, u32[]{:S(2)}) %collective-permute-start.1) | collective-permute-done | bytes 196640 | tf_op jit(solution)/shard_map/ppermute | solution.py:15
  23.2 1.9 %collective-permute-start.2 = (bf16[4,1,384,128]{3,2,0,1:T(8,128)(2,1)S(1)}, bf16[4,1,384,128]{3,2,0,1:T(8,128)(2,1)S(1)}, u32[]{:S(2)}, u32[]{:S(2)}) collective-permute-start(bf16[4,1,384,128]{3,2,0,1:T(8,128)(2,1)S(1)} %fusion.122), channel_id=1, source_target_pairs={{0,4},{4,8},{8,12},{12,16},{16,20},{20,24},{24,28},{1,5},{5,9},{9,... | collective-permute-start | bytes 1179656 | tf_op jit(solution)/shard_map/ppermute | solution.py:14
  25.2 4.8 %collective-permute-start.3 = (bf16[4,1,384,128]{3,2,0,1:T(8,128)(2,1)S(1)}, bf16[4,1,384,128]{3,2,0,1:T(8,128)(2,1)S(1)}, u32[]{:S(2)}, u32[]{:S(2)}) collective-permute-start(bf16[4,1,384,128]{3,2,0,1:T(8,128)(2,1)S(1)} %fusion.122), channel_id=1, source_target_pairs={{4,0},{8,4},{12,8},{16,12},{20,16},{24,20},{28,24},{5,1},{9,5},{13... | collective-permute-start | bytes 1179656 | tf_op jit(solution)/shard_map/ppermute | solution.py:15
  30.0 6.0 %slice_bitcast_fusion = (bf16[192,3,3,3,384]{4,0,3,2,1:T(8,128)(2,1)}, bf16[192,3,3,3,384]{4,0,3,2,1:T(8,128)(2,1)}) fusion(bf16[1,2,192,3,3,3,384]{6,2,5,4,3,1,0:T(8,128)(2,1)} %param.7), kind=kLoop, calls=%fused_computation.72 | loop fusion | bytes 15925248 | tf_op jit(solution)/shard_map/squeeze | solution.py:64
  37.3 8.2 %collective-permute-done.3 = bf16[4,1,384,128]{3,2,0,1:T(8,128)(2,1)S(1)} collective-permute-done((bf16[4,1,384,128]{3,2,0,1:T(8,128)(2,1)S(1)}, bf16[4,1,384,128]{3,2,0,1:T(8,128)(2,1)S(1)}, u32[]{:S(2)}, u32[]{:S(2)}) %collective-permute-start.3) | collective-permute-done | bytes 393248 | tf_op jit(solution)/shard_map/ppermute | solution.py:15
  59.4 2.2 %all_gather.17 = bf16[4,1,384,128]{3,2,0,1:T(8,128)(2,1)S(1)} all-gather(bf16[4,1,192,128]{3,2,0,1:T(8,128)(2,1)S(1)} %fusion.113), channel_id=1, replica_groups=mesh['rows'=8,'segment'=2,'chan'=2] {'chan'}, dimensions={2}, use_global_device_ids=true | all-gather | bytes 589824 | tf_op jit(solution)/shard_map/all_gather | solution.py:33
  62.0 1.9 %collective-permute-start.4 = (bf16[4,1,384,128]{3,2,0,1:T(8,128)(2,1)S(1)}, bf16[4,1,384,128]{3,2,0,1:T(8,128)(2,1)S(1)}, u32[]{:S(2)}, u32[]{:S(2)}) collective-permute-start(bf16[4,1,384,128]{3,2,0,1:T(8,128)(2,1)S(1)} %fusion.130), channel_id=1, source_target_pairs={{0,4},{4,8},{8,12},{12,16},{16,20},{20,24},{24,28},{1,5},{5,9},{9,... | collective-permute-start | bytes 1179656 | tf_op jit(solution)/shard_map/ppermute | solution.py:14
  63.9 5.0 %collective-permute-start.5 = (bf16[4,1,384,128]{3,2,0,1:T(8,128)(2,1)S(1)}, bf16[4,1,384,128]{3,2,0,1:T(8,128)(2,1)S(1)}, u32[]{:S(2)}, u32[]{:S(2)}) collective-permute-start(bf16[4,1,384,128]{3,2,0,1:T(8,128)(2,1)S(1)} %fusion.130), channel_id=1, source_target_pairs={{4,0},{8,4},{12,8},{16,12},{20,16},{24,20},{28,24},{5,1},{9,5},{13... | collective-permute-start | bytes 1179656 | tf_op jit(solution)/shard_map/ppermute | solution.py:15
  69.2 6.8 %collective-permute-done.4 = bf16[4,1,384,128]{3,2,0,1:T(8,128)(2,1)S(1)} collective-permute-done((bf16[4,1,384,128]{3,2,0,1:T(8,128)(2,1)S(1)}, bf16[4,1,384,128]{3,2,0,1:T(8,128)(2,1)S(1)}, u32[]{:S(2)}, u32[]{:S(2)}) %collective-permute-start.4) | collective-permute-done | bytes 393248 | tf_op jit(solution)/shard_map/ppermute | solution.py:14
  76.1 8.3 %collective-permute-done.5 = bf16[4,1,384,128]{3,2,0,1:T(8,128)(2,1)S(1)} collective-permute-done((bf16[4,1,384,128]{3,2,0,1:T(8,128)(2,1)S(1)}, bf16[4,1,384,128]{3,2,0,1:T(8,128)(2,1)S(1)}, u32[]{:S(2)}, u32[]{:S(2)}) %collective-permute-start.5) | collective-permute-done | bytes 393248 | tf_op jit(solution)/shard_map/ppermute | solution.py:15
  95.5 7.4 %collective-permute-done.6 = bf16[4,1,192,128]{3,2,0,1:T(8,128)(2,1)S(1)} collective-permute-done((bf16[4,1,192,128]{3,2,0,1:T(8,128)(2,1)S(1)}, bf16[4,1,192,128]{3,2,0,1:T(8,128)(2,1)S(1)}, u32[]{:S(2)}, u32[]{:S(2)}) %collective-permute-start.6) | collective-permute-done | bytes 196640 | tf_op jit(solution)/shard_map/ppermute | solution.py:23
  103.0 2.1 %all_gather.18 = bf16[4,1,384,128]{3,2,0,1:T(8,128)(2,1)S(1)} all-gather(bf16[4,1,192,128]{3,2,0,1:T(8,128)(2,1)S(1)} %broadcast_select_fusion), channel_id=1, replica_groups=mesh['rows'=8,'segment'=2,'chan'=2] {'chan'}, dimensions={2}, use_global_device_ids=true | all-gather | bytes 589824 | tf_op jit(solution)/shard_map/all_gather | solution.py:33
  105.5 1.9 %collective-permute-start.7 = (bf16[4,1,384,128]{3,2,0,1:T(8,128)(2,1)S(1)}, bf16[4,1,384,128]{3,2,0,1:T(8,128)(2,1)}, u32[]{:S(2)}, u32[]{:S(2)}) collective-permute-start(bf16[4,1,384,128]{3,2,0,1:T(8,128)(2,1)S(1)} %fusion.138), channel_id=1, source_target_pairs={{0,4},{4,8},{8,12},{12,16},{16,20},{20,24},{24,28},{1,5},{5,9},{9,... | collective-permute-start | bytes 1179656 | tf_op jit(solution)/shard_map/ppermute | solution.py:14
  107.4 5.0 %collective-permute-start.8 = (bf16[4,1,384,128]{3,2,0,1:T(8,128)(2,1)S(1)}, bf16[4,1,384,128]{3,2,0,1:T(8,128)(2,1)}, u32[]{:S(2)}, u32[]{:S(2)}) collective-permute-start(bf16[4,1,384,128]{3,2,0,1:T(8,128)(2,1)S(1)} %fusion.138), channel_id=1, source_target_pairs={{4,0},{8,4},{12,8},{16,12},{20,16},{24,20},{28,24},{5,1},{9,5},{13... | collective-permute-start | bytes 1179656 | tf_op jit(solution)/shard_map/ppermute | solution.py:15
  113.7 6.0 %collective-permute-done.7 = bf16[4,1,384,128]{3,2,0,1:T(8,128)(2,1)} collective-permute-done((bf16[4,1,384,128]{3,2,0,1:T(8,128)(2,1)S(1)}, bf16[4,1,384,128]{3,2,0,1:T(8,128)(2,1)}, u32[]{:S(2)}, u32[]{:S(2)}) %collective-permute-start.7) | collective-permute-done | bytes 393248 | tf_op jit(solution)/shard_map/ppermute | solution.py:14
  119.7 8.3 %collective-permute-done.8 = bf16[4,1,384,128]{3,2,0,1:T(8,128)(2,1)} collective-permute-done((bf16[4,1,384,128]{3,2,0,1:T(8,128)(2,1)S(1)}, bf16[4,1,384,128]{3,2,0,1:T(8,128)(2,1)}, u32[]{:S(2)}, u32[]{:S(2)}) %collective-permute-start.8) | collective-permute-done | bytes 393248 | tf_op jit(solution)/shard_map/ppermute | solution.py:15
  128.0 2.0 %fusion.151 = (bf16[1,2,3,384,128]{4,3,1,2,0:T(8,128)(2,1)}, bf16[2,3,384,128]{3,2,0,1:T(8,128)(2,1)S(1)}) fusion(bf16[4,1,384,128]{3,2,0,1:T(8,128)(2,1)} %collective-permute-done.8, bf16[4,1,384,128]{3,2,0,1:T(8,128)(2,1)S(1)} %fusion.138, bf16[4,1,384,128]{3,2,0,1:T(8,128)(2,1)} %collective-permute-done.7, pred[]{:T(512)S(6)} %and.9, ...), kind=kLoop, calls=%fused_computation.288 | loop fusion | flops 1769472 | bytes 4128770 | tf_op jit(solution)/shard_map/stack | solution.py:103
  142.9 2.1 %all_gather.19 = bf16[4,1,384,128]{3,2,0,1:T(8,128)(2,1)S(1)} all-gather(bf16[4,1,192,128]{3,2,0,1:T(8,128)(2,1)S(1)} %fusion.115), channel_id=1, replica_groups=mesh['rows'=8,'segment'=2,'chan'=2] {'chan'}, dimensions={2}, use_global_device_ids=true | all-gather | bytes 589824 | tf_op jit(solution)/shard_map/all_gather | solution.py:33
  145.4 1.9 %collective-permute-start.10 = (bf16[4,1,384,128]{3,2,0,1:T(8,128)(2,1)S(1)}, bf16[4,1,384,128]{3,2,0,1:T(8,128)(2,1)S(1)}, u32[]{:S(2)}, u32[]{:S(2)}) collective-permute-start(bf16[4,1,384,128]{3,2,0,1:T(8,128)(2,1)S(1)} %fusion.146), channel_id=1, source_target_pairs={{4,0},{8,4},{12,8},{16,12},{20,16},{24,20},{28,24},{5,1},{9,5},{13... | collective-permute-start | bytes 1179656 | tf_op jit(solution)/shard_map/ppermute | solution.py:15
  147.4 4.2 %collective-permute-start.9 = (bf16[4,1,384,128]{3,2,0,1:T(8,128)(2,1)S(1)}, bf16[4,1,384,128]{3,2,0,1:T(8,128)(2,1)S(1)}, u32[]{:S(2)}, u32[]{:S(2)}) collective-permute-start(bf16[4,1,384,128]{3,2,0,1:T(8,128)(2,1)S(1)} %fusion.146), channel_id=1, source_target_pairs={{0,4},{4,8},{8,12},{12,16},{16,20},{20,24},{24,28},{1,5},{5,9},{9,... | collective-permute-start | bytes 1179656 | tf_op jit(solution)/shard_map/ppermute | solution.py:14
  152.8 14.2 %collective-permute-done.10 = bf16[4,1,384,128]{3,2,0,1:T(8,128)(2,1)S(1)} collective-permute-done((bf16[4,1,384,128]{3,2,0,1:T(8,128)(2,1)S(1)}, bf16[4,1,384,128]{3,2,0,1:T(8,128)(2,1)S(1)}, u32[]{:S(2)}, u32[]{:S(2)}) %collective-permute-start.10) | collective-permute-done | bytes 393248 | tf_op jit(solution)/shard_map/ppermute | solution.py:15
  (170 shorter events, 58.1 us)
Async XLA Ops:
  7.2 40.7 %all-gather.2.cloned.1.call-start = ((), (), s32[]{:S(2)}) async-start(), calls=%async_computation | async-start | bytes 1769472 | tf_op jit(solution)/shard_map/all_gather | solution.py:78
  7.2 11.4 %collective-permute-start = (bf16[2,2,1,192,128]{4,3,1,2,0:T(8,128)(2,1)}, bf16[2,2,1,192,128]{4,3,1,2,0:T(8,128)(2,1)S(1)}, u32[]{:S(2)}, u32[]{:S(2)}) collective-permute-start(bf16[2,2,1,192,128]{4,3,1,2,0:T(8,128)(2,1)} %bitcast.1077), channel_id=1, source_target_pairs={{0,4},{4,8},{8,12},{12,16},{16,20},{20,24},{24,28},{1,5},{5,9},{9,... | collective-permute-start | bytes 589832 | tf_op jit(solution)/shard_map/ppermute | solution.py:14
  10.6 10.5 %collective-permute-start.1 = (bf16[2,2,1,192,128]{4,3,1,2,0:T(8,128)(2,1)}, bf16[2,2,1,192,128]{4,3,1,2,0:T(8,128)(2,1)S(1)}, u32[]{:S(2)}, u32[]{:S(2)}) collective-permute-start(bf16[2,2,1,192,128]{4,3,1,2,0:T(8,128)(2,1)} %bitcast.1078), channel_id=1, source_target_pairs={{4,0},{8,4},{12,8},{16,12},{20,16},{24,20},{28,24},{5,1},{9,5},{13... | collective-permute-start | bytes 589832 | tf_op jit(solution)/shard_map/ppermute | solution.py:15
  23.2 12.8 %copy-start.14 = (f32[1,2,384]{2,1,0:T(2,128)S(1)}, f32[1,2,384]{2,1,0:T(2,128)}, u32[]{:S(2)}) copy-start(f32[1,2,384]{2,1,0:T(2,128)} %param.8) | copy-start | bytes 9220
  23.2 23.4 %collective-permute-start.2 = (bf16[4,1,384,128]{3,2,0,1:T(8,128)(2,1)S(1)}, bf16[4,1,384,128]{3,2,0,1:T(8,128)(2,1)S(1)}, u32[]{:S(2)}, u32[]{:S(2)}) collective-permute-start(bf16[4,1,384,128]{3,2,0,1:T(8,128)(2,1)S(1)} %fusion.122), channel_id=1, source_target_pairs={{0,4},{4,8},{8,12},{12,16},{16,20},{20,24},{24,28},{1,5},{5,9},{9,... | collective-permute-start | bytes 1179656 | tf_op jit(solution)/shard_map/ppermute | solution.py:14
  25.2 20.3 %collective-permute-start.3 = (bf16[4,1,384,128]{3,2,0,1:T(8,128)(2,1)S(1)}, bf16[4,1,384,128]{3,2,0,1:T(8,128)(2,1)S(1)}, u32[]{:S(2)}, u32[]{:S(2)}) collective-permute-start(bf16[4,1,384,128]{3,2,0,1:T(8,128)(2,1)S(1)} %fusion.122), channel_id=1, source_target_pairs={{4,0},{8,4},{12,8},{16,12},{20,16},{24,20},{28,24},{5,1},{9,5},{13... | collective-permute-start | bytes 1179656 | tf_op jit(solution)/shard_map/ppermute | solution.py:15
  47.9 2.5 %copy-start.2 = (bf16[192,3,3,3,384]{4,0,3,2,1:T(8,128)(2,1)S(1)}, bf16[192,3,3,3,384]{4,0,3,2,1:T(8,128)(2,1)}, u32[]{:S(2)}) copy-start(bf16[192,3,3,3,384]{4,0,3,2,1:T(8,128)(2,1)} %get-tuple-element.11) | copy-start | bytes 11943940
  58.4 10.6 %copy-start = (bf16[192,3,3,3,384]{4,0,3,2,1:T(8,128)(2,1)S(1)}, bf16[192,3,3,3,384]{4,0,3,2,1:T(8,128)(2,1)}, u32[]{:S(2)}) copy-start(bf16[192,3,3,3,384]{4,0,3,2,1:T(8,128)(2,1)} %get-tuple-element.10) | copy-start | bytes 11943940
  62.0 14.1 %collective-permute-start.4 = (bf16[4,1,384,128]{3,2,0,1:T(8,128)(2,1)S(1)}, bf16[4,1,384,128]{3,2,0,1:T(8,128)(2,1)S(1)}, u32[]{:S(2)}, u32[]{:S(2)}) collective-permute-start(bf16[4,1,384,128]{3,2,0,1:T(8,128)(2,1)S(1)} %fusion.130), channel_id=1, source_target_pairs={{0,4},{4,8},{8,12},{12,16},{16,20},{20,24},{24,28},{1,5},{5,9},{9,... | collective-permute-start | bytes 1179656 | tf_op jit(solution)/shard_map/ppermute | solution.py:14
  63.9 20.4 %collective-permute-start.5 = (bf16[4,1,384,128]{3,2,0,1:T(8,128)(2,1)S(1)}, bf16[4,1,384,128]{3,2,0,1:T(8,128)(2,1)S(1)}, u32[]{:S(2)}, u32[]{:S(2)}) collective-permute-start(bf16[4,1,384,128]{3,2,0,1:T(8,128)(2,1)S(1)} %fusion.130), channel_id=1, source_target_pairs={{4,0},{8,4},{12,8},{16,12},{20,16},{24,20},{28,24},{5,1},{9,5},{13... | collective-permute-start | bytes 1179656 | tf_op jit(solution)/shard_map/ppermute | solution.py:15
  84.4 8.5 %copy-start.5 = (bf16[4,1,384,128]{3,2,0,1:T(8,128)(2,1)}, bf16[4,1,384,128]{3,2,0,1:T(8,128)(2,1)S(1)}, u32[]{:S(2)}) copy-start(bf16[4,1,384,128]{3,2,0,1:T(8,128)(2,1)S(1)} %collective-permute-done.5) | copy-start | bytes 1179652
  91.9 1.3 copy-start.11
  93.2 34.8 %copy-start.4 = (bf16[2,2,3,384,128]{4,3,1,2,0:T(8,128)(2,1)S(1)}, bf16[2,2,3,384,128]{4,3,1,2,0:T(8,128)(2,1)}, u32[]{:S(2)}) copy-start(bf16[2,2,3,384,128]{4,3,1,2,0:T(8,128)(2,1)} %all-gather.2.cloned.1.call-done) | copy-start | bytes 3538948
  94.2 1.3 copy-start.12
  94.2 8.7 %collective-permute-start.6 = (bf16[4,1,192,128]{3,2,0,1:T(8,128)(2,1)S(1)}, bf16[4,1,192,128]{3,2,0,1:T(8,128)(2,1)S(1)}, u32[]{:S(2)}, u32[]{:S(2)}) collective-permute-start(bf16[4,1,192,128]{3,2,0,1:T(8,128)(2,1)S(1)} %fusion.114), channel_id=1, source_target_pairs={{0,2},{1,3},{4,6},{5,7},{8,10},{9,11},{12,14},{13,15},{16,18},{17,... | collective-permute-start | bytes 589832 | tf_op jit(solution)/shard_map/ppermute | solution.py:23
  103.0 2.2 %copy-start.8 = (bf16[4,1,192,128]{3,2,0,1:T(8,128)(2,1)}, bf16[4,1,192,128]{3,2,0,1:T(8,128)(2,1)S(1)}, u32[]{:S(2)}) copy-start(bf16[4,1,192,128]{3,2,0,1:T(8,128)(2,1)S(1)} %broadcast_select_fusion) | copy-start | bytes 589828
  105.5 14.2 %collective-permute-start.7 = (bf16[4,1,384,128]{3,2,0,1:T(8,128)(2,1)S(1)}, bf16[4,1,384,128]{3,2,0,1:T(8,128)(2,1)}, u32[]{:S(2)}, u32[]{:S(2)}) collective-permute-start(bf16[4,1,384,128]{3,2,0,1:T(8,128)(2,1)S(1)} %fusion.138), channel_id=1, source_target_pairs={{0,4},{4,8},{8,12},{12,16},{16,20},{20,24},{24,28},{1,5},{5,9},{9,... | collective-permute-start | bytes 1179656 | tf_op jit(solution)/shard_map/ppermute | solution.py:14
  107.4 20.6 %collective-permute-start.8 = (bf16[4,1,384,128]{3,2,0,1:T(8,128)(2,1)S(1)}, bf16[4,1,384,128]{3,2,0,1:T(8,128)(2,1)}, u32[]{:S(2)}, u32[]{:S(2)}) collective-permute-start(bf16[4,1,384,128]{3,2,0,1:T(8,128)(2,1)S(1)} %fusion.138), channel_id=1, source_target_pairs={{4,0},{8,4},{12,8},{16,12},{20,16},{24,20},{28,24},{5,1},{9,5},{13... | collective-permute-start | bytes 1179656 | tf_op jit(solution)/shard_map/ppermute | solution.py:15
  113.7 17.7 %copy-start.3 = (bf16[192,3,3,3,384]{4,0,3,2,1:T(8,128)(2,1)S(1)}, bf16[192,3,3,3,384]{4,0,3,2,1:T(8,128)(2,1)}, u32[]{:S(2)}) copy-start(bf16[192,3,3,3,384]{4,0,3,2,1:T(8,128)(2,1)} %get-tuple-element.11) | copy-start | bytes 11943940
  141.9 25.0 %copy-start.6 = (bf16[4,1,384,128]{3,2,0,1:T(8,128)(2,1)S(1)}, bf16[4,1,384,128]{3,2,0,1:T(8,128)(2,1)}, u32[]{:S(2)}) copy-start(bf16[4,1,384,128]{3,2,0,1:T(8,128)(2,1)} %copy-done.5) | copy-start | bytes 1179652
  145.4 21.5 %collective-permute-start.10 = (bf16[4,1,384,128]{3,2,0,1:T(8,128)(2,1)S(1)}, bf16[4,1,384,128]{3,2,0,1:T(8,128)(2,1)S(1)}, u32[]{:S(2)}, u32[]{:S(2)}) collective-permute-start(bf16[4,1,384,128]{3,2,0,1:T(8,128)(2,1)S(1)} %fusion.146), channel_id=1, source_target_pairs={{4,0},{8,4},{12,8},{16,12},{20,16},{24,20},{28,24},{5,1},{9,5},{13... | collective-permute-start | bytes 1179656 | tf_op jit(solution)/shard_map/ppermute | solution.py:15
  147.4 19.6 %collective-permute-start.9 = (bf16[4,1,384,128]{3,2,0,1:T(8,128)(2,1)S(1)}, bf16[4,1,384,128]{3,2,0,1:T(8,128)(2,1)S(1)}, u32[]{:S(2)}, u32[]{:S(2)}) collective-permute-start(bf16[4,1,384,128]{3,2,0,1:T(8,128)(2,1)S(1)} %fusion.146), channel_id=1, source_target_pairs={{0,4},{4,8},{8,12},{12,16},{16,20},{20,24},{24,28},{1,5},{5,9},{9,... | collective-permute-start | bytes 1179656 | tf_op jit(solution)/shard_map/ppermute | solution.py:14
  152.8 14.5 %copy-start.1 = (bf16[192,3,3,3,384]{4,0,3,2,1:T(8,128)(2,1)S(1)}, bf16[192,3,3,3,384]{4,0,3,2,1:T(8,128)(2,1)}, u32[]{:S(2)}) copy-start(bf16[192,3,3,3,384]{4,0,3,2,1:T(8,128)(2,1)} %get-tuple-element.10) | copy-start | bytes 11943940
  174.6 2.0 %copy-start.9 = (bf16[4,1,192,128]{3,2,0,1:T(8,128)(2,1)S(1)}, bf16[4,1,192,128]{3,2,0,1:T(8,128)(2,1)}, u32[]{:S(2)}) copy-start(bf16[4,1,192,128]{3,2,0,1:T(8,128)(2,1)} %copy-done.8) | copy-start | bytes 589828
  (3 other events, 2.8 us)
Sparse Core Ops, SparseCore 0:
  23.0 9.4 all-gather.1
where the time goes:
time: 186 us; the launch traced here: 185 us
  waiting for transfers between devices  61.8 us (33%)
  matrix products  45 us (24%)
  starting transfers between devices  34.8 us (19%)
  between operations  15.3 us (8%)
  other arithmetic  10 us (5%)
  local copies, waits for them, and re-layouts  9.87 us (5%)
  blocking collectives  8.47 us (5%)
    dot_general x108, matrix products, local_conv(): jnp.einsum('oi,friw->frow', tap_kernel, shifted, preferred_element_type=j...  45 us
    ppermute x5, waiting for transfers between devices, padded_2(): after = lax.ppermute(first, axis, down)  41.5 us
    ppermute x5, starting transfers between devices, padded_2(): after = lax.ppermute(first, axis, down)  20.1 us
    ppermute x5, starting transfers between devices, padded_2(): before = lax.ppermute(last, axis, up)  13.4 us
    ppermute x5, waiting for transfers between devices, padded_2(): before = lax.ppermute(last, axis, up)  12.8 us
    all_gather x4, blocking collectives, conv_input(): widened = lax.all_gather(source, 'chan', axis=2, tiled=True)  8.47 us
    ppermute x1, waiting for transfers between devices, passed_along(): return lax.ppermute(shard, axis, pairs)  7.43 us
    squeeze x1, local copies, waits for them, and re-layouts, residual_block(): product = local_conv(second_window, kernels[1], offsets[1])  6.03 us
  transfers between devices with their start and end apart: 12, of which 8 were waited for; matrix products, arithmetic and copies ran while one was open for 8% of the time, Pallas kernels for 0%

commit v1 on v0

v1 whole, which is shorter than its diff:
```python
import functools

import jax
import jax.numpy as jnp
from jax import lax
from jax.experimental import pallas as pl
from jax.experimental.pallas import tpu as pltpu
from jax.sharding import PartitionSpec as P

BF16 = jnp.bfloat16
F32 = jnp.float32
LANES = 128
VMEM_LIMIT = 56 * 1024 * 1024


def params():
    return pltpu.CompilerParams(vmem_limit_bytes=VMEM_LIMIT)


def turned(x, by):
    by = by % LANES
    return x if by == 0 else pltpu.roll(x, by, x.ndim - 1)


def lane_ids(shape):
    return lax.broadcasted_iota(jnp.int32, shape, len(shape) - 1)


def windows_kernel(count, halo, pitch, features_ref, caches_ref, sent_features_ref, sent_caches_ref):
    frames, channels, cols = features_ref.shape
    own = cols // count
    lane = lane_ids((channels, LANES))
    parts = [
        ([features_ref[f].astype(F32) for f in range(frames)], sent_features_ref),
        ([caches_ref[j, f].astype(F32) for j in range(2) for f in range(2)], sent_caches_ref),
    ]
    for values, sent_ref in parts:
        for device in range(count):
            first = own * device - halo
            total = jnp.zeros((channels, LANES), F32)
            for slot, value in enumerate(values):
                low = pitch * slot + max(0, -first)
                high = pitch * slot + min(pitch, cols - first)
                inside = jnp.logical_and(lane >= low, lane < high)
                total = jnp.where(inside, turned(value, pitch * slot - first), total)
            sent_ref[device] = total.astype(BF16)


def windows(features, caches, count, halo, pitch):
    channels = features.shape[1]
    shape = jax.ShapeDtypeStruct((count, channels, LANES), BF16)
    return pl.pallas_call(
        functools.partial(windows_kernel, count, halo, pitch),
        out_shape=(shape, shape),
        compiler_params=params(),
        name="windows",
    )(features, caches)


def activate(conv, pitch, cols, place_ref, source_ref, cache_ref, gain_ref, window_ref):
    rows, channels = source_ref.shape[1], source_ref.shape[2]
    lane = lane_ids((1, LANES))
    col = place_ref[0] + lane % pitch
    inside = jnp.logical_and(col >= 0, col < cols)
    zero_row = jnp.zeros((2 * channels, LANES), BF16)
    for tap in range(3):
        window_ref[tap, 0] = zero_row
        window_ref[tap, rows + 1] = zero_row

    def row_step(r, carry):
        halves = [source_ref[h, r].astype(F32) for h in range(2)]
        square = sum(jnp.sum(v * v, axis=0, keepdims=True) for v in halves)
        scale = lax.rsqrt(square / (2 * channels) + 1e-06)
        for h, value in enumerate(halves):
            at = pl.ds(h * channels, channels)
            v = gain_ref[at, :] * value * scale
            active = jnp.where(inside, v / (1.0 + jnp.exp(-v)), 0.0)
            active = active.astype(BF16).astype(F32)
            cached = cache_ref[h, r].astype(F32)
            window_ref[2, r + 1, at, :] = active.astype(BF16)
            one = jnp.where(lane < pitch, turned(cached, -pitch * (2 * conv + 1)), turned(active, pitch))
            window_ref[1, r + 1, at, :] = one.astype(BF16)
            two = jnp.where(lane < 2 * pitch, turned(cached, -pitch * 2 * conv), turned(active, 2 * pitch))
            window_ref[0, r + 1, at, :] = two.astype(BF16)
        return carry

    lax.fori_loop(0, rows, row_step, 0)


def conv_kernel(conv, halo, pitch, cols, own, place_ref, source_ref, cache_ref, gain_ref, bias_ref, kernel_ref, *rest):
    if conv == 0:
        out_ref, kept_ref, window_ref, weight_ref, sems = rest
    else:
        base_ref, kept_in_ref, older_ref, out_ref, pack_ref, window_ref, weight_ref, sems = rest
    rows, channels = source_ref.shape[1], source_ref.shape[2]
    taps = weight_ref.shape[0]
    copies = [
        pltpu.make_async_copy(kernel_ref.at[conv, t], weight_ref.at[t], sems.at[t]) for t in range(taps)
    ]
    for copy in copies:
        copy.start()
    activate(conv, pitch, cols, place_ref, source_ref, cache_ref, gain_ref, window_ref)
    for copy in copies:
        copy.wait()
    mine = pl.ds(pl.multiple_of(place_ref[1] * channels, channels), channels)
    lane = lane_ids((channels, LANES))

    def pair_step(p, carry):
        total = None
        for tap in range(taps):
            a, b = tap // 3, tap % 3
            block = jnp.concatenate([window_ref[a, 2 * p + b], window_ref[a, 2 * p + 1 + b]], axis=1)
            part = jnp.dot(weight_ref[tap], block, preferred_element_type=F32)
            total = part if total is None else total + part
        for k in range(2):
            r = 2 * p + k
            left, centre, right = [
                total[d * channels : (d + 1) * channels, k * LANES : (k + 1) * LANES] for d in range(3)
            ]
            product = turned(left, 1) + centre + turned(right, -1) + bias_ref[...]
            if conv == 0:
                out_ref[r] = product.astype(BF16)
                kept_ref[r] = window_ref[2, r + 1, mine, :]
            else:
                result = (base_ref[r].astype(F32) + product).astype(BF16)
                out_ref[r] = result
                values = result.astype(F32)
                firsts = kept_in_ref[r].astype(F32)
                seconds = window_ref[2, r + 1, mine, :].astype(F32)
                frames = LANES // pitch
                slots = [(values, f) for f in range(frames)]
                slots += [(firsts, frames - 2), (firsts, frames - 1), (seconds, frames - 2), (seconds, frames - 1)]
                packed = jnp.zeros((channels, LANES), F32)
                for slot, (value, f) in enumerate(slots):
                    here = jnp.logical_and(lane >= own * slot, lane < own * (slot + 1))
                    packed = jnp.where(here, turned(value, own * slot - pitch * f - halo), packed)
                keep = jnp.broadcast_to(place_ref[2] == 1, (channels, LANES))
                pack_ref[r] = jnp.where(keep, packed, older_ref[r].astype(F32)).astype(BF16)
        return carry

    lax.fori_loop(0, rows // 2, pair_step, 0)


def convolved(conv, halo, pitch, cols, own, place, source, cache, gain, bias, kernel, *more):
    rows, channels = source.shape[1], source.shape[2]
    taps, height, depth = kernel.shape[1:]
    shape = jax.ShapeDtypeStruct((rows, channels, LANES), BF16)
    vmem = pl.BlockSpec(memory_space=pltpu.VMEM)
    in_specs = [pl.BlockSpec(memory_space=pltpu.SMEM), vmem, vmem, vmem, vmem, pl.BlockSpec(memory_space=pl.ANY)]
    in_specs += [vmem] * len(more)
    return pl.pallas_call(
        functools.partial(conv_kernel, conv, halo, pitch, cols, own),
        out_shape=(shape, shape),
        in_specs=in_specs,
        out_specs=(vmem, vmem),
        scratch_shapes=[
            pltpu.VMEM((3, rows + 2, depth, LANES), BF16),
            pltpu.VMEM((taps, height, depth), BF16),
            pltpu.SemaphoreType.DMA((taps,)),
        ],
        compiler_params=params(),
        name=f"conv_{conv}",
    )(place, source, cache, gain, bias, kernel, *more)


def whole_rows_kernel(own, packed_ref, frames_ref, tails_ref):
    count, channels = packed_ref.shape[0], packed_ref.shape[1]
    lane = lane_ids((channels, LANES))
    frames = frames_ref.shape[0]
    for slot in range(frames + 4):
        total = jnp.zeros((channels, LANES), F32)
        for device in range(count):
            here = jnp.logical_and(lane >= own * device, lane < own * (device + 1))
            total = jnp.where(here, turned(packed_ref[device].astype(F32), own * (device - slot)), total)
        if slot < frames:
            frames_ref[slot] = total.astype(BF16)
        else:
            tails_ref[(slot - frames) // 2, (slot - frames) % 2] = total.astype(BF16)


def whole_rows(packed, own, frames):
    channels = packed.shape[1]
    return pl.pallas_call(
        functools.partial(whole_rows_kernel, own),
        out_shape=(
            jax.ShapeDtypeStruct((frames, channels, LANES), BF16),
            jax.ShapeDtypeStruct((2, 2, channels, LANES), BF16),
        ),
        compiler_params=params(),
        name="whole_rows",
    )(packed)


def shards(features, caches, conv_weights, conv_bias, norm_gain):
    count = lax.axis_size("rows")
    segments = lax.axis_size("segment")
    segment = lax.axis_index("segment")
    chan = lax.axis_index("chan")
    frames, _, channels, cols = features.shape
    own = cols // count
    halo = 2 * segments
    pitch = LANES // frames
    depth = conv_weights.shape[-1]
    kernels = jnp.transpose(conv_weights[0], (0, 2, 3, 4, 1, 5)).reshape(2, 9, 3 * channels, depth)
    biases = lax.dynamic_slice_in_dim(conv_bias[0], chan * channels, channels, 1)[:, :, None]
    gains = norm_gain[0][:, :, None]
    first = lax.axis_index("rows") * own - halo

    sent_features, sent_caches = windows(features[:, 0], caches[0][:, :, 0], count, halo, pitch)
    block_input = lax.all_to_all(sent_features, "rows", 0, 0, tiled=True)
    tails = lax.all_to_all(sent_caches, "rows", 0, 0, tiled=True)
    tails = lax.all_gather(tails, "chan", axis=0)
    packed = jnp.zeros_like(block_input)
    for period in range(segments):
        place = jnp.stack([first, chan, (segment == period).astype(jnp.int32)]).astype(jnp.int32)
        source = lax.all_gather(block_input, "chan", axis=0)
        middle, kept = convolved(
            0, halo, pitch, cols, own, place, source, tails, gains[0], biases[0], kernels
        )
        source = lax.all_gather(middle, "chan", axis=0)
        result, packed = convolved(
            1, halo, pitch, cols, own, place, source, tails, gains[1], biases[1], kernels, block_input, kept, packed
        )
        if period < segments - 1:
            pairs = [(i, (i + 1) % segments) for i in range(segments)]
            block_input = lax.ppermute(result, "segment", pairs)
    packed = lax.all_to_all(packed, "rows", 0, 0, tiled=True)
    section_out, tails_out = whole_rows(packed, own, frames)
    return (section_out[None, :, None], tails_out[None, :, :, None])


def solution(mesh):
    in_specs = (
        P(None, "rows", "chan", None),
        P("segment", None, None, "rows", "chan", None),
        P("segment", None, "chan", None, None, None, None),
        P("segment", None, None),
        P("segment", None, None),
    )
    out_specs = (
        P("segment", None, "rows", "chan", None),
        P("segment", None, None, "rows", "chan", None),
    )
    return jax.shard_map(shards, mesh=mesh, in_specs=in_specs, out_specs=out_specs, check_vma=False)
```

time: 186 us -> 134 us (0.72)
  the two profiles are of different devices: /device:TPU:28 before, /device:TPU:0 now
where the time goes in v1:
time: 134 us; the launch traced here: 133 us
  blocking collectives  56.1 us (42%)
  Pallas kernels  51.3 us (38%)
  waiting for transfers between devices  12.9 us (10%)
  local copies, waits for them, and re-layouts  5.59 us (4%)
  starting transfers between devices  5.05 us (4%)
    pallas_call x4, Pallas kernels, convolved(): pl.pallas_call(functools.partial(conv_kernel, conv, halo, pitch, cols, ow...  46.1 us
    all_to_all x1, blocking collectives, shards(): tails = lax.all_to_all(sent_caches, 'rows', 0, 0, tiled=True)  19.3 us
    all_to_all x1, blocking collectives, shards(): packed = lax.all_to_all(packed, 'rows', 0, 0, tiled=True)  17 us
    all_gather x2, blocking collectives, shards(): source = lax.all_gather(middle, 'chan', axis=0)  12.4 us
    ppermute x1, waiting for transfers between devices, shards(): block_input = lax.ppermute(result, 'segment', pairs)  9.45 us
    all_gather x2, blocking collectives, shards(): source = lax.all_gather(block_input, 'chan', axis=0)  4.98 us
    all_to_all x1, starting transfers between devices, shards(): block_input = lax.all_to_all(sent_features, 'rows', 0, 0, tiled=True)  3.45 us
    all_to_all x1, waiting for transfers between devices, shards(): block_input = lax.all_to_all(sent_features, 'rows', 0, 0, tiled=True)  3.4 us
  transfers between devices with their start and end apart: 2, of which 2 were waited for; matrix products, arithmetic and copies ran while one was open for 5% of the time, Pallas kernels for 0%

profile of v1, /device:TPU:0, one launch (start us, length us, event | category | flops | bytes accessed | tf_op | source)
XLA Modules:
  0.0 132.8 jit_solution(8511944159330168204)
XLA Ops:
  0.6 2.6 %windows.1 = (bf16[8,192,128]{2,1,0:T(8,128)(2,1)}, bf16[8,192,128]{2,1,0:T(8,128)(2,1)}) custom-call(bf16[4,192,128]{2,1,0:T(8,128)(2,1)} %bitcast.42, bf16[2,2,192,128]{3,2,1,0:T(8,128)(2,1)} %bitcast.43), custom_call_target="tpu_custom_call" | custom-call | tf_op jit(solution)/shard_map/windows/pallas_call | solution.py:52
  3.3 19.3 %all_to_all.15 = bf16[8,192,128]{2,1,0:T(8,128)(2,1)S(1)} all-to-all(bf16[8,192,128]{2,1,0:T(8,128)(2,1)} %get-tuple-element.14), channel_id=1, replica_groups=mesh['rows'=8,'segment'=2,'chan'=2] {'rows'}, dimensions={0} | all-to-all | bytes 786432 | tf_op jit(solution)/shard_map/all_to_all | solution.py:211
  22.6 3.5 %all-to-all-start = ((bf16[8,192,128]{2,1,0:T(8,128)(2,1)}), bf16[8,192,128]{2,1,0:T(8,128)(2,1)S(1)}, u32[]{:S(2)}, u32[]{:S(2)}) async-start(bf16[8,192,128]{2,1,0:T(8,128)(2,1)} %get-tuple-element.13), calls=%async_computation | async-start | bytes 786432 | tf_op jit(solution)/shard_map/all_to_all | solution.py:210
  26.1 0.8 dynamic-slice_bitcast_fusion
  26.9 0.8 copy.22.bias_ref
  27.7 0.8 copy.20.bias_ref
  28.5 0.8 slice_bitcast_fusion
  29.2 0.8 copy.21.gain_ref
  30.0 0.8 copy.19.gain_ref
  31.5 2.5 %all-gather.1 = bf16[16,192,128]{2,1,0:T(8,128)(2,1)} all-gather(bf16[8,192,128]{2,1,0:T(8,128)(2,1)S(1)} %all_to_all.15), channel_id=3, replica_groups=mesh['rows'=8,'segment'=2,'chan'=2] {'chan'}, dimensions={0}, use_global_device_ids=true | all-gather | bytes 1179648 | tf_op jit(solution)/shard_map/all_gather | solution.py:212
  34.0 3.4 %all-to-all-done.rest_0_ = bf16[8,192,128]{2,1,0:T(8,128)(2,1)S(1)} async-done(((bf16[8,192,128]{2,1,0:T(8,128)(2,1)}), bf16[8,192,128]{2,1,0:T(8,128)(2,1)S(1)}, u32[]{:S(2)}, u32[]{:S(2)}) %all-to-all-start) | async-done | bytes 393248 | tf_op jit(solution)/shard_map/all_to_all | solution.py:210
  37.4 2.5 %all-gather = bf16[16,192,128]{2,1,0:T(8,128)(2,1)} all-gather(bf16[8,192,128]{2,1,0:T(8,128)(2,1)S(1)} %all-to-all-done.rest_0_), channel_id=2, replica_groups=mesh['rows'=8,'segment'=2,'chan'=2] {'chan'}, dimensions={0}, use_global_device_ids=true | all-gather | bytes 1179648 | tf_op jit(solution)/shard_map/all_gather | solution.py:216
  39.9 10.8 %conv_0.2 = (bf16[8,192,128]{2,1,0:T(8,128)(2,1)}, bf16[8,192,128]{2,1,0:T(8,128)(2,1)}) custom-call(s32[3]{0:T(128)} %pad_add_fusion.2.place_ref, bf16[2,8,192,128]{3,2,1,0:T(8,128)(2,1)} %bitcast.39, bf16[2,8,192,128]{3,2,1,0:T(8,128)(2,1)} %bitcast.34, f32[384,1]{1,0:T(8,128)} %copy.19.gain_ref, f32[192,1]{1,0:T(8,128)} %copy.20.bias_ref, ...), custom_call_target="tpu_custom_call" | custom-call | tf_op jit(solution)/shard_map/conv_0/pallas_call | solution.py:151
  50.7 6.2 %all-gather.2 = bf16[16,192,128]{2,1,0:T(8,128)(2,1)} all-gather(bf16[8,192,128]{2,1,0:T(8,128)(2,1)} %get-tuple-element.15), channel_id=4, replica_groups=mesh['rows'=8,'segment'=2,'chan'=2] {'chan'}, dimensions={0}, use_global_device_ids=true | all-gather | bytes 1179648 | tf_op jit(solution)/shard_map/all_gather | solution.py:220
  56.8 0.8 broadcast_in_dim.10.rest_2_
  57.6 12.3 %conv_1.2 = (bf16[8,192,128]{2,1,0:T(8,128)(2,1)}, bf16[8,192,128]{2,1,0:T(8,128)(2,1)}) custom-call(s32[3]{0:T(128)} %pad_add_fusion.2.place_ref, bf16[2,8,192,128]{3,2,1,0:T(8,128)(2,1)} %bitcast.41, bf16[2,8,192,128]{3,2,1,0:T(8,128)(2,1)} %bitcast.35, f32[384,1]{1,0:T(8,128)} %copy.21.gain_ref, f32[192,1]{1,0:T(8,128)} %copy.22.bias_ref, ...), custom_call_target="tpu_custom_call" | custom-call | tf_op jit(solution)/shard_map/conv_1/pallas_call | solution.py:151
  69.9 1.6 %collective-permute-start = (bf16[8,192,128]{2,1,0:T(8,128)(2,1)}, bf16[8,192,128]{2,1,0:T(8,128)(2,1)S(1)}, u32[]{:S(2)}, u32[]{:S(2)}) collective-permute-start(bf16[8,192,128]{2,1,0:T(8,128)(2,1)} %get-tuple-element.17), channel_id=1, source_target_pairs={{0,2},{2,0},{1,3},{3,1},{4,6},{6,4},{5,7},{7,5},{8,10},{10,8},{9,1... | collective-permute-start | bytes 1179656 | tf_op jit(solution)/shard_map/ppermute | solution.py:226
  72.1 9.4 %collective-permute-done.rest_0_ = bf16[8,192,128]{2,1,0:T(8,128)(2,1)S(1)} collective-permute-done((bf16[8,192,128]{2,1,0:T(8,128)(2,1)}, bf16[8,192,128]{2,1,0:T(8,128)(2,1)S(1)}, u32[]{:S(2)}, u32[]{:S(2)}) %collective-permute-start) | collective-permute-done | bytes 393248 | tf_op jit(solution)/shard_map/ppermute | solution.py:226
  81.6 2.5 %all-gather.3 = bf16[16,192,128]{2,1,0:T(8,128)(2,1)} all-gather(bf16[8,192,128]{2,1,0:T(8,128)(2,1)S(1)} %collective-permute-done.rest_0_), channel_id=5, replica_groups=mesh['rows'=8,'segment'=2,'chan'=2] {'chan'}, dimensions={0}, use_global_device_ids=true | all-gather | bytes 1179648 | tf_op jit(solution)/shard_map/all_gather | solution.py:216
  84.1 10.8 %conv_0.3 = (bf16[8,192,128]{2,1,0:T(8,128)(2,1)}, bf16[8,192,128]{2,1,0:T(8,128)(2,1)}) custom-call(s32[3]{0:T(128)} %pad_add_fusion.place_ref, bf16[2,8,192,128]{3,2,1,0:T(8,128)(2,1)} %bitcast.38, bf16[2,8,192,128]{3,2,1,0:T(8,128)(2,1)} %bitcast.36, f32[384,1]{1,0:T(8,128)} %copy.19.gain_ref, f32[192,1]{1,0:T(8,128)} %copy.20.bias_ref, ...), custom_call_target="tpu_custom_call" | custom-call | tf_op jit(solution)/shard_map/conv_0/pallas_call | solution.py:151
  94.9 6.2 %all-gather.4 = bf16[16,192,128]{2,1,0:T(8,128)(2,1)} all-gather(bf16[8,192,128]{2,1,0:T(8,128)(2,1)} %get-tuple-element.18), channel_id=6, replica_groups=mesh['rows'=8,'segment'=2,'chan'=2] {'chan'}, dimensions={0}, use_global_device_ids=true | all-gather | bytes 1179648 | tf_op jit(solution)/shard_map/all_gather | solution.py:220
  101.1 12.3 %conv_1.3 = (bf16[8,192,128]{2,1,0:T(8,128)(2,1)}, bf16[8,192,128]{2,1,0:T(8,128)(2,1)}) custom-call(s32[3]{0:T(128)} %pad_add_fusion.place_ref, bf16[2,8,192,128]{3,2,1,0:T(8,128)(2,1)} %bitcast.40, bf16[2,8,192,128]{3,2,1,0:T(8,128)(2,1)} %bitcast.37, f32[384,1]{1,0:T(8,128)} %copy.21.gain_ref, f32[192,1]{1,0:T(8,128)} %copy.22.bias_ref, ...), custom_call_target="tpu_custom_call" | custom-call | tf_op jit(solution)/shard_map/conv_1/pallas_call | solution.py:151
  113.4 17.0 %all_to_all.16.packed_ref = bf16[8,192,128]{2,1,0:T(8,128)(2,1)} all-to-all(bf16[8,192,128]{2,1,0:T(8,128)(2,1)} %get-tuple-element.21), channel_id=1, replica_groups=mesh['rows'=8,'segment'=2,'chan'=2] {'rows'}, dimensions={0} | all-to-all | bytes 786432 | tf_op jit(solution)/shard_map/all_to_all | solution.py:227
  130.3 2.5 %whole_rows.1 = (bf16[4,192,128]{2,1,0:T(8,128)(2,1)}, bf16[2,2,192,128]{3,2,1,0:T(8,128)(2,1)}) custom-call(bf16[8,192,128]{2,1,0:T(8,128)(2,1)} %all_to_all.16.packed_ref), custom_call_target="tpu_custom_call" | custom-call | tf_op jit(solution)/shard_map/whole_rows/pallas_call | solution.py:183
  (6 shorter events, 1.2 us)
Async XLA Ops:
  22.6 14.8 %all-to-all-start = ((bf16[8,192,128]{2,1,0:T(8,128)(2,1)}), bf16[8,192,128]{2,1,0:T(8,128)(2,1)S(1)}, u32[]{:S(2)}, u32[]{:S(2)}) async-start(bf16[8,192,128]{2,1,0:T(8,128)(2,1)} %get-tuple-element.13), calls=%async_computation | async-start | bytes 786432 | tf_op jit(solution)/shard_map/all_to_all | solution.py:210
  37.4 20.3 %copy-start = (bf16[8,192,128]{2,1,0:T(8,128)(2,1)}, bf16[8,192,128]{2,1,0:T(8,128)(2,1)S(1)}, u32[]{:S(2)}) copy-start(bf16[8,192,128]{2,1,0:T(8,128)(2,1)S(1)} %all-to-all-done.rest_0_) | copy-start | bytes 1179652
  69.9 11.7 %collective-permute-start = (bf16[8,192,128]{2,1,0:T(8,128)(2,1)}, bf16[8,192,128]{2,1,0:T(8,128)(2,1)S(1)}, u32[]{:S(2)}, u32[]{:S(2)}) collective-permute-start(bf16[8,192,128]{2,1,0:T(8,128)(2,1)} %get-tuple-element.17), channel_id=1, source_target_pairs={{0,2},{2,0},{1,3},{3,1},{4,6},{6,4},{5,7},{7,5},{8,10},{10,8},{9,1... | collective-permute-start | bytes 1179656 | tf_op jit(solution)/shard_map/ppermute | solution.py:226
  81.6 19.5 %copy-start.1 = (bf16[8,192,128]{2,1,0:T(8,128)(2,1)}, bf16[8,192,128]{2,1,0:T(8,128)(2,1)S(1)}, u32[]{:S(2)}) copy-start(bf16[8,192,128]{2,1,0:T(8,128)(2,1)S(1)} %collective-permute-done.rest_0_) | copy-start | bytes 1179652

commit v2 on v0

v2 whole, which is shorter than its diff:
```python
import functools

import jax
import jax.numpy as jnp
from jax import lax
from jax.experimental import pallas as pl
from jax.experimental.pallas import tpu as pltpu
from jax.sharding import PartitionSpec as P

BF16 = jnp.bfloat16
F32 = jnp.float32
LANES = 128
SENT = 24
PITCH = 32
MIB = 1024 * 1024
VMEM = pl.BlockSpec(memory_space=pltpu.VMEM)
SMEM = pl.BlockSpec(memory_space=pltpu.SMEM)


def params(mib):
    return pltpu.CompilerParams(vmem_limit_bytes=mib * MIB)


def turned(x, by):
    by = by % LANES
    return x if by == 0 else pltpu.roll(x, by, x.ndim - 1)


def lanes_of(shape):
    return lax.broadcasted_iota(jnp.int32, shape, len(shape) - 1)


def between(lane, low, high):
    return jnp.logical_and(lane >= low, lane < high)


def tile(rows, channels, dtype=BF16):
    return jax.ShapeDtypeStruct((rows, channels, LANES), dtype)


def spread(x, lane):
    total = x
    for f in range(1, LANES // PITCH):
        total = jnp.where(between(lane, PITCH * f, PITCH * (f + 1)), turned(x, (PITCH - SENT) * f), total)
    return total


def gathered(x, lane):
    total = x
    for f in range(1, LANES // PITCH):
        total = jnp.where(between(lane, SENT * f, SENT * (f + 1)), turned(x, (SENT - PITCH) * f), total)
    return total


def fold(x, lane):
    whole = x.shape[0] * 3 // 4
    rest = x[whole:]
    tails = [turned(rest, 96 - 32 * i) for i in range(3)]
    return jnp.where(lane < 96, x[:whole], jnp.concatenate(tails, axis=0))


def unfold(x, lane):
    part = x.shape[0] // 3
    pieces = [turned(x[i * part : (i + 1) * part], 32 * i - 96) for i in range(3)]
    rest = jnp.where(lane < 32, pieces[0], jnp.where(lane < 64, pieces[1], pieces[2]))
    return jnp.concatenate([x, rest], axis=0)


def prepared_kernel(place_ref, gain_ref, bias_ref, gains_ref, biases_ref, all_ref):
    channels = biases_ref.shape[1]
    depth = gains_ref.shape[1]
    mine = pl.ds(pl.multiple_of(place_ref[1] * channels, channels), channels)
    for conv in range(2):
        for source, out in ((gain_ref, gains_ref.at[conv]), (bias_ref, all_ref)):
            for k in range(depth // LANES):
                at = slice(k * LANES, (k + 1) * LANES)
                out[at, :] = jnp.transpose(jnp.broadcast_to(source[conv : conv + 1, at], (LANES, LANES)))
        biases_ref[conv] = all_ref[mine, :]


def prepared(place, gain, bias, channels):
    depth = gain.shape[1]
    return pl.pallas_call(
        prepared_kernel,
        out_shape=(
            jax.ShapeDtypeStruct((2, depth, LANES), F32),
            jax.ShapeDtypeStruct((2, channels, LANES), F32),
        ),
        in_specs=[SMEM, VMEM, VMEM],
        out_specs=(VMEM, VMEM),
        scratch_shapes=[pltpu.VMEM((depth, LANES), F32)],
        compiler_params=params(8),
        name="prepared",
    )(place, gain, bias)


def windows_kernel(count, halo, features_ref, caches_ref, sent_ref):
    frames, channels, cols = features_ref.shape
    own = cols // count
    half = channels // 2
    lane = lanes_of((1, LANES))
    groups = [
        [features_ref[f] for f in range(frames)],
        [caches_ref[j, f] for j in range(2) for f in range(2)],
    ]
    for device in range(count):
        first = own * device - halo
        tiles = []
        for group in groups:
            total = jnp.zeros((channels, LANES), BF16)
            for slot, value in enumerate(group):
                low = SENT * slot + max(0, -first)
                high = SENT * slot + min(SENT, cols - first)
                total = jnp.where(between(lane, low, high), turned(value, SENT * slot - first), total)
            tiles.append(total)
        ahead, tails = tiles
        sent_ref[device, :channels] = jnp.where(lane < 96, ahead, turned(tails, 96))
        sent_ref[device, channels:] = jnp.where(lane < 64, turned(tails[:half], -32), turned(tails[half:], 32))


def windows(features, caches, count, halo):
    channels = features.shape[1]
    return pl.pallas_call(
        functools.partial(windows_kernel, count, halo),
        out_shape=tile(count, channels * 3 // 2),
        compiler_params=params(8 + count // 2),
        name="windows",
    )(features, caches)


def tails_of(sent, lane, channels):
    half = channels // 2
    extra = jnp.concatenate([turned(sent[channels:], 32), turned(sent[channels:], -32)], axis=0)
    return spread(jnp.where(lane < 32, turned(sent[:channels], -96), extra), lane)


def packed_row(own, halo, lane, result, kept):
    frames = LANES // PITCH
    slots = [(result, f) for f in range(frames)]
    slots += [(active, f) for active in kept for f in (frames - 2, frames - 1)]
    total = jnp.zeros(result.shape, BF16)
    for slot, (value, f) in enumerate(slots):
        here = between(lane, own * slot, own * (slot + 1))
        total = jnp.where(here, turned(value, own * slot - PITCH * f - halo), total)
    return total


def pack_kernel(period, own, halo, place_ref, result_ref, kept_0_ref, kept_1_ref, *rest):
    lane = lanes_of((1, LANES))
    out_ref = rest[-1]

    def step(r, carry):
        row = packed_row(own, halo, lane, result_ref[r], (kept_0_ref[r], kept_1_ref[r]))
        out_ref[r] = row if period == 0 else jnp.where(place_ref[2] == period, row, rest[0][r])
        return carry

    for_rows(result_ref.shape[0], step)


def for_rows(count, step):
    if count <= 8:
        for r in range(count):
            step(r, 0)
    else:
        lax.fori_loop(0, count, step, 0)


def packed_period(period, own, halo, place, result, kept, older):
    rows, channels = result.shape[:2]
    more = [] if older is None else [older]
    return pl.pallas_call(
        functools.partial(pack_kernel, period, own, halo),
        out_shape=tile(rows, channels),
        in_specs=[SMEM] + [VMEM] * (3 + len(more)),
        out_specs=VMEM,
        compiler_params=params(8 + rows // 2),
        name="packed_period",
    )(place, result, *kept, *more)


def conv_kernel(conv, first, last, halo, cols, own_cols, names, *refs):
    ref = dict(zip(names, refs))
    place_ref, weight_ref, window_ref = ref["place"], ref["weight"], ref["window"]
    own_ref, other_ref, kept_ref = ref["own"], ref["other"], ref["kept"]
    rows = own_ref.shape[0]
    taps, height, depth = weight_ref.shape
    channels = height // 3
    mine_first = place_ref[1] == 0
    lane = lanes_of((1, LANES))
    col = place_ref[0] + lane % PITCH
    inside = between(col, 0, cols)

    def ordered(own, other):
        return [jnp.where(mine_first, own, other), jnp.where(mine_first, other, own)]

    empty = jnp.zeros((depth, LANES), BF16)
    for tap in range(3):
        window_ref[tap, 0] = empty
        window_ref[tap, rows + 1] = empty

    def activate(r, carry):
        own, other = own_ref[r], other_ref[r]
        if conv == 0:
            if first:
                tails = ordered(*[tails_of(x, lane, channels) for x in (own, other)])
                own, other = [spread(x[:channels], lane) for x in (own, other)]
            else:
                own, other = [spread(unfold(x, lane), lane) for x in (own, other)]
            ref["base_out"][r] = own
        values = [x.astype(F32) for x in ordered(own, other)]
        square = sum(jnp.sum(v * v, axis=0, keepdims=True) for v in values)
        scale = jnp.where(inside, 0.5 * lax.rsqrt(square / depth + 1e-06), 0.0)
        kept = []
        for h, value in enumerate(values):
            at = slice(h * channels, (h + 1) * channels)
            t = ref["gains"][conv, at, :] * value * scale
            active = (t + t * jnp.tanh(t)).astype(BF16)
            if first and conv == 0:
                cached = tails[h]
                ref["tails_out"][r, at, :] = cached
            else:
                cached = ref["tails"][r, at, :]
            window_ref[2, r + 1, at, :] = active
            window_ref[1, r + 1, at, :] = jnp.where(
                lane < PITCH, turned(cached, -PITCH * (2 * conv + 1)), turned(active, PITCH)
            )
            window_ref[0, r + 1, at, :] = jnp.where(
                lane < 2 * PITCH, turned(cached, -PITCH * 2 * conv), turned(active, 2 * PITCH)
            )
            kept.append(active)
        kept_ref[r] = jnp.where(mine_first, *kept)
        return carry

    def multiply(r0, count):
        block = jnp.concatenate(
            [
                jnp.concatenate([window_ref[t // 3, r0 + t % 3 + i] for i in range(count)], axis=1)
                for t in range(taps)
            ],
            axis=0,
        )
        weight = jnp.concatenate([weight_ref[t] for t in range(taps)], axis=1)
        total = jnp.dot(weight, block, preferred_element_type=F32)
        offset = ref["biases"][conv]
        for k in range(count):
            r = r0 + k
            left, centre, right = [
                total[d * channels : (d + 1) * channels, k * LANES : (k + 1) * LANES] for d in range(3)
            ]
            product = turned(left, 1) + centre + turned(right, -1) + offset
            if conv == 0:
                ref["out"][r] = product.astype(BF16)
                continue
            result = (ref["base"][r].astype(F32) + product).astype(BF16)
            if last:
                row = packed_row(own_cols, halo, lane, result, (ref["kept_0"][r], kept_ref[r]))
                ref["out"][r] = jnp.where(place_ref[2] == last, row, ref["older"][r])
            else:
                ref["out"][r] = result
                ref["sent"][r] = fold(gathered(result, lane), lane)

    steps = 4
    if rows <= 8:
        done = 0
        for r0 in range(0, rows, steps):
            need = min(rows, r0 + steps + 1)
            for r in range(done, need):
                activate(r, 0)
            done = need
            multiply(r0, steps)
    else:
        lax.fori_loop(0, rows, activate, 0)
        lax.fori_loop(0, rows // steps, lambda g, c: (multiply(g * steps, steps), c)[1], 0)


def convolved(conv, first, last, halo, cols, own_cols, arrays, outs):
    rows = arrays["own"].shape[0]
    taps, height, depth = arrays["weight"].shape
    scratch = {"window": pltpu.VMEM((3, rows + 2, depth, LANES), BF16)}
    if "kept" not in outs:
        scratch["kept"] = pltpu.VMEM((rows, height // 3, LANES), BF16)
    names = [*arrays, *outs, *scratch]
    results = pl.pallas_call(
        functools.partial(conv_kernel, conv, first, last, halo, cols, own_cols, names),
        out_shape=[tile(rows, size) for size in outs.values()],
        in_specs=[SMEM if name == "place" else VMEM for name in arrays],
        out_specs=[VMEM] * len(outs),
        scratch_shapes=list(scratch.values()),
        compiler_params=params(9 + 5 * rows // 8),
        name=f"conv_{conv}",
    )(*arrays.values())
    return dict(zip(outs, results))


def whole_rows_kernel(own, packed_ref, frames_ref, tails_ref):
    count, channels = packed_ref.shape[0], packed_ref.shape[1]
    lane = lanes_of((1, LANES))
    frames = frames_ref.shape[0]
    for slot in range(frames + 4):
        total = jnp.zeros((channels, LANES), BF16)
        for device in range(count):
            here = between(lane, own * device, own * (device + 1))
            total = jnp.where(here, turned(packed_ref[device], own * (device - slot)), total)
        if slot < frames:
            frames_ref[slot] = total
        else:
            tails_ref[(slot - frames) // 2, (slot - frames) % 2] = total


def whole_rows(packed, own, frames):
    count, channels = packed.shape[:2]
    return pl.pallas_call(
        functools.partial(whole_rows_kernel, own),
        out_shape=(tile(frames, channels), jax.ShapeDtypeStruct((2, 2, channels, LANES), BF16)),
        compiler_params=params(8 + count // 2),
        name="whole_rows",
    )(packed)


def swapped(x):
    return lax.ppermute(x, "chan", [(0, 1), (1, 0)])


def shards(features, caches, conv_weights, conv_bias, norm_gain):
    count = lax.axis_size("rows")
    segments = lax.axis_size("segment")
    frames, _, channels, cols = features.shape
    depth = conv_weights.shape[-1]
    own = cols // count
    halo = 2 * segments
    assert own + 2 * halo <= SENT and frames * PITCH == LANES
    kernels = jnp.transpose(conv_weights[0], (0, 2, 3, 4, 1, 5)).reshape(2, 9, 3 * channels, depth)
    first = lax.axis_index("rows") * own - halo
    place = jnp.stack([first, lax.axis_index("chan"), lax.axis_index("segment")]).astype(jnp.int32)

    sent = windows(features[:, 0], caches[0][:, :, 0], count, halo)
    gains, biases = prepared(place, norm_gain[0], conv_bias[0], channels)
    source = lax.all_to_all(sent, "rows", 0, 0, tiled=True)
    source, gains, biases = lax.optimization_barrier((source, gains, biases))
    common = {"place": place, "gains": gains, "biases": biases}
    packed = tails = None
    kernels_0 = kernels[0]
    for period in range(segments):
        last = period if period == segments - 1 else 0
        arrays = common | {"weight": kernels_0, "own": source, "other": swapped(source)}
        outs = {"out": channels, "kept": channels, "base_out": channels}
        if period == 0:
            outs["tails_out"] = depth
        else:
            arrays["tails"] = tails
        one = convolved(0, period == 0, last, halo, cols, own, arrays, outs)
        middle = one["out"]
        if period == 0:
            tails = one["tails_out"]
            middle, kernels = lax.optimization_barrier((middle, kernels))
            kernels_1 = kernels[1]
        arrays = common | {"weight": kernels_1, "own": middle, "other": swapped(middle)}
        arrays |= {"tails": tails, "base": one["base_out"]}
        if last:
            arrays |= {"kept_0": one["kept"], "older": packed}
            packed = convolved(1, False, last, halo, cols, own, arrays, {"out": channels})["out"]
        else:
            outs = {"out": channels, "kept": channels, "sent": channels * 3 // 4}
            two = convolved(1, False, last, halo, cols, own, arrays, outs)
            source = lax.ppermute(two["sent"], "segment", [(i, (i + 1) % segments) for i in range(segments)])
            kept = (one["kept"], two["kept"])
            packed = packed_period(period, own, halo, place, two["out"], kept, packed)
    packed = lax.all_to_all(packed, "rows", 0, 0, tiled=True)
    section_out, tails_out = whole_rows(packed, own, frames)
    return (section_out[None, :, None], tails_out[None, :, :, None])


def solution(mesh):
    in_specs = (
        P(None, "rows", "chan", None),
        P("segment", None, None, "rows", "chan", None),
        P("segment", None, "chan", None, None, None, None),
        P("segment", None, None),
        P("segment", None, None),
    )
    out_specs = (
        P("segment", None, "rows", "chan", None),
        P("segment", None, None, "rows", "chan", None),
    )
    return jax.shard_map(shards, mesh=mesh, in_specs=in_specs, out_specs=out_specs, check_vma=False)
```

time: 186 us -> 87.3 us (0.47)
  the two profiles are of different devices: /device:TPU:28 before, /device:TPU:0 now
where the time goes in v2:
time: 87.3 us; the launch traced here: 87 us
  Pallas kernels  30.3 us (35%)
  waiting for transfers between devices  24 us (27%)
  blocking collectives  15.9 us (18%)
  starting transfers between devices  9.62 us (11%)
  local copies, waits for them, and re-layouts  6.32 us (7%)
    pallas_call x4, Pallas kernels, convolved(): pl.pallas_call(functools.partial(conv_kernel, conv, first, last, halo, co...  24.3 us
    all_to_all x1, blocking collectives, shards(): packed = lax.all_to_all(packed, 'rows', 0, 0, tiled=True)  15.9 us
    all_to_all x1, waiting for transfers between devices, shards(): source = lax.all_to_all(sent, 'rows', 0, 0, tiled=True)  13.6 us
    ppermute x1, waiting for transfers between devices, shards(): lax.ppermute(two['sent'], 'segment', [(i, (i + 1) % segments) for i in ra...  7.75 us
    all_to_all x1, starting transfers between devices, shards(): source = lax.all_to_all(sent, 'rows', 0, 0, tiled=True)  7.25 us
    unnamed x10, local copies, waits for them, and re-layouts  3.22 us
    slice x1, local copies, waits for them, and re-layouts, shards(): kernels_0 = kernels[0]  2.68 us
    ppermute x4, waiting for transfers between devices, swapped(): return lax.ppermute(x, 'chan', [(0, 1), (1, 0)])  2.66 us
  transfers between devices with their start and end apart: 6, of which 5 were waited for; matrix products, arithmetic and copies ran while one was open for 4% of the time, Pallas kernels for 3%

profile of v2, /device:TPU:0, one launch (start us, length us, event | category | flops | bytes accessed | tf_op | source)
XLA Modules:
  0.0 87.0 jit_solution(8568175747787328325)
XLA Ops:
  0.6 0.9 %copy-done = bf16[4,1,192,128]{3,2,1,0:T(8,128)(2,1)S(1)} copy-done((bf16[4,1,192,128]{3,2,1,0:T(8,128)(2,1)S(1)}, bf16[4,1,192,128]{3,2,1,0:T(8,128)(2,1)}, u32[]{:S(2)}) %copy-start) | copy-done | bytes 196632
  1.6 0.9 %copy-done.1 = bf16[1,2,2,1,192,128]{5,4,3,2,1,0:T(8,128)(2,1)S(1)} copy-done((bf16[1,2,2,1,192,128]{5,4,3,2,1,0:T(8,128)(2,1)S(1)}, bf16[1,2,2,1,192,128]{5,4,3,2,1,0:T(8,128)(2,1)}, u32[]{:S(2)}) %copy-start.1) | copy-done | bytes 196632
  2.5 2.3 %windows.1 = bf16[8,288,128]{2,1,0:T(8,128)(2,1)} custom-call(bf16[4,192,128]{2,1,0:T(8,128)(2,1)S(1)} %bitcast.23, bf16[2,2,192,128]{3,2,1,0:T(8,128)(2,1)S(1)} %bitcast.24), custom_call_target="tpu_custom_call" | custom-call | tf_op jit(solution)/shard_map/windows/pallas_call | solution.py:123
  4.8 7.3 %all-to-all-start = ((bf16[8,288,128]{2,1,0:T(8,128)(2,1)}), bf16[8,288,128]{2,1,0:T(8,128)(2,1)S(1)}, u32[]{:S(2)}, u32[]{:S(2)}) async-start(bf16[8,288,128]{2,1,0:T(8,128)(2,1)} %windows.1), calls=%async_computation | async-start | bytes 1179648 | tf_op jit(solution)/shard_map/all_to_all | solution.py:338
  12.1 0.7 copy-done.2
  12.8 0.7 copy-done.3
  13.5 0.8 prepared.1
  14.3 13.6 %all-to-all-done.refs_4_ = bf16[8,288,128]{2,1,0:T(8,128)(2,1)S(1)} async-done(((bf16[8,288,128]{2,1,0:T(8,128)(2,1)}), bf16[8,288,128]{2,1,0:T(8,128)(2,1)S(1)}, u32[]{:S(2)}, u32[]{:S(2)}) %all-to-all-start) | async-done | bytes 589856 | tf_op jit(solution)/shard_map/all_to_all | solution.py:338
  27.9 2.7 %slice.9 = bf16[1,3,3,3,192,384]{5,4,3,2,1,0:T(8,128)(2,1)S(1)} slice(bf16[2,3,3,3,192,384]{5,4,3,2,1,0:T(8,128)(2,1)} %bitcast.27), slice={[0:1], [0:3], [0:3], [0:3], [0:192], [0:384]} | slice | bytes 7962624 | tf_op jit(solution)/shard_map/slice | solution.py:342
  30.6 6.4 %conv_0.2 = (bf16[8,192,128]{2,1,0:T(8,128)(2,1)S(1)}, bf16[8,192,128]{2,1,0:T(8,128)(2,1)S(1)}, bf16[8,192,128]{2,1,0:T(8,128)(2,1)S(1)}, bf16[8,384,128]{2,1,0:T(8,128)(2,1)S(1)}) custom-call(s32[3]{0:T(128)S(1)} %pad_add_fusion.place_ref.refs_0_, f32[2,384,128]{2,1,0:T(8,128)S(1)} %get-tuple-element.23.refs_1_, ...), custom_call_target="tpu_custom_call" | custom-call | tf_op jit(solution)/shard_map/conv_0/pallas_call | solution.py:283
  37.0 0.6 collective-permute-start.1
  37.6 0.4 slice_bitcast_fusion.refs_3_
  38.0 0.9 %collective-permute-done.1.refs_5_ = bf16[8,192,128]{2,1,0:T(8,128)(2,1)S(1)} collective-permute-done((bf16[8,192,128]{2,1,0:T(8,128)(2,1)S(1)}, bf16[8,192,128]{2,1,0:T(8,128)(2,1)S(1)}, u32[]{:S(2)}, u32[]{:S(2)}) %collective-permute-start.1) | collective-permute-done | bytes 393248 | tf_op jit(solution)/shard_map/ppermute | solution.py:321
  38.9 5.9 %conv_1.2 = (bf16[8,192,128]{2,1,0:T(8,128)(2,1)S(1)}, bf16[8,192,128]{2,1,0:T(8,128)(2,1)S(1)}, bf16[8,144,128]{2,1,0:T(8,128)(2,1)S(1)}) custom-call(s32[3]{0:T(128)S(1)} %pad_add_fusion.place_ref.refs_0_, f32[2,384,128]{2,1,0:T(8,128)S(1)} %get-tuple-element.23.refs_1_, f32[2,192,128]{2,1,0:T(8,128)S(1)} %get-tuple-element.24.refs_2_, ...), custom_call_target="tpu_custom_call" | custom-call | tf_op jit(solution)/shard_map/conv_1/pallas_call | solution.py:283
  44.8 1.6 %collective-permute-start.2 = (bf16[8,144,128]{2,1,0:T(8,128)(2,1)S(1)}, bf16[8,144,128]{2,1,0:T(8,128)(2,1)S(1)}, u32[]{:S(2)}, u32[]{:S(2)}) collective-permute-start(bf16[8,144,128]{2,1,0:T(8,128)(2,1)S(1)} %get-tuple-element.31), channel_id=1, source_target_pairs={{0,2},{2,0},{1,3},{3,1},{4,6},{6,4},{5,7},{7,5},{8,10},{10,8},{9,1... | collective-permute-start | bytes 884744 | tf_op jit(solution)/shard_map/ppermute | solution.py:365
  46.4 7.8 %collective-permute-done.2.refs_4_ = bf16[8,144,128]{2,1,0:T(8,128)(2,1)S(1)} collective-permute-done((bf16[8,144,128]{2,1,0:T(8,128)(2,1)S(1)}, bf16[8,144,128]{2,1,0:T(8,128)(2,1)S(1)}, u32[]{:S(2)}, u32[]{:S(2)}) %collective-permute-start.2) | collective-permute-done | bytes 294944 | tf_op jit(solution)/shard_map/ppermute | solution.py:365
  54.2 1.6 %collective-permute-done.3.refs_5_ = bf16[8,144,128]{2,1,0:T(8,128)(2,1)S(1)} collective-permute-done((bf16[8,144,128]{2,1,0:T(8,128)(2,1)S(1)}, bf16[8,144,128]{2,1,0:T(8,128)(2,1)S(1)}, u32[]{:S(2)}, u32[]{:S(2)}) %collective-permute-start.3) | collective-permute-done | bytes 294944 | tf_op jit(solution)/shard_map/ppermute | solution.py:321
  55.8 6.1 %conv_0.3 = (bf16[8,192,128]{2,1,0:T(8,128)(2,1)S(1)}, bf16[8,192,128]{2,1,0:T(8,128)(2,1)S(1)}, bf16[8,192,128]{2,1,0:T(8,128)(2,1)S(1)}) custom-call(s32[3]{0:T(128)S(1)} %pad_add_fusion.place_ref.refs_0_, f32[2,384,128]{2,1,0:T(8,128)S(1)} %get-tuple-element.23.refs_1_, f32[2,192,128]{2,1,0:T(8,128)S(1)} %get-tuple-element.24.refs_2_, ...), custom_call_target="tpu_custom_call" | custom-call | tf_op jit(solution)/shard_map/conv_0/pallas_call | solution.py:283
  61.9 0.2 collective-permute-start.4
  62.1 1.4 %packed_period.1.refs_9_ = bf16[8,192,128]{2,1,0:T(8,128)(2,1)S(1)} custom-call(s32[3]{0:T(128)S(1)} %pad_add_fusion.place_ref.refs_0_, bf16[8,192,128]{2,1,0:T(8,128)(2,1)S(1)} %get-tuple-element.35.result_ref, bf16[8,192,128]{2,1,0:T(8,128)(2,1)S(1)} %get-tuple-element.36.kept_0_ref, bf16[8,192,128]{2,1,0:T(8,128)(2,1)S(1)} %get-tuple-element.37.kept_1_ref), custom_call_target="tpu_custom_call" | custom-call | tf_op jit(solution)/shard_map/packed_period/pallas_call | solution.py:171
  63.5 0.2 collective-permute-done.4.refs_5_
  63.7 5.9 %conv_1.3 = bf16[8,192,128]{2,1,0:T(8,128)(2,1)S(1)} custom-call(s32[3]{0:T(128)S(1)} %pad_add_fusion.place_ref.refs_0_, f32[2,384,128]{2,1,0:T(8,128)S(1)} %get-tuple-element.23.refs_1_, f32[2,192,128]{2,1,0:T(8,128)S(1)} %get-tuple-element.24.refs_2_, bf16[9,576,384]{2,1,0:T(8,128)(2,1)S(1)} %slice_bitcast_fusion.refs_3_, ...), custom_call_target="tpu_custom_call" | custom-call | tf_op jit(solution)/shard_map/conv_1/pallas_call | solution.py:283
  69.6 15.9 %all_to_all.10.packed_ref = bf16[8,192,128]{2,1,0:T(8,128)(2,1)S(1)} all-to-all(bf16[8,192,128]{2,1,0:T(8,128)(2,1)S(1)} %conv_1.3), channel_id=1, replica_groups=mesh['rows'=8,'segment'=2,'chan'=2] {'rows'}, dimensions={0} | all-to-all | bytes 786432 | tf_op jit(solution)/shard_map/all_to_all | solution.py:368
  85.5 1.5 %whole_rows.1 = (bf16[4,192,128]{2,1,0:T(8,128)(2,1)}, bf16[2,2,192,128]{3,2,1,0:T(8,128)(2,1)}) custom-call(bf16[8,192,128]{2,1,0:T(8,128)(2,1)S(1)} %all_to_all.10.packed_ref), custom_call_target="tpu_custom_call" | custom-call | tf_op jit(solution)/shard_map/whole_rows/pallas_call | solution.py:312
  (10 shorter events, 0.1 us)
Async XLA Ops:
  0.6 0.9 %copy-start = (bf16[4,1,192,128]{3,2,1,0:T(8,128)(2,1)S(1)}, bf16[4,1,192,128]{3,2,1,0:T(8,128)(2,1)}, u32[]{:S(2)}) copy-start(bf16[4,1,192,128]{3,2,1,0:T(8,128)(2,1)} %param.5) | copy-start | bytes 589828
  1.6 0.9 %copy-start.1 = (bf16[1,2,2,1,192,128]{5,4,3,2,1,0:T(8,128)(2,1)S(1)}, bf16[1,2,2,1,192,128]{5,4,3,2,1,0:T(8,128)(2,1)}, u32[]{:S(2)}) copy-start(bf16[1,2,2,1,192,128]{5,4,3,2,1,0:T(8,128)(2,1)} %param.6) | copy-start | bytes 589828
  4.8 23.1 %all-to-all-start = ((bf16[8,288,128]{2,1,0:T(8,128)(2,1)}), bf16[8,288,128]{2,1,0:T(8,128)(2,1)S(1)}, u32[]{:S(2)}, u32[]{:S(2)}) async-start(bf16[8,288,128]{2,1,0:T(8,128)(2,1)} %windows.1), calls=%async_computation | async-start | bytes 1179648 | tf_op jit(solution)/shard_map/all_to_all | solution.py:338
  12.1 0.7 copy-start.2
  12.8 0.7 copy-start.3
  27.9 2.7 %collective-permute-start = (bf16[8,288,128]{2,1,0:T(8,128)(2,1)S(1)}, bf16[8,288,128]{2,1,0:T(8,128)(2,1)S(1)}, u32[]{:S(2)}, u32[]{:S(2)}) collective-permute-start(bf16[8,288,128]{2,1,0:T(8,128)(2,1)S(1)} %all-to-all-done.refs_4_), channel_id=1, source_target_pairs={{0,1},{1,0},{2,3},{3,2},{4,5},{5,4},{6,7},{7,6},{8,9},{9,8},{10,11... | collective-permute-start | bytes 1769480 | tf_op jit(solution)/shard_map/ppermute | solution.py:321
  27.9 9.6 %copy-start.4 = (bf16[1,2,192,3,3,3,384]{6,2,5,4,3,1,0:T(8,128)(2,1)S(1)}, bf16[1,2,192,3,3,3,384]{6,2,5,4,3,1,0:T(8,128)(2,1)}, u32[]{:S(2)}) copy-start(bf16[1,2,192,3,3,3,384]{6,2,5,4,3,1,0:T(8,128)(2,1)} %param.7) | copy-start | bytes 23887876
  37.0 1.9 %collective-permute-start.1 = (bf16[8,192,128]{2,1,0:T(8,128)(2,1)S(1)}, bf16[8,192,128]{2,1,0:T(8,128)(2,1)S(1)}, u32[]{:S(2)}, u32[]{:S(2)}) collective-permute-start(bf16[8,192,128]{2,1,0:T(8,128)(2,1)S(1)} %get-tuple-element.28.refs_4_), channel_id=1, source_target_pairs={{0,1},{1,0},{2,3},{3,2},{4,5},{5,4},{6,7},{7,6},{8,9},{9,8},{10,11... | collective-permute-start | bytes 1179656 | tf_op jit(solution)/shard_map/ppermute | solution.py:321
  44.8 9.4 %collective-permute-start.2 = (bf16[8,144,128]{2,1,0:T(8,128)(2,1)S(1)}, bf16[8,144,128]{2,1,0:T(8,128)(2,1)S(1)}, u32[]{:S(2)}, u32[]{:S(2)}) collective-permute-start(bf16[8,144,128]{2,1,0:T(8,128)(2,1)S(1)} %get-tuple-element.31), channel_id=1, source_target_pairs={{0,2},{2,0},{1,3},{3,1},{4,6},{6,4},{5,7},{7,5},{8,10},{10,8},{9,1... | collective-permute-start | bytes 884744 | tf_op jit(solution)/shard_map/ppermute | solution.py:365
  54.2 1.6 %collective-permute-start.3 = (bf16[8,144,128]{2,1,0:T(8,128)(2,1)S(1)}, bf16[8,144,128]{2,1,0:T(8,128)(2,1)S(1)}, u32[]{:S(2)}, u32[]{:S(2)}) collective-permute-start(bf16[8,144,128]{2,1,0:T(8,128)(2,1)S(1)} %collective-permute-done.2.refs_4_), channel_id=1, source_target_pairs={{0,1},{1,0},{2,3},{3,2},{4,5},{5,4},{6,7},{7,6},{8,9},{9,8},{10,11... | collective-permute-start | bytes 884744 | tf_op jit(solution)/shard_map/ppermute | solution.py:321
  61.9 1.8 %collective-permute-start.4 = (bf16[8,192,128]{2,1,0:T(8,128)(2,1)S(1)}, bf16[8,192,128]{2,1,0:T(8,128)(2,1)S(1)}, u32[]{:S(2)}, u32[]{:S(2)}) collective-permute-start(bf16[8,192,128]{2,1,0:T(8,128)(2,1)S(1)} %get-tuple-element.32.refs_4_), channel_id=1, source_target_pairs={{0,1},{1,0},{2,3},{3,2},{4,5},{5,4},{6,7},{7,6},{8,9},{9,8},{10,11... | collective-permute-start | bytes 1179656 | tf_op jit(solution)/shard_map/ppermute | solution.py:321

commit v3 on v0

v3 whole, which is shorter than its diff:
```python
import functools

import jax
import jax.numpy as jnp
from jax import lax
from jax.experimental import pallas as pl
from jax.experimental.pallas import tpu as pltpu
from jax.sharding import PartitionSpec as P

BF16 = jnp.bfloat16
F32 = jnp.float32
LANES = 128
MIB = 1024 * 1024
VMEM = pl.BlockSpec(memory_space=pltpu.VMEM)
SMEM = pl.BlockSpec(memory_space=pltpu.SMEM)
TAILS = 4


def params(mib):
    return pltpu.CompilerParams(vmem_limit_bytes=mib * MIB)


def turned(x, by):
    by = by % LANES
    return x if by == 0 else pltpu.roll(x, by, x.ndim - 1)


def tiles(count, channels, dtype=BF16):
    return jax.ShapeDtypeStruct((count, channels, LANES), dtype)


def prepared_kernel(place_ref, gain_ref, bias_ref, kernels_ref, gains_ref, biases_ref, all_ref):
    channels = biases_ref.shape[1]
    depth = gains_ref.shape[1]
    mine = pl.ds(pl.multiple_of(place_ref[0] * channels, channels), channels)
    for conv in range(2):
        for source, out in ((gain_ref, gains_ref.at[conv]), (bias_ref, all_ref)):
            for k in range(depth // LANES):
                at = slice(k * LANES, (k + 1) * LANES)
                out[at, :] = jnp.transpose(jnp.broadcast_to(source[conv : conv + 1, at], (LANES, LANES)))
        biases_ref[conv] = all_ref[mine, :]


def prepared(place, gain, bias, kernels, channels):
    depth = gain.shape[1]
    return pl.pallas_call(
        prepared_kernel,
        out_shape=(
            jax.ShapeDtypeStruct((2, depth, LANES), F32),
            jax.ShapeDtypeStruct((2, channels, LANES), F32),
        ),
        in_specs=[SMEM, VMEM, VMEM, VMEM],
        out_specs=(VMEM, VMEM),
        scratch_shapes=[pltpu.VMEM((depth, LANES), F32)],
        compiler_params=params(16),
        name="prepared",
    )(place, gain, bias, kernels)


class Part:
    def __init__(self, conv, ref, count):
        self.conv, self.ref, self.count = conv, ref, count
        self.window = ref["window"]
        self.weight = ref["weight"]
        _, self.taps, height, self.depth = self.weight.shape
        self.channels = height // 3
        self.mine_first = ref["place"][0] == 0
        self.side = ref["place"][1]
        self.lane = lax.broadcasted_iota(jnp.int32, (1, LANES), 1)

    def ordered(self, name, tile):
        own, other = self.ref[name][tile], self.ref[name + "_other"][tile]
        return [jnp.where(self.mine_first, own, other), jnp.where(self.mine_first, other, own)]

    def activate(self, slot, frame, name, tile, valid=None):
        values = [x.astype(F32) for x in self.ordered(name, tile)]
        square = sum(jnp.sum(v * v, axis=0, keepdims=True) for v in values)
        scale = 0.5 * lax.rsqrt(square / self.depth + 1e-06)
        if valid is not None:
            scale = jnp.where(valid, scale, 0.0)
        kept = []
        for h, value in enumerate(values):
            at = slice(h * self.channels, (h + 1) * self.channels)
            t = self.ref["gains"][self.conv, at, :] * value * scale
            active = (t + t * jnp.tanh(t)).astype(BF16)
            self.window[slot, frame + 2, at, :] = active
            kept.append(active)
        return jnp.where(self.mine_first, *kept)

    def cached(self, slot, name, tile):
        for f in range(2):
            for h, value in enumerate(self.ordered(name, tile + 2 * self.conv + f)):
                self.window[slot, f, h * self.channels : (h + 1) * self.channels, :] = value

    def product(self, slots, first, frames):
        block, weight = [], []
        for slot, tap in slots:
            row_tap = 1 + self.side * (tap - 1)
            for a in range(3):
                weight.append(self.weight[self.conv, 3 * a + row_tap])
                block.append(
                    jnp.concatenate([self.window[slot, first + f + a] for f in range(frames)], axis=1)
                )
        total = jnp.dot(
            jnp.concatenate(weight, axis=1), jnp.concatenate(block, axis=0), preferred_element_type=F32
        )
        sums = []
        for f in range(frames):
            left, centre, right = [
                total[d * self.channels : (d + 1) * self.channels, f * LANES : (f + 1) * LANES] for d in range(3)
            ]
            left = jnp.where(self.lane == 0, 0.0, turned(left, 1))
            right = jnp.where(self.lane == LANES - 1, 0.0, turned(right, -1))
            sums.append(left + centre + right)
        return sums


def near_kernel(frames, base, names, *refs):
    ref = dict(zip(names, refs))
    part = Part(0, ref, frames)
    sums = ref["sums"]
    bias = ref["biases"][0]
    places = [("own", 0), ("beside", 0), ("beside", 1), ("beside", 2)]
    cache_tiles = ref["tails_own"].shape[0]

    def load(slot):
        name, group = places[slot]
        part.cached(slot, "tails_" + name, group * cache_tiles)
        for f in range(frames):
            kept = part.activate(slot, f, name, group * (frames + base) + base + f)
            if slot == 0 and f >= frames - 2:
                ref["kept"][f - frames + 2] = kept

    def store(o, slots):
        for f, value in enumerate(part.product(slots, 0, frames)):
            sums[(o + 1) * frames + f] = value + bias

    load(0)
    load(1)
    store(0, [(1, 0), (0, 1)])
    load(2)
    store(-1, [(2, 0), (1, 1), (0, 2)])
    load(3)
    store(1, [(0, 0), (3, 2)])


def far_kernel(frames, base, names, *refs):
    ref = dict(zip(names, refs))
    part = Part(0, ref, frames)
    out, sums = ref["out"], ref["sums"]
    part.cached(0, "tails_diagonal", 0)
    for f in range(frames):
        part.activate(0, f, "diagonal", base + f)
    for f in range(frames):
        out[f] = sums[f].astype(BF16)
    for o, tap in ((0, 2), (1, 1)):
        for f, value in enumerate(part.product([(0, tap)], 0, frames)):
            at = (o + 1) * frames + f
            out[at] = (sums[at] + value).astype(BF16)


def second_kernel(frames, base, period, count, names, *refs):
    ref = dict(zip(names, refs))
    part = Part(1, ref, frames)
    row, segment = ref["place"][2], ref["place"][3]
    bias = ref["biases"][1]
    places = [("tails_own", 0), ("tails_beside", 0), ("tails_diagonal", 0)]
    offsets = (0, -1, 1)

    def load(first, last):
        for slot, q in enumerate(offsets):
            at = row + part.side * q
            valid = None if q == 0 else jnp.broadcast_to(jnp.logical_and(at >= 0, at < count), (1, LANES))
            for f in range(first, last):
                kept = part.activate(slot, f, "middle", (q + 1) * frames + f, valid)
                if slot == 0 and f >= frames - 2:
                    new_tails[2 + f - frames + 2] = kept

    new_tails = {f: ref["kept"][f] for f in range(2)}

    def store(first, last):
        sums = part.product([(1, 0), (0, 1), (2, 2)], first, last - first)
        for f, value in enumerate(sums, first):
            result = (ref["source"][base + f].astype(F32) + (value + bias)).astype(BF16)
            if "result" in ref:
                ref["result"][f] = result
            ref["out"][f] = jnp.where(segment == period, result, ref["older"][f]) if period else result

    for slot, (name, tile) in enumerate(places):
        part.cached(slot, name, tile)
    half = frames // 2
    load(0, half)
    store(0, half)
    load(half, frames)
    store(half, frames)
    for f in range(4):
        tail = new_tails[f]
        ref["tails"][f] = jnp.where(segment == period, tail, ref["older_tails"][f]) if period else tail


def call(kernel, name, arrays, outs, slots):
    depth = arrays["weight"].shape[-1]
    frames = 4
    scratch = {"window": pltpu.VMEM((slots, frames + 2, depth, LANES), BF16)}
    names = [*arrays, *outs, *scratch]
    results = pl.pallas_call(
        functools.partial(kernel, names),
        out_shape=list(outs.values()),
        in_specs=[SMEM if key == "place" else VMEM for key in arrays],
        out_specs=[VMEM] * len(outs),
        scratch_shapes=list(scratch.values()),
        compiler_params=params(16),
        name=name,
    )(*arrays.values())
    return dict(zip(outs, results))


def swapped(x):
    return lax.ppermute(x, "chan", [(0, 1), (1, 0)])


def with_other(name, x):
    return {name: x, name + "_other": swapped(x)}


def exchanged(x, count, kind, pair, *beside_it):
    pairs = count // 2
    across = [(i, i ^ 1) for i in range(count)]
    even, odd = [], []
    for i in range(count):
        k = i // 2
        for k_to, group in ((k ^ 1, even), (k + 1 if k % 2 else k - 1, odd)):
            if 0 <= k_to < pairs:
                group.append((i, 2 * k_to + i % 2))
    beside = lax.ppermute(x, "rows", across)
    a = lax.ppermute(x, "rows", even)
    b = lax.ppermute(x, "rows", odd)
    if beside_it:
        beside, a, b, beside_it = lax.optimization_barrier((beside, a, b, beside_it))
    to_a = kind == pair % 2
    near, far = jnp.where(to_a, a, b), jnp.where(to_a, b, a)
    diagonal = lax.ppermute(near, "rows", across)
    return jnp.concatenate([beside, near, far], axis=0), diagonal, beside_it


def shards(features, caches, conv_weights, conv_bias, norm_gain):
    count = lax.axis_size("rows")
    segments = lax.axis_size("segment")
    row = lax.axis_index("rows")
    frames, _, channels, _ = features.shape
    depth = conv_weights.shape[-1]
    kernels = jnp.transpose(conv_weights[0], (0, 2, 3, 4, 1, 5)).reshape(2, 9, 3 * channels, depth)
    kind, pair = row % 2, row // 2
    place = [lax.axis_index("chan"), 2 * kind - 1, row, lax.axis_index("segment")]
    place = jnp.stack(place).astype(jnp.int32)

    source = jnp.concatenate([caches[0].reshape(TAILS, channels, LANES), features[:, 0]], axis=0)
    fixed = prepared(place, norm_gain[0], conv_bias[0], kernels, channels)
    out = tails = None
    cached = {}
    for period in range(segments):
        base = TAILS if period == 0 else 0
        own = with_other("own", source)
        beside, diagonal, done = exchanged(source, count, kind, pair, *(() if period else fixed))
        beside = with_other("beside", beside)
        if period == 0:
            common = {"place": place, "gains": done[0], "biases": done[1], "weight": kernels}
            cached = {"tails_" + key: value for key, value in (own | beside).items()}
        tails_of = lambda *keys: {"tails_" + k + o: cached["tails_" + k + o] for k in keys for o in ("", "_other")}
        outs = {"sums": tiles(3 * frames, channels, F32), "kept": tiles(2, channels)}
        near = call(
            functools.partial(near_kernel, frames, base),
            "near_rows",
            common | own | beside | tails_of("own", "beside"),
            outs,
            4,
        )
        diagonal, sums = lax.optimization_barrier((diagonal, near["sums"]))
        diagonal = with_other("diagonal", diagonal)
        if period == 0:
            cached |= {"tails_" + key: value for key, value in diagonal.items()}
        middle = call(
            functools.partial(far_kernel, frames, base),
            "far_row",
            common | diagonal | tails_of("diagonal") | {"sums": sums},
            {"out": tiles(3 * frames, channels)},
            1,
        )["out"]
        arrays = common | with_other("middle", middle) | tails_of("own", "beside", "diagonal")
        arrays |= {"source": source, "kept": near["kept"]}
        outs = {"out": tiles(frames, channels), "tails": tiles(TAILS, channels)}
        if period:
            arrays |= {"older": out, "older_tails": tails}
            if period < segments - 1:
                outs["result"] = tiles(frames, channels)
        second = call(
            functools.partial(second_kernel, frames, base, period, count), "second", arrays, outs, 3
        )
        out, tails = second["out"], second["tails"]
        if period < segments - 1:
            result = second["result"] if period else out
            source = lax.ppermute(result, "segment", [(i, (i + 1) % segments) for i in range(segments)])
    return (out[None, :, None], tails.reshape(1, 2, 2, 1, channels, LANES))


def solution(mesh):
    in_specs = (
        P(None, "rows", "chan", None),
        P("segment", None, None, "rows", "chan", None),
        P("segment", None, "chan", None, None, None, None),
        P("segment", None, None),
        P("segment", None, None),
    )
    out_specs = (
        P("segment", None, "rows", "chan", None),
        P("segment", None, None, "rows", "chan", None),
    )
    return jax.shard_map(shards, mesh=mesh, in_specs=in_specs, out_specs=out_specs, check_vma=False)
```

time: 186 us -> 75.4 us (0.41)
  the two profiles are of different devices: /device:TPU:28 before, /device:TPU:0 now
where the time goes in v3:
time: 75.4 us; the launch traced here: 75.2 us
  Pallas kernels  26.5 us (35%)
  waiting for transfers between devices  23.1 us (31%)
  starting transfers between devices  18.8 us (25%)
  local copies, waits for them, and re-layouts  4.63 us (6%)
  other arithmetic  1.42 us (2%)
  between operations  0.76 us (1%)
    pallas_call x6, Pallas kernels, call(): pl.pallas_call(functools.partial(kernel, names), out_shape=list(outs.valu...  25.6 us
    ppermute x8, waiting for transfers between devices, swapped(): return lax.ppermute(x, 'chan', [(0, 1), (1, 0)])  8.45 us
    ppermute x2, starting transfers between devices, exchanged(): a = lax.ppermute(x, 'rows', even)  8 us
    ppermute x1, waiting for transfers between devices, shards(): lax.ppermute(result, 'segment', [(i, (i + 1) % segments) for i in range(s...  5.42 us
    unnamed x8, local copies, waits for them, and re-layouts  4.63 us
    ppermute x2, waiting for transfers between devices, exchanged(): a = lax.ppermute(x, 'rows', even)  4.4 us
    ppermute x2, waiting for transfers between devices, exchanged(): beside = lax.ppermute(x, 'rows', across)  3 us
    ppermute x2, starting transfers between devices, exchanged(): diagonal = lax.ppermute(near, 'rows', across)  2.98 us
  transfers between devices with their start and end apart: 17, of which 12 were waited for; matrix products, arithmetic and copies ran while one was open for 0% of the time, Pallas kernels for 18%

profile of v3, /device:TPU:0, one launch (start us, length us, event | category | flops | bytes accessed | tf_op | source)
XLA Modules:
  0.0 75.2 jit_solution(17060134730110445627)
XLA Ops:
  2.4 5.9 %collective-permute-start.1 = (bf16[8,192,128]{2,1,0:T(8,128)(2,1)S(1)}, bf16[8,192,128]{2,1,0:T(8,128)(2,1)S(1)}, u32[]{:S(2)}, u32[]{:S(2)}) collective-permute-start(bf16[8,192,128]{2,1,0:T(8,128)(2,1)S(1)} %pad_maximum_fusion.2.refs_4_.refs_8_.refs_6_.refs_12_), channel_id=1, source_target_pairs={{0,8},{4,12},{8,0},{12,4},{16,24},{20,28},{24,16},{28,20},{1,9},{5... | collective-permute-start | bytes 1179656 | tf_op jit(solution)/shard_map/ppermute | solution.py:236
  8.3 1.5 %collective-permute-start = (bf16[8,192,128]{2,1,0:T(8,128)(2,1)S(1)}, bf16[8,192,128]{2,1,0:T(8,128)(2,1)S(1)}, u32[]{:S(2)}, u32[]{:S(2)}) collective-permute-start(bf16[8,192,128]{2,1,0:T(8,128)(2,1)S(1)} %pad_maximum_fusion.2.refs_4_.refs_8_.refs_6_.refs_12_), channel_id=1, source_target_pairs={{0,4},{4,0},{8,12},{12,8},{16,20},{20,16},{24,28},{28,24},{1,5},{5... | collective-permute-start | bytes 1179656 | tf_op jit(solution)/shard_map/ppermute | solution.py:235
  9.8 3.3 %copy-done = bf16[1,2,192,3,3,3,384]{6,2,5,4,3,1,0:T(8,128)(2,1)S(1)} copy-done((bf16[1,2,192,3,3,3,384]{6,2,5,4,3,1,0:T(8,128)(2,1)S(1)}, bf16[1,2,192,3,3,3,384]{6,2,5,4,3,1,0:T(8,128)(2,1)}, u32[]{:S(2)}) %copy-start) | copy-done | bytes 7962648
  15.3 1.8 %collective-permute-done.1 = bf16[8,192,128]{2,1,0:T(8,128)(2,1)S(1)} collective-permute-done((bf16[8,192,128]{2,1,0:T(8,128)(2,1)S(1)}, bf16[8,192,128]{2,1,0:T(8,128)(2,1)S(1)}, u32[]{:S(2)}, u32[]{:S(2)}) %collective-permute-start.1) | collective-permute-done | bytes 393248 | tf_op jit(solution)/shard_map/ppermute | solution.py:236
  17.1 1.5 %collective-permute-done = bf16[8,192,128]{2,1,0:T(8,128)(2,1)S(1)} collective-permute-done((bf16[8,192,128]{2,1,0:T(8,128)(2,1)S(1)}, bf16[8,192,128]{2,1,0:T(8,128)(2,1)S(1)}, u32[]{:S(2)}, u32[]{:S(2)}) %collective-permute-start) | collective-permute-done | bytes 393248 | tf_op jit(solution)/shard_map/ppermute | solution.py:235
  19.3 1.5 %collective-permute-start.3 = (bf16[8,192,128]{2,1,0:T(8,128)(2,1)S(1)}, bf16[8,192,128]{2,1,0:T(8,128)(2,1)S(1)}, u32[]{:S(2)}, u32[]{:S(2)}) collective-permute-start(bf16[8,192,128]{2,1,0:T(8,128)(2,1)S(1)} %get-tuple-element.43), channel_id=1, source_target_pairs={{0,4},{4,0},{8,12},{12,8},{16,20},{20,16},{24,28},{28,24},{1,5},{5... | collective-permute-start | bytes 1179656 | tf_op jit(solution)/shard_map/ppermute | solution.py:242
  20.8 1.4 %collective-permute-done.4.refs_5_.refs_9_.refs_7_ = bf16[8,192,128]{2,1,0:T(8,128)(2,1)S(1)} collective-permute-done((bf16[8,192,128]{2,1,0:T(8,128)(2,1)S(1)}, bf16[8,192,128]{2,1,0:T(8,128)(2,1)S(1)}, u32[]{:S(2)}, u32[]{:S(2)}) %collective-permute-start.4) | collective-permute-done | bytes 393248 | tf_op jit(solution)/shard_map/ppermute | solution.py:219
  22.2 6.4 %near_rows.2 = (f32[12,192,128]{2,1,0:T(8,128)S(1)}, bf16[2,192,128]{2,1,0:T(8,128)(2,1)S(1)}) custom-call(s32[4]{0:T(128)S(1)} %pad_add_fusion.place_ref.refs_0_, f32[2,384,128]{2,1,0:T(8,128)S(1)} %get-tuple-element.23.refs_1_, f32[2,192,128]{2,1,0:T(8,128)S(1)} %get-tuple-element.24.refs_2_, bf16[2,9,576,384]{3,2,1,0:T(8,128)(2,1)S(1)} %bitcast.20, ...), custom_call_target="tpu_custom_call" | custom-call | tf_op jit(solution)/shard_map/near_rows/pallas_call | solution.py:206
  28.6 1.8 %collective-permute-done.3.refs_4_.refs_6_.refs_10_ = bf16[8,192,128]{2,1,0:T(8,128)(2,1)S(1)} collective-permute-done((bf16[8,192,128]{2,1,0:T(8,128)(2,1)S(1)}, bf16[8,192,128]{2,1,0:T(8,128)(2,1)S(1)}, u32[]{:S(2)}, u32[]{:S(2)}) %collective-permute-start.3) | collective-permute-done | bytes 393248 | tf_op jit(solution)/shard_map/ppermute | solution.py:242
  30.4 1.7 %collective-permute-done.6.refs_5_.refs_7_.refs_11_ = bf16[8,192,128]{2,1,0:T(8,128)(2,1)S(1)} collective-permute-done((bf16[8,192,128]{2,1,0:T(8,128)(2,1)S(1)}, bf16[8,192,128]{2,1,0:T(8,128)(2,1)S(1)}, u32[]{:S(2)}, u32[]{:S(2)}) %collective-permute-start.6) | collective-permute-done | bytes 393248 | tf_op jit(solution)/shard_map/ppermute | solution.py:219
  32.2 2.6 %far_row.2.refs_4_ = bf16[12,192,128]{2,1,0:T(8,128)(2,1)S(1)} custom-call(s32[4]{0:T(128)S(1)} %pad_add_fusion.place_ref.refs_0_, f32[2,384,128]{2,1,0:T(8,128)S(1)} %get-tuple-element.23.refs_1_, f32[2,192,128]{2,1,0:T(8,128)S(1)} %get-tuple-element.24.refs_2_, bf16[2,9,576,384]{3,2,1,0:T(8,128)(2,1)S(1)} %bitcast.21, ...), custom_call_target="tpu_custom_call" | custom-call | tf_op jit(solution)/shard_map/far_row/pallas_call | solution.py:206
  35.0 1.9 %collective-permute-done.7.refs_5_ = bf16[12,192,128]{2,1,0:T(8,128)(2,1)S(1)} collective-permute-done((bf16[12,192,128]{2,1,0:T(8,128)(2,1)S(1)}, bf16[12,192,128]{2,1,0:T(8,128)(2,1)S(1)}, u32[]{:S(2)}, u32[]{:S(2)}) %collective-permute-start.7) | collective-permute-done | bytes 589856 | tf_op jit(solution)/shard_map/ppermute | solution.py:219
  36.9 3.4 %second.2 = (bf16[4,192,128]{2,1,0:T(8,128)(2,1)S(1)}, bf16[4,192,128]{2,1,0:T(8,128)(2,1)S(1)}) custom-call(s32[4]{0:T(128)S(1)} %pad_add_fusion.place_ref.refs_0_, f32[2,384,128]{2,1,0:T(8,128)S(1)} %get-tuple-element.23.refs_1_, f32[2,192,128]{2,1,0:T(8,128)S(1)} %get-tuple-element.24.refs_2_, bf16[2,9,576,384]{3,2,1,0:T(8,128)(2,1)S(1)} %bitcast.22, ...), custom_call_target="tpu_custom_call" | custom-call | tf_op jit(solution)/shard_map/second/pallas_call | solution.py:206
  40.3 1.6 %collective-permute-start.8 = (bf16[4,192,128]{2,1,0:T(8,128)(2,1)S(1)}, bf16[4,192,128]{2,1,0:T(8,128)(2,1)S(1)}, u32[]{:S(2)}, u32[]{:S(2)}) collective-permute-start(bf16[4,192,128]{2,1,0:T(8,128)(2,1)S(1)} %get-tuple-element.32.refs_14_), channel_id=1, source_target_pairs={{0,2},{2,0},{1,3},{3,1},{4,6},{6,4},{5,7},{7,5},{8,10},{10,8},{9,1... | collective-permute-start | bytes 589832 | tf_op jit(solution)/shard_map/ppermute | solution.py:302
  41.9 5.4 %collective-permute-done.8.refs_4_.refs_12_ = bf16[4,192,128]{2,1,0:T(8,128)(2,1)S(1)} collective-permute-done((bf16[4,192,128]{2,1,0:T(8,128)(2,1)S(1)}, bf16[4,192,128]{2,1,0:T(8,128)(2,1)S(1)}, u32[]{:S(2)}, u32[]{:S(2)}) %collective-permute-start.8) | collective-permute-done | bytes 196640 | tf_op jit(solution)/shard_map/ppermute | solution.py:302
  48.2 2.1 %collective-permute-start.9 = (bf16[4,192,128]{2,1,0:T(8,128)(2,1)S(1)}, bf16[4,192,128]{2,1,0:T(8,128)(2,1)S(1)}, u32[]{:S(2)}, u32[]{:S(2)}) collective-permute-start(bf16[4,192,128]{2,1,0:T(8,128)(2,1)S(1)} %collective-permute-done.8.refs_4_.refs_12_), channel_id=1, source_target_pairs={{0,8},{4,12},{8,0},{12,4},{16,24},{20,28},{24,16},{28,20},{1,9},{5... | collective-permute-start | bytes 589832 | tf_op jit(solution)/shard_map/ppermute | solution.py:236
  50.3 1.5 %collective-permute-start.13 = (bf16[4,192,128]{2,1,0:T(8,128)(2,1)S(1)}, bf16[4,192,128]{2,1,0:T(8,128)(2,1)S(1)}, u32[]{:S(2)}, u32[]{:S(2)}) collective-permute-start(bf16[4,192,128]{2,1,0:T(8,128)(2,1)S(1)} %collective-permute-done.8.refs_4_.refs_12_), channel_id=1, source_target_pairs={{0,4},{4,0},{8,12},{12,8},{16,20},{20,16},{24,28},{28,24},{1,5},{5... | collective-permute-start | bytes 589832 | tf_op jit(solution)/shard_map/ppermute | solution.py:235
  51.8 2.6 %collective-permute-done.9 = bf16[4,192,128]{2,1,0:T(8,128)(2,1)S(1)} collective-permute-done((bf16[4,192,128]{2,1,0:T(8,128)(2,1)S(1)}, bf16[4,192,128]{2,1,0:T(8,128)(2,1)S(1)}, u32[]{:S(2)}, u32[]{:S(2)}) %collective-permute-start.9) | collective-permute-done | bytes 196640 | tf_op jit(solution)/shard_map/ppermute | solution.py:236
  54.4 1.5 %collective-permute-done.13 = bf16[4,192,128]{2,1,0:T(8,128)(2,1)S(1)} collective-permute-done((bf16[4,192,128]{2,1,0:T(8,128)(2,1)S(1)}, bf16[4,192,128]{2,1,0:T(8,128)(2,1)S(1)}, u32[]{:S(2)}, u32[]{:S(2)}) %collective-permute-start.13) | collective-permute-done | bytes 196640 | tf_op jit(solution)/shard_map/ppermute | solution.py:235
  56.6 1.5 %collective-permute-start.11 = (bf16[4,192,128]{2,1,0:T(8,128)(2,1)S(1)}, bf16[4,192,128]{2,1,0:T(8,128)(2,1)S(1)}, u32[]{:S(2)}, u32[]{:S(2)}) collective-permute-start(bf16[4,192,128]{2,1,0:T(8,128)(2,1)S(1)} %get-tuple-element.45), channel_id=1, source_target_pairs={{0,4},{4,0},{8,12},{12,8},{16,20},{20,16},{24,28},{28,24},{1,5},{5... | collective-permute-start | bytes 589832 | tf_op jit(solution)/shard_map/ppermute | solution.py:242
  58.4 6.4 %near_rows.3 = (f32[12,192,128]{2,1,0:T(8,128)S(1)}, bf16[2,192,128]{2,1,0:T(8,128)(2,1)S(1)}) custom-call(s32[4]{0:T(128)S(1)} %pad_add_fusion.place_ref.refs_0_, f32[2,384,128]{2,1,0:T(8,128)S(1)} %get-tuple-element.23.refs_1_, f32[2,192,128]{2,1,0:T(8,128)S(1)} %get-tuple-element.24.refs_2_, bf16[2,9,576,384]{3,2,1,0:T(8,128)(2,1)S(1)} %bitcast.23, ...), custom_call_target="tpu_custom_call" | custom-call | tf_op jit(solution)/shard_map/near_rows/pallas_call | solution.py:206
  66.3 2.6 %far_row.3.refs_4_ = bf16[12,192,128]{2,1,0:T(8,128)(2,1)S(1)} custom-call(s32[4]{0:T(128)S(1)} %pad_add_fusion.place_ref.refs_0_, f32[2,384,128]{2,1,0:T(8,128)S(1)} %get-tuple-element.23.refs_1_, f32[2,192,128]{2,1,0:T(8,128)S(1)} %get-tuple-element.24.refs_2_, bf16[2,9,576,384]{3,2,1,0:T(8,128)(2,1)S(1)} %bitcast.24, ...), custom_call_target="tpu_custom_call" | custom-call | tf_op jit(solution)/shard_map/far_row/pallas_call | solution.py:206
  69.1 1.9 %collective-permute-done.16.refs_5_ = bf16[12,192,128]{2,1,0:T(8,128)(2,1)S(1)} collective-permute-done((bf16[12,192,128]{2,1,0:T(8,128)(2,1)S(1)}, bf16[12,192,128]{2,1,0:T(8,128)(2,1)S(1)}, u32[]{:S(2)}, u32[]{:S(2)}) %collective-permute-start.16) | collective-permute-done | bytes 589856 | tf_op jit(solution)/shard_map/ppermute | solution.py:219
  71.0 4.2 %second.3 = (bf16[4,192,128]{2,1,0:T(8,128)(2,1)}, bf16[4,192,128]{2,1,0:T(8,128)(2,1)}) custom-call(s32[4]{0:T(128)S(1)} %pad_add_fusion.place_ref.refs_0_, f32[2,384,128]{2,1,0:T(8,128)S(1)} %get-tuple-element.23.refs_1_, f32[2,192,128]{2,1,0:T(8,128)S(1)} %get-tuple-element.24.refs_2_, bf16[2,9,576,384]{3,2,1,0:T(8,128)(2,1)S(1)} %bitcast.25, ...), custom_call_target="tpu_custom_call" | custom-call | tf_op jit(solution)/shard_map/second/pallas_call | solution.py:206
  (31 shorter events, 8.5 us)
Async XLA Ops:
  1.7 13.6 %collective-permute-start.2 = (bf16[8,192,128]{2,1,0:T(8,128)(2,1)S(1)}, bf16[8,192,128]{2,1,0:T(8,128)(2,1)S(1)}, u32[]{:S(2)}, u32[]{:S(2)}) collective-permute-start(bf16[8,192,128]{2,1,0:T(8,128)(2,1)S(1)} %pad_maximum_fusion.2.refs_4_.refs_8_.refs_6_.refs_12_), channel_id=1, source_target_pairs={{8,16},{12,20},{16,8},{20,12},{9,17},{13,21},{17,9},{21,13},{10,18... | collective-permute-start | bytes 1179656 | tf_op jit(solution)/shard_map/ppermute | solution.py:237
  2.4 14.7 %collective-permute-start.1 = (bf16[8,192,128]{2,1,0:T(8,128)(2,1)S(1)}, bf16[8,192,128]{2,1,0:T(8,128)(2,1)S(1)}, u32[]{:S(2)}, u32[]{:S(2)}) collective-permute-start(bf16[8,192,128]{2,1,0:T(8,128)(2,1)S(1)} %pad_maximum_fusion.2.refs_4_.refs_8_.refs_6_.refs_12_), channel_id=1, source_target_pairs={{0,8},{4,12},{8,0},{12,4},{16,24},{20,28},{24,16},{28,20},{1,9},{5... | collective-permute-start | bytes 1179656 | tf_op jit(solution)/shard_map/ppermute | solution.py:236
  8.3 10.3 %collective-permute-start = (bf16[8,192,128]{2,1,0:T(8,128)(2,1)S(1)}, bf16[8,192,128]{2,1,0:T(8,128)(2,1)S(1)}, u32[]{:S(2)}, u32[]{:S(2)}) collective-permute-start(bf16[8,192,128]{2,1,0:T(8,128)(2,1)S(1)} %pad_maximum_fusion.2.refs_4_.refs_8_.refs_6_.refs_12_), channel_id=1, source_target_pairs={{0,4},{4,0},{8,12},{12,8},{16,20},{20,16},{24,28},{28,24},{1,5},{5... | collective-permute-start | bytes 1179656 | tf_op jit(solution)/shard_map/ppermute | solution.py:235
  9.8 3.3 %copy-start = (bf16[1,2,192,3,3,3,384]{6,2,5,4,3,1,0:T(8,128)(2,1)S(1)}, bf16[1,2,192,3,3,3,384]{6,2,5,4,3,1,0:T(8,128)(2,1)}, u32[]{:S(2)}) copy-start(bf16[1,2,192,3,3,3,384]{6,2,5,4,3,1,0:T(8,128)(2,1)} %param.7) | copy-start | bytes 23887876
  13.1 0.7 copy-start.2
  13.8 0.7 copy-start.3
  14.5 7.8 %copy-start.1 = (bf16[1,2,192,3,3,3,384]{6,2,5,4,3,1,0:T(8,128)(2,1)S(1)}, bf16[1,2,192,3,3,3,384]{6,2,5,4,3,1,0:T(8,128)(2,1)}, u32[]{:S(2)}) copy-start(bf16[1,2,192,3,3,3,384]{6,2,5,4,3,1,0:T(8,128)(2,1)} %param.7) | copy-start | bytes 23887876
  18.8 3.5 %collective-permute-start.5 = (bf16[24,192,128]{2,1,0:T(8,128)(2,1)S(1)}, bf16[24,192,128]{2,1,0:T(8,128)(2,1)S(1)}, u32[]{:S(2)}, u32[]{:S(2)}) collective-permute-start(bf16[24,192,128]{2,1,0:T(8,128)(2,1)S(1)} %pad_maximum_fusion.refs_6_.refs_10_.refs_8_), channel_id=1, source_target_pairs={{0,1},{1,0},{2,3},{3,2},{4,5},{5,4},{6,7},{7,6},{8,9},{9,8},{10,11... | collective-permute-start | bytes 3538952 | tf_op jit(solution)/shard_map/ppermute | solution.py:219
  18.8 3.4 %collective-permute-start.4 = (bf16[8,192,128]{2,1,0:T(8,128)(2,1)S(1)}, bf16[8,192,128]{2,1,0:T(8,128)(2,1)S(1)}, u32[]{:S(2)}, u32[]{:S(2)}) collective-permute-start(bf16[8,192,128]{2,1,0:T(8,128)(2,1)S(1)} %pad_maximum_fusion.2.refs_4_.refs_8_.refs_6_.refs_12_), channel_id=1, source_target_pairs={{0,1},{1,0},{2,3},{3,2},{4,5},{5,4},{6,7},{7,6},{8,9},{9,8},{10,11... | collective-permute-start | bytes 1179656 | tf_op jit(solution)/shard_map/ppermute | solution.py:219
  19.3 11.1 %collective-permute-start.3 = (bf16[8,192,128]{2,1,0:T(8,128)(2,1)S(1)}, bf16[8,192,128]{2,1,0:T(8,128)(2,1)S(1)}, u32[]{:S(2)}, u32[]{:S(2)}) collective-permute-start(bf16[8,192,128]{2,1,0:T(8,128)(2,1)S(1)} %get-tuple-element.43), channel_id=1, source_target_pairs={{0,4},{4,0},{8,12},{12,8},{16,20},{20,16},{24,28},{28,24},{1,5},{5... | collective-permute-start | bytes 1179656 | tf_op jit(solution)/shard_map/ppermute | solution.py:242
  30.4 1.7 %collective-permute-start.6 = (bf16[8,192,128]{2,1,0:T(8,128)(2,1)S(1)}, bf16[8,192,128]{2,1,0:T(8,128)(2,1)S(1)}, u32[]{:S(2)}, u32[]{:S(2)}) collective-permute-start(bf16[8,192,128]{2,1,0:T(8,128)(2,1)S(1)} %collective-permute-done.3.refs_4_.refs_6_.refs_10_), channel_id=1, source_target_pairs={{0,1},{1,0},{2,3},{3,2},{4,5},{5,4},{6,7},{7,6},{8,9},{9,8},{10,11... | collective-permute-start | bytes 1179656 | tf_op jit(solution)/shard_map/ppermute | solution.py:219
  34.8 2.1 %collective-permute-start.7 = (bf16[12,192,128]{2,1,0:T(8,128)(2,1)S(1)}, bf16[12,192,128]{2,1,0:T(8,128)(2,1)S(1)}, u32[]{:S(2)}, u32[]{:S(2)}) collective-permute-start(bf16[12,192,128]{2,1,0:T(8,128)(2,1)S(1)} %far_row.2.refs_4_), channel_id=1, source_target_pairs={{0,1},{1,0},{2,3},{3,2},{4,5},{5,4},{6,7},{7,6},{8,9},{9,8},{10,11... | collective-permute-start | bytes 1769480 | tf_op jit(solution)/shard_map/ppermute | solution.py:219
  40.3 7.0 %collective-permute-start.8 = (bf16[4,192,128]{2,1,0:T(8,128)(2,1)S(1)}, bf16[4,192,128]{2,1,0:T(8,128)(2,1)S(1)}, u32[]{:S(2)}, u32[]{:S(2)}) collective-permute-start(bf16[4,192,128]{2,1,0:T(8,128)(2,1)S(1)} %get-tuple-element.32.refs_14_), channel_id=1, source_target_pairs={{0,2},{2,0},{1,3},{3,1},{4,6},{6,4},{5,7},{7,5},{8,10},{10,8},{9,1... | collective-permute-start | bytes 589832 | tf_op jit(solution)/shard_map/ppermute | solution.py:302
  47.3 4.5 %collective-permute-start.10 = (bf16[4,192,128]{2,1,0:T(8,128)(2,1)S(1)}, bf16[4,192,128]{2,1,0:T(8,128)(2,1)S(1)}, u32[]{:S(2)}, u32[]{:S(2)}) collective-permute-start(bf16[4,192,128]{2,1,0:T(8,128)(2,1)S(1)} %collective-permute-done.8.refs_4_.refs_12_), channel_id=1, source_target_pairs={{8,16},{12,20},{16,8},{20,12},{9,17},{13,21},{17,9},{21,13},{10,18... | collective-permute-start | bytes 589832 | tf_op jit(solution)/shard_map/ppermute | solution.py:237
  48.2 6.2 %collective-permute-start.9 = (bf16[4,192,128]{2,1,0:T(8,128)(2,1)S(1)}, bf16[4,192,128]{2,1,0:T(8,128)(2,1)S(1)}, u32[]{:S(2)}, u32[]{:S(2)}) collective-permute-start(bf16[4,192,128]{2,1,0:T(8,128)(2,1)S(1)} %collective-permute-done.8.refs_4_.refs_12_), channel_id=1, source_target_pairs={{0,8},{4,12},{8,0},{12,4},{16,24},{20,28},{24,16},{28,20},{1,9},{5... | collective-permute-start | bytes 589832 | tf_op jit(solution)/shard_map/ppermute | solution.py:236
  50.3 5.7 %collective-permute-start.13 = (bf16[4,192,128]{2,1,0:T(8,128)(2,1)S(1)}, bf16[4,192,128]{2,1,0:T(8,128)(2,1)S(1)}, u32[]{:S(2)}, u32[]{:S(2)}) collective-permute-start(bf16[4,192,128]{2,1,0:T(8,128)(2,1)S(1)} %collective-permute-done.8.refs_4_.refs_12_), channel_id=1, source_target_pairs={{0,4},{4,0},{8,12},{12,8},{16,20},{20,16},{24,28},{28,24},{1,5},{5... | collective-permute-start | bytes 589832 | tf_op jit(solution)/shard_map/ppermute | solution.py:235
  56.0 2.4 %collective-permute-start.14 = (bf16[12,192,128]{2,1,0:T(8,128)(2,1)S(1)}, bf16[12,192,128]{2,1,0:T(8,128)(2,1)S(1)}, u32[]{:S(2)}, u32[]{:S(2)}) collective-permute-start(bf16[12,192,128]{2,1,0:T(8,128)(2,1)S(1)} %pad_maximum_fusion.1.refs_6_), channel_id=1, source_target_pairs={{0,1},{1,0},{2,3},{3,2},{4,5},{5,4},{6,7},{7,6},{8,9},{9,8},{10,11... | collective-permute-start | bytes 1769480 | tf_op jit(solution)/shard_map/ppermute | solution.py:219
  56.1 2.3 %collective-permute-start.12 = (bf16[4,192,128]{2,1,0:T(8,128)(2,1)S(1)}, bf16[4,192,128]{2,1,0:T(8,128)(2,1)S(1)}, u32[]{:S(2)}, u32[]{:S(2)}) collective-permute-start(bf16[4,192,128]{2,1,0:T(8,128)(2,1)S(1)} %collective-permute-done.8.refs_4_.refs_12_), channel_id=1, source_target_pairs={{0,1},{1,0},{2,3},{3,2},{4,5},{5,4},{6,7},{7,6},{8,9},{9,8},{10,11... | collective-permute-start | bytes 589832 | tf_op jit(solution)/shard_map/ppermute | solution.py:219
  56.6 8.2 %collective-permute-start.11 = (bf16[4,192,128]{2,1,0:T(8,128)(2,1)S(1)}, bf16[4,192,128]{2,1,0:T(8,128)(2,1)S(1)}, u32[]{:S(2)}, u32[]{:S(2)}) collective-permute-start(bf16[4,192,128]{2,1,0:T(8,128)(2,1)S(1)} %get-tuple-element.45), channel_id=1, source_target_pairs={{0,4},{4,0},{8,12},{12,8},{16,20},{20,16},{24,28},{28,24},{1,5},{5... | collective-permute-start | bytes 589832 | tf_op jit(solution)/shard_map/ppermute | solution.py:242
  64.8 1.5 %collective-permute-start.15 = (bf16[4,192,128]{2,1,0:T(8,128)(2,1)S(1)}, bf16[4,192,128]{2,1,0:T(8,128)(2,1)S(1)}, u32[]{:S(2)}, u32[]{:S(2)}) collective-permute-start(bf16[4,192,128]{2,1,0:T(8,128)(2,1)S(1)} %collective-permute-done.11.refs_4_), channel_id=1, source_target_pairs={{0,1},{1,0},{2,3},{3,2},{4,5},{5,4},{6,7},{7,6},{8,9},{9,8},{10,11... | collective-permute-start | bytes 589832 | tf_op jit(solution)/shard_map/ppermute | solution.py:219
  68.9 2.1 %collective-permute-start.16 = (bf16[12,192,128]{2,1,0:T(8,128)(2,1)S(1)}, bf16[12,192,128]{2,1,0:T(8,128)(2,1)S(1)}, u32[]{:S(2)}, u32[]{:S(2)}) collective-permute-start(bf16[12,192,128]{2,1,0:T(8,128)(2,1)S(1)} %far_row.3.refs_4_), channel_id=1, source_target_pairs={{0,1},{1,0},{2,3},{3,2},{4,5},{5,4},{6,7},{7,6},{8,9},{9,8},{10,11... | collective-permute-start | bytes 1769480 | tf_op jit(solution)/shard_map/ppermute | solution.py:219

commit v4 on v3

--- a/solution.py
+++ b/solution.py
@@ -13,7 +13,7 @@
 MIB = 1024 * 1024
 VMEM = pl.BlockSpec(memory_space=pltpu.VMEM)
 SMEM = pl.BlockSpec(memory_space=pltpu.SMEM)
-TAILS = 4
+TAILS = 2
 
 
 def params(mib):
@@ -58,8 +58,8 @@
 
 
 class Part:
-    def __init__(self, conv, ref, count):
-        self.conv, self.ref, self.count = conv, ref, count
+    def __init__(self, conv, ref):
+        self.conv, self.ref = conv, ref
         self.window = ref["window"]
         self.weight = ref["weight"]
         _, self.taps, height, self.depth = self.weight.shape
@@ -89,18 +89,21 @@
 
     def cached(self, slot, name, tile):
         for f in range(2):
-            for h, value in enumerate(self.ordered(name, tile + 2 * self.conv + f)):
+            for h, value in enumerate(self.ordered(name, tile + f)):
                 self.window[slot, f, h * self.channels : (h + 1) * self.channels, :] = value
 
-    def product(self, slots, first, frames):
+    def product(self, slots, first, frames, held=(True, True)):
         block, weight = [], []
+        nothing = jnp.zeros((self.depth, LANES), BF16)
         for slot, tap in slots:
             row_tap = 1 + self.side * (tap - 1)
             for a in range(3):
-                weight.append(self.weight[self.conv, 3 * a + row_tap])
-                block.append(
-                    jnp.concatenate([self.window[slot, first + f + a] for f in range(frames)], axis=1)
-                )
+                wanted = [first + f + a for f in range(frames)]
+                here = [held[0 if frame < 2 else 1] for frame in wanted]
+                if any(here):
+                    tile = [self.window[slot, frame] if h else nothing for frame, h in zip(wanted, here)]
+                    weight.append(self.weight[self.conv, 3 * a + row_tap])
+                    block.append(jnp.concatenate(tile, axis=1))
         total = jnp.dot(
             jnp.concatenate(weight, axis=1), jnp.concatenate(block, axis=0), preferred_element_type=F32
         )
@@ -117,54 +120,112 @@
 
 def near_kernel(frames, base, names, *refs):
     ref = dict(zip(names, refs))
-    part = Part(0, ref, frames)
-    sums = ref["sums"]
+    part = Part(0, ref)
+    half = frames // 2
     bias = ref["biases"][0]
     places = [("own", 0), ("beside", 0), ("beside", 1), ("beside", 2)]
-    cache_tiles = ref["tails_own"].shape[0]
-
-    def load(slot):
+
+    def load(slot, first):
         name, group = places[slot]
-        part.cached(slot, "tails_" + name, group * cache_tiles)
-        for f in range(frames):
+        if first == 0:
+            part.cached(slot, "tails_" + name, group * ref["tails_own"].shape[0])
+        for f in range(first, first + half):
             kept = part.activate(slot, f, name, group * (frames + base) + base + f)
             if slot == 0 and f >= frames - 2:
                 ref["kept"][f - frames + 2] = kept
 
-    def store(o, slots):
-        for f, value in enumerate(part.product(slots, 0, frames)):
-            sums[(o + 1) * frames + f] = value + bias
-
-    load(0)
-    load(1)
-    store(0, [(1, 0), (0, 1)])
-    load(2)
-    store(-1, [(2, 0), (1, 1), (0, 2)])
-    load(3)
-    store(1, [(0, 0), (3, 2)])
+    def store(q, slots, first):
+        for f, value in enumerate(part.product(slots, first, half), first):
+            ref["sums"][(q + 1) * frames + f] = value + bias
+
+    for first in (0, half):
+        load(0, first)
+        load(1, first)
+        store(0, [(1, 0), (0, 1)], first)
+        load(2, first)
+        store(-1, [(2, 0), (1, 1), (0, 2)], first)
+        load(3, first)
+        store(1, [(0, 0), (3, 2)], first)
+
+
+def cached_kernel(names, *refs):
+    ref = dict(zip(names, refs))
+    first, second = Part(0, ref), Part(1, ref)
+    tails = ref["tails_own"].shape[0]
+    held = (True, False)
+    first.cached(0, "tails_own", 0)
+    for group in range(3):
+        first.cached(1 + group, "tails_beside", group * tails)
+    first.cached(4, "tails_diagonal", 0)
+    for q, slots in ((-1, [(2, 0), (1, 1), (0, 2)]), (0, [(1, 0), (0, 1), (4, 2)]), (1, [(0, 0), (4, 1), (3, 2)])):
+        for f, value in enumerate(first.product(slots, 0, 2, held)):
+            ref["cached_sums"][2 * (q + 1) + f] = value + ref["biases"][0]
+    for slot in range(3):
+        second.cached(5 + slot, "seconds", TAILS * slot)
+    for f, value in enumerate(second.product([(6, 0), (5, 1), (7, 2)], 0, 2, held)):
+        ref["cached_seconds"][f] = value + ref["biases"][1]
+
+
+def own_kernel(frames, names, *refs):
+    ref = dict(zip(names, refs))
+    part = Part(0, ref)
+    half = frames // 2
+    for first in (0, half):
+        for f in range(first, first + half):
+            kept = part.activate(0, f, "own", f)
+            if f >= frames - 2:
+                ref["kept"][f - frames + 2] = kept
+        for q in (-1, 0, 1):
+            for f, value in enumerate(part.product([(0, 1 - q)], first, half, (False, True)), first):
+                before = ref["cached_sums"][2 * (q + 1) + f] if f < 2 else ref["biases"][0]
+                ref["sums"][(q + 1) * frames + f] = value + before
+
+
+def beside_kernel(frames, names, *refs):
+    ref = dict(zip(names, refs))
+    part = Part(0, ref)
+    half = frames // 2
+
+    def load(slot, first):
+        for f in range(first, first + half):
+            part.activate(slot, f, "beside", slot * frames + f)
+
+    def store(q, slots, first):
+        for f, value in enumerate(part.product(slots, first, half, (False, True)), first):
+            at = (q + 1) * frames + f
+            ref["sums"][at] = ref["sums_before"][at] + value
+
+    for first in (0, half):
+        load(0, first)
+        store(0, [(0, 0)], first)
+        load(1, first)
+        store(-1, [(1, 0), (0, 1)], first)
+        load(2, first)
+        store(1, [(2, 2)], first)
 
 
 def far_kernel(frames, base, names, *refs):
     ref = dict(zip(names, refs))
-    part = Part(0, ref, frames)
+    part = Part(0, ref)
+    half = frames // 2
     out, sums = ref["out"], ref["sums"]
-    part.cached(0, "tails_diagonal", 0)
-    for f in range(frames):
-        part.activate(0, f, "diagonal", base + f)
-    for f in range(frames):
-        out[f] = sums[f].astype(BF16)
-    for o, tap in ((0, 2), (1, 1)):
-        for f, value in enumerate(part.product([(0, tap)], 0, frames)):
-            at = (o + 1) * frames + f
-            out[at] = (sums[at] + value).astype(BF16)
+    if base:
+        part.cached(0, "tails_diagonal", 0)
+    for first in (0, half):
+        for f in range(first, first + half):
+            part.activate(0, f, "diagonal", base + f)
+            out[f] = sums[f].astype(BF16)
+        for q, tap in ((0, 2), (1, 1)):
+            for f, value in enumerate(part.product([(0, tap)], first, half, (base > 0, True)), first):
+                at = (q + 1) * frames + f
+                out[at] = (sums[at] + value).astype(BF16)
 
 
 def second_kernel(frames, base, period, count, names, *refs):
     ref = dict(zip(names, refs))
-    part = Part(1, ref, frames)
+    part = Part(1, ref)
     row, segment = ref["place"][2], ref["place"][3]
     bias = ref["biases"][1]
-    places = [("tails_own", 0), ("tails_beside", 0), ("tails_diagonal", 0)]
     offsets = (0, -1, 1)
 
     def load(first, last):
@@ -179,15 +240,17 @@
     new_tails = {f: ref["kept"][f] for f in range(2)}
 
     def store(first, last):
-        sums = part.product([(1, 0), (0, 1), (2, 2)], first, last - first)
+        sums = part.product([(1, 0), (0, 1), (2, 2)], first, last - first, (period == 0, True))
         for f, value in enumerate(sums, first):
-            result = (ref["source"][base + f].astype(F32) + (value + bias)).astype(BF16)
+            before = ref["cached_seconds"][f] if period and f < 2 else bias
+            result = (ref["source"][base + f].astype(F32) + (value + before)).astype(BF16)
             if "result" in ref:
                 ref["result"][f] = result
             ref["out"][f] = jnp.where(segment == period, result, ref["older"][f]) if period else result
 
-    for slot, (name, tile) in enumerate(places):
-        part.cached(slot, name, tile)
+    if period == 0:
+        for slot in range(len(offsets)):
+            part.cached(slot, "seconds", TAILS * slot)
     half = frames // 2
     load(0, half)
     store(0, half)
@@ -223,24 +286,19 @@
     return {name: x, name + "_other": swapped(x)}
 
 
-def exchanged(x, count, kind, pair, *beside_it):
+def across(count):
+    return [(i, i ^ 1) for i in range(count)]
+
+
+def exchanged(x, count):
     pairs = count // 2
-    across = [(i, i ^ 1) for i in range(count)]
     even, odd = [], []
     for i in range(count):
         k = i // 2
         for k_to, group in ((k ^ 1, even), (k + 1 if k % 2 else k - 1, odd)):
             if 0 <= k_to < pairs:
                 group.append((i, 2 * k_to + i % 2))
-    beside = lax.ppermute(x, "rows", across)
-    a = lax.ppermute(x, "rows", even)
-    b = lax.ppermute(x, "rows", odd)
-    if beside_it:
-        beside, a, b, beside_it = lax.optimization_barrier((beside, a, b, beside_it))
-    to_a = kind == pair % 2
-    near, far = jnp.where(to_a, a, b), jnp.where(to_a, b, a)
-    diagonal = lax.ppermute(near, "rows", across)
-    return jnp.concatenate([beside, near, far], axis=0), diagonal, beside_it
+    return [lax.ppermute(x, "rows", pairs) for pairs in (across(count), even, odd)]
 
 
 def shards(features, caches, conv_weights, conv_bias, norm_gain):
@@ -254,52 +312,71 @@
     place = [lax.axis_index("chan"), 2 * kind - 1, row, lax.axis_index("segment")]
     place = jnp.stack(place).astype(jnp.int32)
 
-    source = jnp.concatenate([caches[0].reshape(TAILS, channels, LANES), features[:, 0]], axis=0)
-    fixed = prepared(place, norm_gain[0], conv_bias[0], kernels, channels)
-    out = tails = None
-    cached = {}
+    source = jnp.concatenate([caches[0].reshape(2 * TAILS, channels, LANES), features[:, 0]], axis=0)
+    gains, biases = prepared(place, norm_gain[0], conv_bias[0], kernels, channels)
+    source = jnp.concatenate([caches[0].reshape(2 * TAILS, channels, LANES), features[:, 0]], axis=0)
+    sums_shape, kept_shape = tiles(3 * frames, channels, F32), tiles(2, channels)
+    near_first = kind == pair % 2
+    out = tails = cached_seconds = None
     for period in range(segments):
-        base = TAILS if period == 0 else 0
-        own = with_other("own", source)
-        beside, diagonal, done = exchanged(source, count, kind, pair, *(() if period else fixed))
-        beside = with_other("beside", beside)
+        base = 0 if period else TAILS
+        beside, even, odd = exchanged(source, count)
         if period == 0:
-            common = {"place": place, "gains": done[0], "biases": done[1], "weight": kernels}
-            cached = {"tails_" + key: value for key, value in (own | beside).items()}
-        tails_of = lambda *keys: {"tails_" + k + o: cached["tails_" + k + o] for k in keys for o in ("", "_other")}
-        outs = {"sums": tiles(3 * frames, channels, F32), "kept": tiles(2, channels)}
-        near = call(
-            functools.partial(near_kernel, frames, base),
-            "near_rows",
-            common | own | beside | tails_of("own", "beside"),
-            outs,
-            4,
-        )
-        diagonal, sums = lax.optimization_barrier((diagonal, near["sums"]))
-        diagonal = with_other("diagonal", diagonal)
+            beside, even, odd, gains, biases = lax.optimization_barrier((beside, even, odd, gains, biases))
+            common = {"place": place, "gains": gains, "biases": biases, "weight": kernels}
+        else:
+            arrays = common | with_other("own", source) | {"cached_sums": cached_sums}
+            outs = {"sums": sums_shape, "kept": kept_shape}
+            first = call(functools.partial(own_kernel, frames), "own_row", arrays, outs, 1)
+            sums, kept = first["sums"], first["kept"]
+            even, odd, sums, kept = lax.optimization_barrier((even, odd, sums, kept))
+        near, far = jnp.where(near_first, even, odd), jnp.where(near_first, odd, even)
         if period == 0:
-            cached |= {"tails_" + key: value for key, value in diagonal.items()}
-        middle = call(
-            functools.partial(far_kernel, frames, base),
-            "far_row",
-            common | diagonal | tails_of("diagonal") | {"sums": sums},
-            {"out": tiles(3 * frames, channels)},
-            1,
-        )["out"]
-        arrays = common | with_other("middle", middle) | tails_of("own", "beside", "diagonal")
-        arrays |= {"source": source, "kept": near["kept"]}
-        outs = {"out": tiles(frames, channels), "tails": tiles(TAILS, channels)}
+            seconds = [x[TAILS : 2 * TAILS] for x in (source, beside, near)]
+            source, beside, near, far = [
+                jnp.concatenate([x[:TAILS], x[2 * TAILS :]], axis=0) for x in (source, beside, near, far)
+            ]
+        diagonal = lax.ppermute(near, "rows", across(count))
+        arrays = with_other("beside", jnp.concatenate([beside, near, far], axis=0))
+        if period == 0:
+            arrays |= with_other("own", source)
+            cached = {"tails_" + key: value for key, value in arrays.items()}
+            outs = {"sums": sums_shape, "kept": kept_shape}
+            first = call(functools.partial(near_kernel, frames, base), "near_rows", common | arrays | cached, outs, 4)
+            sums, kept = first["sums"], first["kept"]
+        else:
+            arrays |= common | {"sums_before": sums}
+            sums = call(functools.partial(beside_kernel, frames), "beside_rows", arrays, {"sums": sums_shape}, 3)["sums"]
+        diagonal, sums = lax.optimization_barrier((diagonal, sums))
+        arrays = with_other("diagonal", diagonal)
+        if period == 0:
+            away = {"tails_" + key: value for key, value in arrays.items()}
+            seconds, sums = lax.optimization_barrier((seconds, sums))
+            seconds[2] = lax.ppermute(seconds[2], "rows", across(count))
+            seconds = with_other("seconds", jnp.concatenate(seconds, axis=0))
+            arrays |= away
+        arrays |= common | {"sums": sums}
+        outs = {"out": tiles(3 * frames, channels)}
+        middle = call(functools.partial(far_kernel, frames, base), "far_row", arrays, outs, 1)["out"]
+        arrays = common | with_other("middle", middle) | {"source": source, "kept": kept}
+        outs = {"out": tiles(frames, channels), "tails": tiles(2 * TAILS, channels)}
         if period:
-            arrays |= {"older": out, "older_tails": tails}
+            arrays |= {"older": out, "older_tails": tails, "cached_seconds": cached_seconds}
             if period < segments - 1:
                 outs["result"] = tiles(frames, channels)
-        second = call(
-            functools.partial(second_kernel, frames, base, period, count), "second", arrays, outs, 3
-        )
+        else:
+            arrays |= seconds
+        second = call(functools.partial(second_kernel, frames, base, period, count), "second", arrays, outs, 3)
         out, tails = second["out"], second["tails"]
         if period < segments - 1:
             result = second["result"] if period else out
             source = lax.ppermute(result, "segment", [(i, (i + 1) % segments) for i in range(segments)])
+            if period == 0:
+                arrays, result = lax.optimization_barrier((common | cached | away | seconds, result))
+                outs = {"cached_sums": tiles(6, channels, F32), "cached_seconds": tiles(2, channels, F32)}
+                sums = call(cached_kernel, "cached_rows", arrays, outs, 8)
+                cached_sums, cached_seconds = sums["cached_sums"], sums["cached_seconds"]
+                source, cached_sums, cached_seconds = lax.optimization_barrier((source, cached_sums, cached_seconds))
     return (out[None, :, None], tails.reshape(1, 2, 2, 1, channels, LANES))
 
 

time: 75.4 us -> 73.5 us (0.975)
  starting transfers between devices: 18.8 us -> 15 us
  Pallas kernels: 26.5 us -> 29.7 us
  waiting for transfers between devices: 23.1 us -> 20.4 us
  local copies, waits for them, and re-layouts: 4.63 us -> 5.61 us
    ppermute x1, waiting for transfers between devices: 5.42 us -> 1.62 us  [shards(): lax.ppermute(result, 'segment', [(i, (i + 1) % segments) for i in range(s...]
    pallas_call x6 -> x8, Pallas kernels: 25.6 us -> 28.9 us  [call(): pl.pallas_call(functools.partial(kernel, names), out_shape=list(outs.valu...]
    ppermute x8 -> x9, starting transfers between devices: 15.5 us -> 12.7 us  [the longest x6 11.3 us: exchanged(): lax.ppermute(x, 'rows', pairs)]
    ppermute x8 -> x9, starting transfers between devices: 1.75 us -> 0.71 us  [swapped(): return lax.ppermute(x, 'chan', [(0, 1), (1, 0)])]
    unnamed x8 -> x17, local copies, waits for them, and re-layouts: 4.63 us -> 5.5 us
    ppermute x8 -> x9, waiting for transfers between devices: 9.21 us -> 9.81 us  [the longest x6 6.23 us: exchanged(): lax.ppermute(x, 'rows', pairs)]
    ppermute x8 -> x9, waiting for transfers between devices: 8.45 us -> 8.99 us  [swapped(): return lax.ppermute(x, 'chan', [(0, 1), (1, 0)])]
  transfers between devices with their start and end apart: 17 -> 19, of which waited for: 12 -> 14; matrix products, arithmetic and copies ran while one was open for 0% -> 0% of each run, Pallas kernels for 18% -> 28%
where the time goes in v4:
time: 73.5 us; the launch traced here: 72.9 us
  Pallas kernels  29.7 us (40%)
  waiting for transfers between devices  20.4 us (28%)
  starting transfers between devices  15 us (20%)
  local copies, waits for them, and re-layouts  5.61 us (8%)
  other arithmetic  1.35 us (2%)
  between operations  0.89 us (1%)
    pallas_call x8, Pallas kernels, call(): pl.pallas_call(functools.partial(kernel, names), out_shape=list(outs.valu...  28.9 us
    ppermute x6, starting transfers between devices, exchanged(): lax.ppermute(x, 'rows', pairs)  11.3 us
    ppermute x9, waiting for transfers between devices, swapped(): return lax.ppermute(x, 'chan', [(0, 1), (1, 0)])  8.99 us
    ppermute x6, waiting for transfers between devices, exchanged(): lax.ppermute(x, 'rows', pairs)  6.23 us
    unnamed x17, local copies, waits for them, and re-layouts  5.5 us
    ppermute x2, waiting for transfers between devices, shards(): diagonal = lax.ppermute(near, 'rows', across(count))  2.75 us
    ppermute x1, waiting for transfers between devices, shards(): lax.ppermute(result, 'segment', [(i, (i + 1) % segments) for i in range(s...  1.62 us
    ppermute x1, starting transfers between devices, shards(): lax.ppermute(result, 'segment', [(i, (i + 1) % segments) for i in range(s...  1.58 us
  transfers between devices with their start and end apart: 19, of which 14 were waited for; matrix products, arithmetic and copies ran while one was open for 0% of the time, Pallas kernels for 28%

profile of v4, /device:TPU:0, one launch (start us, length us, event | category | flops | bytes accessed | tf_op | source)
XLA Modules:
  0.0 72.9 jit_solution(248899453972886738)
XLA Ops:
  1.7 3.0 %collective-permute-start = (bf16[8,192,128]{2,1,0:T(8,128)(2,1)S(1)}, bf16[8,192,128]{2,1,0:T(8,128)(2,1)S(1)}, u32[]{:S(2)}, u32[]{:S(2)}) collective-permute-start(bf16[8,192,128]{2,1,0:T(8,128)(2,1)S(1)} %pad_maximum_fusion.1), channel_id=1, source_target_pairs={{0,4},{4,0},{8,12},{12,8},{16,20},{20,16},{24,28},{28,24},{1,5},{5... | collective-permute-start | bytes 1179656 | tf_op jit(solution)/shard_map/ppermute | solution.py:301
  4.7 1.6 %collective-permute-start.1 = (bf16[8,192,128]{2,1,0:T(8,128)(2,1)S(1)}, bf16[8,192,128]{2,1,0:T(8,128)(2,1)S(1)}, u32[]{:S(2)}, u32[]{:S(2)}) collective-permute-start(bf16[8,192,128]{2,1,0:T(8,128)(2,1)S(1)} %pad_maximum_fusion.1), channel_id=1, source_target_pairs={{0,8},{4,12},{8,0},{12,4},{16,24},{20,28},{24,16},{28,20},{1,9},{5... | collective-permute-start | bytes 1179656 | tf_op jit(solution)/shard_map/ppermute | solution.py:301
  7.1 3.3 %copy-done = bf16[1,2,192,3,3,3,384]{6,2,5,4,3,1,0:T(8,128)(2,1)S(1)} copy-done((bf16[1,2,192,3,3,3,384]{6,2,5,4,3,1,0:T(8,128)(2,1)S(1)}, bf16[1,2,192,3,3,3,384]{6,2,5,4,3,1,0:T(8,128)(2,1)}, u32[]{:S(2)}) %copy-start) | copy-done | bytes 7962648
  12.5 1.3 %collective-permute-done = bf16[8,192,128]{2,1,0:T(8,128)(2,1)S(1)} collective-permute-done((bf16[8,192,128]{2,1,0:T(8,128)(2,1)S(1)}, bf16[8,192,128]{2,1,0:T(8,128)(2,1)S(1)}, u32[]{:S(2)}, u32[]{:S(2)}) %collective-permute-start) | collective-permute-done | bytes 393248 | tf_op jit(solution)/shard_map/ppermute | solution.py:301
  13.8 1.5 %collective-permute-done.1 = bf16[8,192,128]{2,1,0:T(8,128)(2,1)S(1)} collective-permute-done((bf16[8,192,128]{2,1,0:T(8,128)(2,1)S(1)}, bf16[8,192,128]{2,1,0:T(8,128)(2,1)S(1)}, u32[]{:S(2)}, u32[]{:S(2)}) %collective-permute-start.1) | collective-permute-done | bytes 393248 | tf_op jit(solution)/shard_map/ppermute | solution.py:301
  17.0 1.5 %collective-permute-done.5.refs_7_.refs_11_.refs_10_ = bf16[6,192,128]{2,1,0:T(8,128)(2,1)S(1)} collective-permute-done((bf16[6,192,128]{2,1,0:T(8,128)(2,1)S(1)}, bf16[6,192,128]{2,1,0:T(8,128)(2,1)S(1)}, u32[]{:S(2)}, u32[]{:S(2)}) %collective-permute-start.5) | collective-permute-done | bytes 294944 | tf_op jit(solution)/shard_map/ppermute | solution.py:282
  18.5 6.4 %near_rows.1 = (f32[12,192,128]{2,1,0:T(8,128)S(1)}, bf16[2,192,128]{2,1,0:T(8,128)(2,1)S(1)}) custom-call(s32[4]{0:T(128)S(1)} %pad_add_fusion.place_ref.refs_0_.refs_4_.refs_2_, f32[2,384,128]{2,1,0:T(8,128)S(1)} %get-tuple-element.63.refs_1_.refs_5_.refs_3_, f32[2,192,128]{2,1,0:T(8,128)S(1)} %get-tuple-element.62.refs_2_.refs_6_.refs_0_.refs_4_, ...), custom_call_target="tpu_custom_call" | custom-call | tf_op jit(solution)/shard_map/near_rows/pallas_call | solution.py:269
  26.4 1.2 %collective-permute-done.6.refs_1_.refs_3_.refs_8_ = bf16[6,192,128]{2,1,0:T(8,128)(2,1)S(1)} collective-permute-done((bf16[6,192,128]{2,1,0:T(8,128)(2,1)S(1)}, bf16[6,192,128]{2,1,0:T(8,128)(2,1)S(1)}, u32[]{:S(2)}, u32[]{:S(2)}) %collective-permute-start.6) | collective-permute-done | bytes 294944 | tf_op jit(solution)/shard_map/ppermute | solution.py:282
  27.6 2.5 %far_row.2.refs_4_ = bf16[12,192,128]{2,1,0:T(8,128)(2,1)S(1)} custom-call(bf16[6,192,128]{2,1,0:T(8,128)(2,1)S(1)} %collective-permute-done.3.refs_0_.refs_2_.refs_7_, bf16[6,192,128]{2,1,0:T(8,128)(2,1)S(1)} %collective-permute-done.6.refs_1_.refs_3_.refs_8_, bf16[6,192,128]{2,1,0:T(8,128)(2,1)S(1)} %collective-permute-done.3.refs_0_.refs_2_.refs_7_, ...), custom_call_target="tpu_custom_call" | custom-call | tf_op jit(solution)/shard_map/far_row/pallas_call | solution.py:269
  31.3 1.6 %collective-permute-done.9.refs_9_.refs_4_ = bf16[6,192,128]{2,1,0:T(8,128)(2,1)S(1)} collective-permute-done((bf16[6,192,128]{2,1,0:T(8,128)(2,1)S(1)}, bf16[6,192,128]{2,1,0:T(8,128)(2,1)S(1)}, u32[]{:S(2)}, u32[]{:S(2)}) %collective-permute-start.9) | collective-permute-done | bytes 294944 | tf_op jit(solution)/shard_map/ppermute | solution.py:282
  32.9 3.5 %second.2 = (bf16[4,192,128]{2,1,0:T(8,128)(2,1)S(1)}, bf16[4,192,128]{2,1,0:T(8,128)(2,1)S(1)}) custom-call(s32[4]{0:T(128)S(1)} %pad_add_fusion.place_ref.refs_0_.refs_4_.refs_2_, f32[2,384,128]{2,1,0:T(8,128)S(1)} %get-tuple-element.63.refs_1_.refs_5_.refs_3_, f32[2,192,128]{2,1,0:T(8,128)S(1)} %get-tuple-element.62.refs_2_.refs_6_.refs_0_.refs_4_, ...), custom_call_target="tpu_custom_call" | custom-call | tf_op jit(solution)/shard_map/second/pallas_call | solution.py:269
  36.4 1.6 %collective-permute-start.10 = (bf16[4,192,128]{2,1,0:T(8,128)(2,1)S(1)}, bf16[4,192,128]{2,1,0:T(8,128)(2,1)S(1)}, u32[]{:S(2)}, u32[]{:S(2)}) collective-permute-start(bf16[4,192,128]{2,1,0:T(8,128)(2,1)S(1)} %get-tuple-element.61.refs_8_), channel_id=1, source_target_pairs={{0,2},{2,0},{1,3},{3,1},{4,6},{6,4},{5,7},{7,5},{8,10},{10,8},{9,1... | collective-permute-start | bytes 589832 | tf_op jit(solution)/shard_map/ppermute | solution.py:373
  38.0 3.8 %cached_rows.1 = (f32[6,192,128]{2,1,0:T(8,128)S(1)}, f32[2,192,128]{2,1,0:T(8,128)S(1)}) custom-call(f32[2,192,128]{2,1,0:T(8,128)S(1)} %get-tuple-element.62.refs_2_.refs_6_.refs_0_.refs_4_, f32[2,384,128]{2,1,0:T(8,128)S(1)} %get-tuple-element.63.refs_1_.refs_5_.refs_3_, s32[4]{0:T(128)S(1)} %pad_add_fusion.place_ref.refs_0_.refs_4_.refs_2_, ...), custom_call_target="tpu_custom_call" | custom-call | tf_op jit(solution)/shard_map/cached_rows/pallas_call | solution.py:269
  41.8 1.6 %collective-permute-done.10.refs_4_.refs_6_ = bf16[4,192,128]{2,1,0:T(8,128)(2,1)S(1)} collective-permute-done((bf16[4,192,128]{2,1,0:T(8,128)(2,1)S(1)}, bf16[4,192,128]{2,1,0:T(8,128)(2,1)S(1)}, u32[]{:S(2)}, u32[]{:S(2)}) %collective-permute-start.10) | collective-permute-done | bytes 196640 | tf_op jit(solution)/shard_map/ppermute | solution.py:373
  43.4 4.6 %collective-permute-start.11 = (bf16[4,192,128]{2,1,0:T(8,128)(2,1)S(1)}, bf16[4,192,128]{2,1,0:T(8,128)(2,1)S(1)}, u32[]{:S(2)}, u32[]{:S(2)}) collective-permute-start(bf16[4,192,128]{2,1,0:T(8,128)(2,1)S(1)} %collective-permute-done.10.refs_4_.refs_6_), channel_id=1, source_target_pairs={{0,8},{4,12},{8,0},{12,4},{16,24},{20,28},{24,16},{28,20},{1,9},{5... | collective-permute-start | bytes 589832 | tf_op jit(solution)/shard_map/ppermute | solution.py:301
  49.4 3.0 %own_row.1 = (f32[12,192,128]{2,1,0:T(8,128)S(1)}, bf16[2,192,128]{2,1,0:T(8,128)(2,1)S(1)}) custom-call(s32[4]{0:T(128)S(1)} %pad_add_fusion.place_ref.refs_0_.refs_4_.refs_2_, f32[2,384,128]{2,1,0:T(8,128)S(1)} %get-tuple-element.63.refs_1_.refs_5_.refs_3_, f32[2,192,128]{2,1,0:T(8,128)S(1)} %get-tuple-element.62.refs_2_.refs_6_.refs_0_.refs_4_, ...), custom_call_target="tpu_custom_call" | custom-call | tf_op jit(solution)/shard_map/own_row/pallas_call | solution.py:269
  53.6 2.3 %collective-permute-done.15 = bf16[4,192,128]{2,1,0:T(8,128)(2,1)S(1)} collective-permute-done((bf16[4,192,128]{2,1,0:T(8,128)(2,1)S(1)}, bf16[4,192,128]{2,1,0:T(8,128)(2,1)S(1)}, u32[]{:S(2)}, u32[]{:S(2)}) %collective-permute-start.15) | collective-permute-done | bytes 196640 | tf_op jit(solution)/shard_map/ppermute | solution.py:301
  56.7 1.4 %collective-permute-done.16.refs_1_ = bf16[12,192,128]{2,1,0:T(8,128)(2,1)S(1)} collective-permute-done((bf16[12,192,128]{2,1,0:T(8,128)(2,1)S(1)}, bf16[12,192,128]{2,1,0:T(8,128)(2,1)S(1)}, u32[]{:S(2)}, u32[]{:S(2)}) %collective-permute-start.16) | collective-permute-done | bytes 589856 | tf_op jit(solution)/shard_map/ppermute | solution.py:282
  58.1 3.7 %beside_rows.1.refs_6_ = f32[12,192,128]{2,1,0:T(8,128)S(1)} custom-call(bf16[12,192,128]{2,1,0:T(8,128)(2,1)S(1)} %pad_maximum_fusion.refs_0_, bf16[12,192,128]{2,1,0:T(8,128)(2,1)S(1)} %collective-permute-done.16.refs_1_, s32[4]{0:T(128)S(1)} %pad_add_fusion.place_ref.refs_0_.refs_4_.refs_2_, f32[2,384,128]{2,1,0:T(8,128)S(1)} %get-tuple-element.63.refs_1_.refs_5_.refs_3_, ...), custom_call_target="tpu_custom_call" | custom-call | tf_op jit(solution)/shard_map/beside_rows/pallas_call | solution.py:269
  61.8 1.6 %collective-permute-done.14.refs_0_ = bf16[4,192,128]{2,1,0:T(8,128)(2,1)S(1)} collective-permute-done((bf16[4,192,128]{2,1,0:T(8,128)(2,1)S(1)}, bf16[4,192,128]{2,1,0:T(8,128)(2,1)S(1)}, u32[]{:S(2)}, u32[]{:S(2)}) %collective-permute-start.14) | collective-permute-done | bytes 196640 | tf_op jit(solution)/shard_map/ppermute | solution.py:339
  63.4 1.4 %collective-permute-done.17.refs_1_ = bf16[4,192,128]{2,1,0:T(8,128)(2,1)S(1)} collective-permute-done((bf16[4,192,128]{2,1,0:T(8,128)(2,1)S(1)}, bf16[4,192,128]{2,1,0:T(8,128)(2,1)S(1)}, u32[]{:S(2)}, u32[]{:S(2)}) %collective-permute-start.17) | collective-permute-done | bytes 196640 | tf_op jit(solution)/shard_map/ppermute | solution.py:282
  64.8 2.3 %far_row.3.refs_4_ = bf16[12,192,128]{2,1,0:T(8,128)(2,1)S(1)} custom-call(bf16[4,192,128]{2,1,0:T(8,128)(2,1)S(1)} %collective-permute-done.14.refs_0_, bf16[4,192,128]{2,1,0:T(8,128)(2,1)S(1)} %collective-permute-done.17.refs_1_, s32[4]{0:T(128)S(1)} %pad_add_fusion.place_ref.refs_0_.refs_4_.refs_2_, ...), custom_call_target="tpu_custom_call" | custom-call | tf_op jit(solution)/shard_map/far_row/pallas_call | solution.py:269
  67.3 1.9 %collective-permute-done.18.refs_5_ = bf16[12,192,128]{2,1,0:T(8,128)(2,1)S(1)} collective-permute-done((bf16[12,192,128]{2,1,0:T(8,128)(2,1)S(1)}, bf16[12,192,128]{2,1,0:T(8,128)(2,1)S(1)}, u32[]{:S(2)}, u32[]{:S(2)}) %collective-permute-start.18) | collective-permute-done | bytes 589856 | tf_op jit(solution)/shard_map/ppermute | solution.py:282
  69.2 3.8 %second.3 = (bf16[4,192,128]{2,1,0:T(8,128)(2,1)}, bf16[4,192,128]{2,1,0:T(8,128)(2,1)}) custom-call(s32[4]{0:T(128)S(1)} %pad_add_fusion.place_ref.refs_0_.refs_4_.refs_2_, f32[2,384,128]{2,1,0:T(8,128)S(1)} %get-tuple-element.63.refs_1_.refs_5_.refs_3_, f32[2,192,128]{2,1,0:T(8,128)S(1)} %get-tuple-element.62.refs_2_.refs_6_.refs_0_.refs_4_, ...), custom_call_target="tpu_custom_call" | custom-call | tf_op jit(solution)/shard_map/second/pallas_call | solution.py:269
  (52 shorter events, 11.9 us)
Async XLA Ops:
  1.7 12.1 %collective-permute-start = (bf16[8,192,128]{2,1,0:T(8,128)(2,1)S(1)}, bf16[8,192,128]{2,1,0:T(8,128)(2,1)S(1)}, u32[]{:S(2)}, u32[]{:S(2)}) collective-permute-start(bf16[8,192,128]{2,1,0:T(8,128)(2,1)S(1)} %pad_maximum_fusion.1), channel_id=1, source_target_pairs={{0,4},{4,0},{8,12},{12,8},{16,20},{20,16},{24,28},{28,24},{1,5},{5... | collective-permute-start | bytes 1179656 | tf_op jit(solution)/shard_map/ppermute | solution.py:301
  4.7 10.6 %collective-permute-start.1 = (bf16[8,192,128]{2,1,0:T(8,128)(2,1)S(1)}, bf16[8,192,128]{2,1,0:T(8,128)(2,1)S(1)}, u32[]{:S(2)}, u32[]{:S(2)}) collective-permute-start(bf16[8,192,128]{2,1,0:T(8,128)(2,1)S(1)} %pad_maximum_fusion.1), channel_id=1, source_target_pairs={{0,8},{4,12},{8,0},{12,4},{16,24},{20,28},{24,16},{28,20},{1,9},{5... | collective-permute-start | bytes 1179656 | tf_op jit(solution)/shard_map/ppermute | solution.py:301
  6.3 9.0 %collective-permute-start.2 = (bf16[8,192,128]{2,1,0:T(8,128)(2,1)S(1)}, bf16[8,192,128]{2,1,0:T(8,128)(2,1)S(1)}, u32[]{:S(2)}, u32[]{:S(2)}) collective-permute-start(bf16[8,192,128]{2,1,0:T(8,128)(2,1)S(1)} %pad_maximum_fusion.1), channel_id=1, source_target_pairs={{8,16},{12,20},{16,8},{20,12},{9,17},{13,21},{17,9},{21,13},{10,18... | collective-permute-start | bytes 1179656 | tf_op jit(solution)/shard_map/ppermute | solution.py:301
  7.1 3.3 %copy-start = (bf16[1,2,192,3,3,3,384]{6,2,5,4,3,1,0:T(8,128)(2,1)S(1)}, bf16[1,2,192,3,3,3,384]{6,2,5,4,3,1,0:T(8,128)(2,1)}, u32[]{:S(2)}) copy-start(bf16[1,2,192,3,3,3,384]{6,2,5,4,3,1,0:T(8,128)(2,1)} %param.7) | copy-start | bytes 23887876
  10.3 0.7 copy-start.2
  11.7 6.8 %copy-start.1 = (bf16[1,2,192,3,3,3,384]{6,2,5,4,3,1,0:T(8,128)(2,1)S(1)}, bf16[1,2,192,3,3,3,384]{6,2,5,4,3,1,0:T(8,128)(2,1)}, u32[]{:S(2)}) copy-start(bf16[1,2,192,3,3,3,384]{6,2,5,4,3,1,0:T(8,128)(2,1)} %param.7) | copy-start | bytes 23887876
  15.4 0.9 %copy-start.4 = (bf16[1,2,2,1,192,128]{5,4,3,2,1,0:T(8,128)(2,1)S(1)}, bf16[1,2,2,1,192,128]{5,4,3,2,1,0:T(8,128)(2,1)}, u32[]{:S(2)}) copy-start(bf16[1,2,2,1,192,128]{5,4,3,2,1,0:T(8,128)(2,1)} %param.6) | copy-start | bytes 589828
  15.4 1.0 %copy-start.5 = (bf16[4,1,192,128]{3,2,1,0:T(8,128)(2,1)S(1)}, bf16[4,1,192,128]{3,2,1,0:T(8,128)(2,1)}, u32[]{:S(2)}) copy-start(bf16[4,1,192,128]{3,2,1,0:T(8,128)(2,1)} %param.5) | copy-start | bytes 589828
  15.6 2.9 %collective-permute-start.4 = (bf16[18,192,128]{2,1,0:T(8,128)(2,1)S(1)}, bf16[18,192,128]{2,1,0:T(8,128)(2,1)S(1)}, u32[]{:S(2)}, u32[]{:S(2)}) collective-permute-start(bf16[18,192,128]{2,1,0:T(8,128)(2,1)S(1)} %slice_dynamic-update-slice_fusion.refs_4_.refs_8_.refs_5_), channel_id=1, source_target_pairs={{0,1},{1,0},{2,3},{3,2},{4,5},{5,4},{6,7},{7,6},{8,9},{9,8},{10,11... | collective-permute-start | bytes 2654216 | tf_op jit(solution)/shard_map/ppermute | solution.py:282
  16.5 2.1 %collective-permute-start.5 = (bf16[6,192,128]{2,1,0:T(8,128)(2,1)S(1)}, bf16[6,192,128]{2,1,0:T(8,128)(2,1)S(1)}, u32[]{:S(2)}, u32[]{:S(2)}) collective-permute-start(bf16[6,192,128]{2,1,0:T(8,128)(2,1)S(1)} %pad_maximum_fusion.3.refs_6_.refs_10_.refs_9_), channel_id=1, source_target_pairs={{0,1},{1,0},{2,3},{3,2},{4,5},{5,4},{6,7},{7,6},{8,9},{9,8},{10,11... | collective-permute-start | bytes 884744 | tf_op jit(solution)/shard_map/ppermute | solution.py:282
  16.6 9.5 %collective-permute-start.3 = (bf16[6,192,128]{2,1,0:T(8,128)(2,1)S(1)}, bf16[6,192,128]{2,1,0:T(8,128)(2,1)S(1)}, u32[]{:S(2)}, u32[]{:S(2)}) collective-permute-start(bf16[6,192,128]{2,1,0:T(8,128)(2,1)S(1)} %pad_maximum_fusion.2), channel_id=1, source_target_pairs={{0,4},{4,0},{8,12},{12,8},{16,20},{20,16},{24,28},{28,24},{1,5},{5... | collective-permute-start | bytes 884744 | tf_op jit(solution)/shard_map/ppermute | solution.py:339
  26.0 1.6 %collective-permute-start.6 = (bf16[6,192,128]{2,1,0:T(8,128)(2,1)S(1)}, bf16[6,192,128]{2,1,0:T(8,128)(2,1)S(1)}, u32[]{:S(2)}, u32[]{:S(2)}) collective-permute-start(bf16[6,192,128]{2,1,0:T(8,128)(2,1)S(1)} %collective-permute-done.3.refs_0_.refs_2_.refs_7_), channel_id=1, source_target_pairs={{0,1},{1,0},{2,3},{3,2},{4,5},{5,4},{6,7},{7,6},{8,9},{9,8},{10,11... | collective-permute-start | bytes 884744 | tf_op jit(solution)/shard_map/ppermute | solution.py:282
  26.0 5.2 %collective-permute-start.8 = (bf16[2,192,128]{2,1,0:T(8,128)(2,1)S(1)}, bf16[2,192,128]{2,1,0:T(8,128)(2,1)S(1)}, u32[]{:S(2)}, u32[]{:S(2)}) collective-permute-start(bf16[2,192,128]{2,1,0:T(8,128)(2,1)S(1)} %get-tuple-element.60), channel_id=1, source_target_pairs={{0,4},{4,0},{8,12},{12,8},{16,20},{20,16},{24,28},{28,24},{1,5},{5... | collective-permute-start | bytes 294920 | tf_op jit(solution)/shard_map/ppermute | solution.py:355
  30.2 2.7 %collective-permute-start.7 = (bf16[12,192,128]{2,1,0:T(8,128)(2,1)S(1)}, bf16[12,192,128]{2,1,0:T(8,128)(2,1)S(1)}, u32[]{:S(2)}, u32[]{:S(2)}) collective-permute-start(bf16[12,192,128]{2,1,0:T(8,128)(2,1)S(1)} %far_row.2.refs_4_), channel_id=1, source_target_pairs={{0,1},{1,0},{2,3},{3,2},{4,5},{5,4},{6,7},{7,6},{8,9},{9,8},{10,11... | collective-permute-start | bytes 1769480 | tf_op jit(solution)/shard_map/ppermute | solution.py:282
  31.3 1.6 %collective-permute-start.9 = (bf16[6,192,128]{2,1,0:T(8,128)(2,1)S(1)}, bf16[6,192,128]{2,1,0:T(8,128)(2,1)S(1)}, u32[]{:S(2)}, u32[]{:S(2)}) collective-permute-start(bf16[6,192,128]{2,1,0:T(8,128)(2,1)S(1)} %constant_dynamic-update-slice_fusion.2.refs_8_.refs_3_), channel_id=1, source_target_pairs={{0,1},{1,0},{2,3},{3,2},{4,5},{5,4},{6,7},{7,6},{8,9},{9,8},{10,11... | collective-permute-start | bytes 884744 | tf_op jit(solution)/shard_map/ppermute | solution.py:282
  36.4 7.0 %collective-permute-start.10 = (bf16[4,192,128]{2,1,0:T(8,128)(2,1)S(1)}, bf16[4,192,128]{2,1,0:T(8,128)(2,1)S(1)}, u32[]{:S(2)}, u32[]{:S(2)}) collective-permute-start(bf16[4,192,128]{2,1,0:T(8,128)(2,1)S(1)} %get-tuple-element.61.refs_8_), channel_id=1, source_target_pairs={{0,2},{2,0},{1,3},{3,1},{4,6},{6,4},{5,7},{7,5},{8,10},{10,8},{9,1... | collective-permute-start | bytes 589832 | tf_op jit(solution)/shard_map/ppermute | solution.py:373
  43.4 6.0 %collective-permute-start.13 = (bf16[4,192,128]{2,1,0:T(8,128)(2,1)S(1)}, bf16[4,192,128]{2,1,0:T(8,128)(2,1)S(1)}, u32[]{:S(2)}, u32[]{:S(2)}) collective-permute-start(bf16[4,192,128]{2,1,0:T(8,128)(2,1)S(1)} %collective-permute-done.10.refs_4_.refs_6_), channel_id=1, source_target_pairs={{0,1},{1,0},{2,3},{3,2},{4,5},{5,4},{6,7},{7,6},{8,9},{9,8},{10,11... | collective-permute-start | bytes 589832 | tf_op jit(solution)/shard_map/ppermute | solution.py:282
  43.4 10.2 %collective-permute-start.11 = (bf16[4,192,128]{2,1,0:T(8,128)(2,1)S(1)}, bf16[4,192,128]{2,1,0:T(8,128)(2,1)S(1)}, u32[]{:S(2)}, u32[]{:S(2)}) collective-permute-start(bf16[4,192,128]{2,1,0:T(8,128)(2,1)S(1)} %collective-permute-done.10.refs_4_.refs_6_), channel_id=1, source_target_pairs={{0,8},{4,12},{8,0},{12,4},{16,24},{20,28},{24,16},{28,20},{1,9},{5... | collective-permute-start | bytes 589832 | tf_op jit(solution)/shard_map/ppermute | solution.py:301
  48.0 5.6 %collective-permute-start.12 = (bf16[4,192,128]{2,1,0:T(8,128)(2,1)S(1)}, bf16[4,192,128]{2,1,0:T(8,128)(2,1)S(1)}, u32[]{:S(2)}, u32[]{:S(2)}) collective-permute-start(bf16[4,192,128]{2,1,0:T(8,128)(2,1)S(1)} %collective-permute-done.10.refs_4_.refs_6_), channel_id=1, source_target_pairs={{8,16},{12,20},{16,8},{20,12},{9,17},{13,21},{17,9},{21,13},{10,18... | collective-permute-start | bytes 589832 | tf_op jit(solution)/shard_map/ppermute | solution.py:301
  48.8 7.1 %collective-permute-start.15 = (bf16[4,192,128]{2,1,0:T(8,128)(2,1)S(1)}, bf16[4,192,128]{2,1,0:T(8,128)(2,1)S(1)}, u32[]{:S(2)}, u32[]{:S(2)}) collective-permute-start(bf16[4,192,128]{2,1,0:T(8,128)(2,1)S(1)} %collective-permute-done.10.refs_4_.refs_6_), channel_id=1, source_target_pairs={{0,4},{4,0},{8,12},{12,8},{16,20},{20,16},{24,28},{28,24},{1,5},{5... | collective-permute-start | bytes 589832 | tf_op jit(solution)/shard_map/ppermute | solution.py:301
  56.0 2.1 %collective-permute-start.16 = (bf16[12,192,128]{2,1,0:T(8,128)(2,1)S(1)}, bf16[12,192,128]{2,1,0:T(8,128)(2,1)S(1)}, u32[]{:S(2)}, u32[]{:S(2)}) collective-permute-start(bf16[12,192,128]{2,1,0:T(8,128)(2,1)S(1)} %pad_maximum_fusion.refs_0_), channel_id=1, source_target_pairs={{0,1},{1,0},{2,3},{3,2},{4,5},{5,4},{6,7},{7,6},{8,9},{9,8},{10,11... | collective-permute-start | bytes 1769480 | tf_op jit(solution)/shard_map/ppermute | solution.py:282
  56.1 7.3 %collective-permute-start.14 = (bf16[4,192,128]{2,1,0:T(8,128)(2,1)S(1)}, bf16[4,192,128]{2,1,0:T(8,128)(2,1)S(1)}, u32[]{:S(2)}, u32[]{:S(2)}) collective-permute-start(bf16[4,192,128]{2,1,0:T(8,128)(2,1)S(1)} %get-tuple-element.95), channel_id=1, source_target_pairs={{0,4},{4,0},{8,12},{12,8},{16,20},{20,16},{24,28},{28,24},{1,5},{5... | collective-permute-start | bytes 589832 | tf_op jit(solution)/shard_map/ppermute | solution.py:339
  63.4 1.4 %collective-permute-start.17 = (bf16[4,192,128]{2,1,0:T(8,128)(2,1)S(1)}, bf16[4,192,128]{2,1,0:T(8,128)(2,1)S(1)}, u32[]{:S(2)}, u32[]{:S(2)}) collective-permute-start(bf16[4,192,128]{2,1,0:T(8,128)(2,1)S(1)} %collective-permute-done.14.refs_0_), channel_id=1, source_target_pairs={{0,1},{1,0},{2,3},{3,2},{4,5},{5,4},{6,7},{7,6},{8,9},{9,8},{10,11... | collective-permute-start | bytes 589832 | tf_op jit(solution)/shard_map/ppermute | solution.py:282
  67.1 2.1 %collective-permute-start.18 = (bf16[12,192,128]{2,1,0:T(8,128)(2,1)S(1)}, bf16[12,192,128]{2,1,0:T(8,128)(2,1)S(1)}, u32[]{:S(2)}, u32[]{:S(2)}) collective-permute-start(bf16[12,192,128]{2,1,0:T(8,128)(2,1)S(1)} %far_row.3.refs_4_), channel_id=1, source_target_pairs={{0,1},{1,0},{2,3},{3,2},{4,5},{5,4},{6,7},{7,6},{8,9},{9,8},{10,11... | collective-permute-start | bytes 1769480 | tf_op jit(solution)/shard_map/ppermute | solution.py:282
  (1 other events, 0.7 us)

commit v5 on v4

--- a/solution.py
+++ b/solution.py
@@ -290,7 +290,7 @@
     return [(i, i ^ 1) for i in range(count)]
 
 
-def exchanged(x, count):
+def exchanged(x, x_later, count):
     pairs = count // 2
     even, odd = [], []
     for i in range(count):
@@ -298,7 +298,8 @@
         for k_to, group in ((k ^ 1, even), (k + 1 if k % 2 else k - 1, odd)):
             if 0 <= k_to < pairs:
                 group.append((i, 2 * k_to + i % 2))
-    return [lax.ppermute(x, "rows", pairs) for pairs in (across(count), even, odd)]
+    even, odd = [lax.ppermute(x, "rows", pairs) for pairs in (even, odd)]
+    return lax.ppermute(x_later, "rows", across(count)), even, odd
 
 
 def shards(features, caches, conv_weights, conv_bias, norm_gain):
@@ -320,12 +321,14 @@
     out = tails = cached_seconds = None
     for period in range(segments):
         base = 0 if period else TAILS
-        beside, even, odd = exchanged(source, count)
+        own = with_other("own", source)
+        source, own["own_other"] = lax.optimization_barrier((source, own["own_other"]))
+        beside, even, odd = exchanged(own["own"], own["own"] if period else source, count)
         if period == 0:
-            beside, even, odd, gains, biases = lax.optimization_barrier((beside, even, odd, gains, biases))
+            even, odd, gains, biases = lax.optimization_barrier((even, odd, gains, biases))
             common = {"place": place, "gains": gains, "biases": biases, "weight": kernels}
         else:
-            arrays = common | with_other("own", source) | {"cached_sums": cached_sums}
+            arrays = common | own | {"cached_sums": cached_sums}
             outs = {"sums": sums_shape, "kept": kept_shape}
             first = call(functools.partial(own_kernel, frames), "own_row", arrays, outs, 1)
             sums, kept = first["sums"], first["kept"]

time: 73.5 us -> 72.6 us (0.988)
  starting transfers between devices: 15 us -> 19 us
  waiting for transfers between devices: 20.4 us -> 16.5 us
    ppermute x9, waiting for transfers between devices: 8.99 us -> 6.01 us  [swapped(): return lax.ppermute(x, 'chan', [(0, 1), (1, 0)])]
    ppermute x2, starting transfers between devices: 1.03 us -> 3.11 us  [shards(): diagonal = lax.ppermute(near, 'rows', across(count))]
    ppermute x1, starting transfers between devices: 0.37 us -> 1.49 us  [shards(): seconds[2] = lax.ppermute(seconds[2], 'rows', across(count))]
    unnamed x17 -> x13, local copies, waits for them, and re-layouts: 5.5 us -> 4.77 us
where the time goes in v5:
time: 72.6 us; the launch traced here: 72.3 us
  Pallas kernels  29.7 us (41%)
  starting transfers between devices  19 us (26%)
  waiting for transfers between devices  16.5 us (23%)
  local copies, waits for them, and re-layouts  4.9 us (7%)
  other arithmetic  1.34 us (2%)
  between operations  0.83 us (1%)
    pallas_call x8, Pallas kernels, call(): pl.pallas_call(functools.partial(kernel, names), out_shape=list(outs.valu...  28.9 us
    ppermute x4, starting transfers between devices, exchanged(): even, odd = [lax.ppermute(x, 'rows', pairs) for pairs in (even, odd)]  8.52 us
    ppermute x9, waiting for transfers between devices, swapped(): return lax.ppermute(x, 'chan', [(0, 1), (1, 0)])  6.01 us
    unnamed x13, local copies, waits for them, and re-layouts  4.77 us
    ppermute x2, waiting for transfers between devices, exchanged(): return (lax.ppermute(x_later, 'rows', across(count)), even, odd)  4.3 us
    ppermute x2, starting transfers between devices, shards(): diagonal = lax.ppermute(near, 'rows', across(count))  3.11 us
    ppermute x2, starting transfers between devices, exchanged(): return (lax.ppermute(x_later, 'rows', across(count)), even, odd)  3.11 us
    ppermute x2, waiting for transfers between devices, shards(): diagonal = lax.ppermute(near, 'rows', across(count))  2.05 us
  transfers between devices with their start and end apart: 19, of which 14 were waited for; matrix products, arithmetic and copies ran while one was open for 0% of the time, Pallas kernels for 28%

profile of v5, /device:TPU:0, one launch (start us, length us, event | category | flops | bytes accessed | tf_op | source)
XLA Modules:
  0.0 72.3 jit_solution(6683165834289302201)
XLA Ops:
  1.7 3.1 %collective-permute-start = (bf16[8,192,128]{2,1,0:T(8,128)(2,1)S(1)}, bf16[8,192,128]{2,1,0:T(8,128)(2,1)S(1)}, u32[]{:S(2)}, u32[]{:S(2)}) collective-permute-start(bf16[8,192,128]{2,1,0:T(8,128)(2,1)S(1)} %pad_maximum_fusion.1), channel_id=1, source_target_pairs={{0,8},{4,12},{8,0},{12,4},{16,24},{20,28},{24,16},{28,20},{1,9},{5... | collective-permute-start | bytes 1179656 | tf_op jit(solution)/shard_map/ppermute | solution.py:301
  5.5 1.6 %collective-permute-start.3 = (bf16[8,192,128]{2,1,0:T(8,128)(2,1)S(1)}, bf16[8,192,128]{2,1,0:T(8,128)(2,1)S(1)}, u32[]{:S(2)}, u32[]{:S(2)}) collective-permute-start(bf16[8,192,128]{2,1,0:T(8,128)(2,1)S(1)} %pad_maximum_fusion.1), channel_id=1, source_target_pairs={{0,4},{4,0},{8,12},{12,8},{16,20},{20,16},{24,28},{28,24},{1,5},{5... | collective-permute-start | bytes 1179656 | tf_op jit(solution)/shard_map/ppermute | solution.py:302
  7.1 3.3 %copy-done = bf16[1,2,192,3,3,3,384]{6,2,5,4,3,1,0:T(8,128)(2,1)S(1)} copy-done((bf16[1,2,192,3,3,3,384]{6,2,5,4,3,1,0:T(8,128)(2,1)S(1)}, bf16[1,2,192,3,3,3,384]{6,2,5,4,3,1,0:T(8,128)(2,1)}, u32[]{:S(2)}) %copy-start) | copy-done | bytes 7962648
  14.0 2.1 %collective-permute-done.3 = bf16[8,192,128]{2,1,0:T(8,128)(2,1)S(1)} collective-permute-done((bf16[8,192,128]{2,1,0:T(8,128)(2,1)S(1)}, bf16[8,192,128]{2,1,0:T(8,128)(2,1)S(1)}, u32[]{:S(2)}, u32[]{:S(2)}) %collective-permute-start.3) | collective-permute-done | bytes 393248 | tf_op jit(solution)/shard_map/ppermute | solution.py:302
  17.1 1.6 %collective-permute-start.2 = (bf16[6,192,128]{2,1,0:T(8,128)(2,1)S(1)}, bf16[6,192,128]{2,1,0:T(8,128)(2,1)S(1)}, u32[]{:S(2)}, u32[]{:S(2)}) collective-permute-start(bf16[6,192,128]{2,1,0:T(8,128)(2,1)S(1)} %pad_maximum_fusion.2), channel_id=1, source_target_pairs={{0,4},{4,0},{8,12},{12,8},{16,20},{20,16},{24,28},{28,24},{1,5},{5... | collective-permute-start | bytes 884744 | tf_op jit(solution)/shard_map/ppermute | solution.py:342
  19.3 6.4 %near_rows.1 = (f32[12,192,128]{2,1,0:T(8,128)S(1)}, bf16[2,192,128]{2,1,0:T(8,128)(2,1)S(1)}) custom-call(s32[4]{0:T(128)S(1)} %pad_add_fusion.place_ref.refs_0_.refs_4_.refs_2_, f32[2,384,128]{2,1,0:T(8,128)S(1)} %get-tuple-element.63.refs_1_.refs_5_.refs_3_, f32[2,192,128]{2,1,0:T(8,128)S(1)} %get-tuple-element.62.refs_2_.refs_6_.refs_0_.refs_4_, ...), custom_call_target="tpu_custom_call" | custom-call | tf_op jit(solution)/shard_map/near_rows/pallas_call | solution.py:269
  26.1 1.5 %collective-permute-start.8 = (bf16[2,192,128]{2,1,0:T(8,128)(2,1)S(1)}, bf16[2,192,128]{2,1,0:T(8,128)(2,1)S(1)}, u32[]{:S(2)}, u32[]{:S(2)}) collective-permute-start(bf16[2,192,128]{2,1,0:T(8,128)(2,1)S(1)} %get-tuple-element.60), channel_id=1, source_target_pairs={{0,4},{4,0},{8,12},{12,8},{16,20},{20,16},{24,28},{28,24},{1,5},{5... | collective-permute-start | bytes 294920 | tf_op jit(solution)/shard_map/ppermute | solution.py:358
  27.7 2.6 %far_row.2.refs_4_ = bf16[12,192,128]{2,1,0:T(8,128)(2,1)S(1)} custom-call(bf16[6,192,128]{2,1,0:T(8,128)(2,1)S(1)} %collective-permute-done.2.refs_0_.refs_2_.refs_7_, bf16[6,192,128]{2,1,0:T(8,128)(2,1)S(1)} %collective-permute-done.6.refs_1_.refs_3_.refs_8_, bf16[6,192,128]{2,1,0:T(8,128)(2,1)S(1)} %collective-permute-done.2.refs_0_.refs_2_.refs_7_, ...), custom_call_target="tpu_custom_call" | custom-call | tf_op jit(solution)/shard_map/far_row/pallas_call | solution.py:269
  31.4 1.6 %collective-permute-done.9.refs_9_.refs_4_ = bf16[6,192,128]{2,1,0:T(8,128)(2,1)S(1)} collective-permute-done((bf16[6,192,128]{2,1,0:T(8,128)(2,1)S(1)}, bf16[6,192,128]{2,1,0:T(8,128)(2,1)S(1)}, u32[]{:S(2)}, u32[]{:S(2)}) %collective-permute-start.9) | collective-permute-done | bytes 294944 | tf_op jit(solution)/shard_map/ppermute | solution.py:282
  33.0 3.5 %second.2 = (bf16[4,192,128]{2,1,0:T(8,128)(2,1)S(1)}, bf16[4,192,128]{2,1,0:T(8,128)(2,1)S(1)}) custom-call(s32[4]{0:T(128)S(1)} %pad_add_fusion.place_ref.refs_0_.refs_4_.refs_2_, f32[2,384,128]{2,1,0:T(8,128)S(1)} %get-tuple-element.63.refs_1_.refs_5_.refs_3_, f32[2,192,128]{2,1,0:T(8,128)S(1)} %get-tuple-element.62.refs_2_.refs_6_.refs_0_.refs_4_, ...), custom_call_target="tpu_custom_call" | custom-call | tf_op jit(solution)/shard_map/second/pallas_call | solution.py:269
  36.4 1.6 %collective-permute-start.10 = (bf16[4,192,128]{2,1,0:T(8,128)(2,1)S(1)}, bf16[4,192,128]{2,1,0:T(8,128)(2,1)S(1)}, u32[]{:S(2)}, u32[]{:S(2)}) collective-permute-start(bf16[4,192,128]{2,1,0:T(8,128)(2,1)S(1)} %get-tuple-element.61.refs_8_), channel_id=1, source_target_pairs={{0,2},{2,0},{1,3},{3,1},{4,6},{6,4},{5,7},{7,5},{8,10},{10,8},{9,1... | collective-permute-start | bytes 589832 | tf_op jit(solution)/shard_map/ppermute | solution.py:376
  38.0 3.8 %cached_rows.1 = (f32[6,192,128]{2,1,0:T(8,128)S(1)}, f32[2,192,128]{2,1,0:T(8,128)S(1)}) custom-call(f32[2,192,128]{2,1,0:T(8,128)S(1)} %get-tuple-element.62.refs_2_.refs_6_.refs_0_.refs_4_, f32[2,384,128]{2,1,0:T(8,128)S(1)} %get-tuple-element.63.refs_1_.refs_5_.refs_3_, s32[4]{0:T(128)S(1)} %pad_add_fusion.place_ref.refs_0_.refs_4_.refs_2_, ...), custom_call_target="tpu_custom_call" | custom-call | tf_op jit(solution)/shard_map/cached_rows/pallas_call | solution.py:269
  41.8 1.6 %collective-permute-done.10.refs_4_.refs_6_ = bf16[4,192,128]{2,1,0:T(8,128)(2,1)S(1)} collective-permute-done((bf16[4,192,128]{2,1,0:T(8,128)(2,1)S(1)}, bf16[4,192,128]{2,1,0:T(8,128)(2,1)S(1)}, u32[]{:S(2)}, u32[]{:S(2)}) %collective-permute-start.10) | collective-permute-done | bytes 196640 | tf_op jit(solution)/shard_map/ppermute | solution.py:376
  43.4 4.1 %collective-permute-start.11 = (bf16[4,192,128]{2,1,0:T(8,128)(2,1)S(1)}, bf16[4,192,128]{2,1,0:T(8,128)(2,1)S(1)}, u32[]{:S(2)}, u32[]{:S(2)}) collective-permute-start(bf16[4,192,128]{2,1,0:T(8,128)(2,1)S(1)} %collective-permute-done.10.refs_4_.refs_6_), channel_id=1, source_target_pairs={{0,8},{4,12},{8,0},{12,4},{16,24},{20,28},{24,16},{28,20},{1,9},{5... | collective-permute-start | bytes 589832 | tf_op jit(solution)/shard_map/ppermute | solution.py:301
  48.2 1.6 %collective-permute-start.15 = (bf16[4,192,128]{2,1,0:T(8,128)(2,1)S(1)}, bf16[4,192,128]{2,1,0:T(8,128)(2,1)S(1)}, u32[]{:S(2)}, u32[]{:S(2)}) collective-permute-start(bf16[4,192,128]{2,1,0:T(8,128)(2,1)S(1)} %collective-permute-done.10.refs_4_.refs_6_), channel_id=1, source_target_pairs={{0,4},{4,0},{8,12},{12,8},{16,20},{20,16},{24,28},{28,24},{1,5},{5... | collective-permute-start | bytes 589832 | tf_op jit(solution)/shard_map/ppermute | solution.py:302
  49.8 3.0 %own_row.1 = (f32[12,192,128]{2,1,0:T(8,128)S(1)}, bf16[2,192,128]{2,1,0:T(8,128)(2,1)S(1)}) custom-call(s32[4]{0:T(128)S(1)} %pad_add_fusion.place_ref.refs_0_.refs_4_.refs_2_, f32[2,384,128]{2,1,0:T(8,128)S(1)} %get-tuple-element.63.refs_1_.refs_5_.refs_3_, f32[2,192,128]{2,1,0:T(8,128)S(1)} %get-tuple-element.62.refs_2_.refs_6_.refs_0_.refs_4_, ...), custom_call_target="tpu_custom_call" | custom-call | tf_op jit(solution)/shard_map/own_row/pallas_call | solution.py:269
  53.1 2.2 %collective-permute-done.15 = bf16[4,192,128]{2,1,0:T(8,128)(2,1)S(1)} collective-permute-done((bf16[4,192,128]{2,1,0:T(8,128)(2,1)S(1)}, bf16[4,192,128]{2,1,0:T(8,128)(2,1)S(1)}, u32[]{:S(2)}, u32[]{:S(2)}) %collective-permute-start.15) | collective-permute-done | bytes 196640 | tf_op jit(solution)/shard_map/ppermute | solution.py:302
  55.5 1.6 %collective-permute-start.14 = (bf16[4,192,128]{2,1,0:T(8,128)(2,1)S(1)}, bf16[4,192,128]{2,1,0:T(8,128)(2,1)S(1)}, u32[]{:S(2)}, u32[]{:S(2)}) collective-permute-start(bf16[4,192,128]{2,1,0:T(8,128)(2,1)S(1)} %get-tuple-element.97), channel_id=1, source_target_pairs={{0,4},{4,0},{8,12},{12,8},{16,20},{20,16},{24,28},{28,24},{1,5},{5... | collective-permute-start | bytes 589832 | tf_op jit(solution)/shard_map/ppermute | solution.py:342
  57.4 3.7 %beside_rows.1.refs_6_ = f32[12,192,128]{2,1,0:T(8,128)S(1)} custom-call(bf16[12,192,128]{2,1,0:T(8,128)(2,1)S(1)} %pad_maximum_fusion.refs_0_, bf16[12,192,128]{2,1,0:T(8,128)(2,1)S(1)} %collective-permute-done.16.refs_1_, s32[4]{0:T(128)S(1)} %pad_add_fusion.place_ref.refs_0_.refs_4_.refs_2_, f32[2,384,128]{2,1,0:T(8,128)S(1)} %get-tuple-element.63.refs_1_.refs_5_.refs_3_, ...), custom_call_target="tpu_custom_call" | custom-call | tf_op jit(solution)/shard_map/beside_rows/pallas_call | solution.py:269
  61.2 1.6 %collective-permute-done.14.refs_0_ = bf16[4,192,128]{2,1,0:T(8,128)(2,1)S(1)} collective-permute-done((bf16[4,192,128]{2,1,0:T(8,128)(2,1)S(1)}, bf16[4,192,128]{2,1,0:T(8,128)(2,1)S(1)}, u32[]{:S(2)}, u32[]{:S(2)}) %collective-permute-start.14) | collective-permute-done | bytes 196640 | tf_op jit(solution)/shard_map/ppermute | solution.py:342
  62.8 1.4 %collective-permute-done.17.refs_1_ = bf16[4,192,128]{2,1,0:T(8,128)(2,1)S(1)} collective-permute-done((bf16[4,192,128]{2,1,0:T(8,128)(2,1)S(1)}, bf16[4,192,128]{2,1,0:T(8,128)(2,1)S(1)}, u32[]{:S(2)}, u32[]{:S(2)}) %collective-permute-start.17) | collective-permute-done | bytes 196640 | tf_op jit(solution)/shard_map/ppermute | solution.py:282
  64.2 2.3 %far_row.3.refs_4_ = bf16[12,192,128]{2,1,0:T(8,128)(2,1)S(1)} custom-call(bf16[4,192,128]{2,1,0:T(8,128)(2,1)S(1)} %collective-permute-done.14.refs_0_, bf16[4,192,128]{2,1,0:T(8,128)(2,1)S(1)} %collective-permute-done.17.refs_1_, s32[4]{0:T(128)S(1)} %pad_add_fusion.place_ref.refs_0_.refs_4_.refs_2_, ...), custom_call_target="tpu_custom_call" | custom-call | tf_op jit(solution)/shard_map/far_row/pallas_call | solution.py:269
  66.7 1.9 %collective-permute-done.18.refs_5_ = bf16[12,192,128]{2,1,0:T(8,128)(2,1)S(1)} collective-permute-done((bf16[12,192,128]{2,1,0:T(8,128)(2,1)S(1)}, bf16[12,192,128]{2,1,0:T(8,128)(2,1)S(1)}, u32[]{:S(2)}, u32[]{:S(2)}) %collective-permute-start.18) | collective-permute-done | bytes 589856 | tf_op jit(solution)/shard_map/ppermute | solution.py:282
  68.6 3.8 %second.3 = (bf16[4,192,128]{2,1,0:T(8,128)(2,1)}, bf16[4,192,128]{2,1,0:T(8,128)(2,1)}) custom-call(s32[4]{0:T(128)S(1)} %pad_add_fusion.place_ref.refs_0_.refs_4_.refs_2_, f32[2,384,128]{2,1,0:T(8,128)S(1)} %get-tuple-element.63.refs_1_.refs_5_.refs_3_, f32[2,192,128]{2,1,0:T(8,128)S(1)} %get-tuple-element.62.refs_2_.refs_6_.refs_0_.refs_4_, ...), custom_call_target="tpu_custom_call" | custom-call | tf_op jit(solution)/shard_map/second/pallas_call | solution.py:269
  (49 shorter events, 10.4 us)
Async XLA Ops:
  1.7 12.2 %collective-permute-start = (bf16[8,192,128]{2,1,0:T(8,128)(2,1)S(1)}, bf16[8,192,128]{2,1,0:T(8,128)(2,1)S(1)}, u32[]{:S(2)}, u32[]{:S(2)}) collective-permute-start(bf16[8,192,128]{2,1,0:T(8,128)(2,1)S(1)} %pad_maximum_fusion.1), channel_id=1, source_target_pairs={{0,8},{4,12},{8,0},{12,4},{16,24},{20,28},{24,16},{28,20},{1,9},{5... | collective-permute-start | bytes 1179656 | tf_op jit(solution)/shard_map/ppermute | solution.py:301
  4.8 9.1 %collective-permute-start.1 = (bf16[8,192,128]{2,1,0:T(8,128)(2,1)S(1)}, bf16[8,192,128]{2,1,0:T(8,128)(2,1)S(1)}, u32[]{:S(2)}, u32[]{:S(2)}) collective-permute-start(bf16[8,192,128]{2,1,0:T(8,128)(2,1)S(1)} %pad_maximum_fusion.1), channel_id=1, source_target_pairs={{8,16},{12,20},{16,8},{20,12},{9,17},{13,21},{17,9},{21,13},{10,18... | collective-permute-start | bytes 1179656 | tf_op jit(solution)/shard_map/ppermute | solution.py:301
  5.5 10.6 %collective-permute-start.3 = (bf16[8,192,128]{2,1,0:T(8,128)(2,1)S(1)}, bf16[8,192,128]{2,1,0:T(8,128)(2,1)S(1)}, u32[]{:S(2)}, u32[]{:S(2)}) collective-permute-start(bf16[8,192,128]{2,1,0:T(8,128)(2,1)S(1)} %pad_maximum_fusion.1), channel_id=1, source_target_pairs={{0,4},{4,0},{8,12},{12,8},{16,20},{20,16},{24,28},{28,24},{1,5},{5... | collective-permute-start | bytes 1179656 | tf_op jit(solution)/shard_map/ppermute | solution.py:302
  7.1 3.3 %copy-start = (bf16[1,2,192,3,3,3,384]{6,2,5,4,3,1,0:T(8,128)(2,1)S(1)}, bf16[1,2,192,3,3,3,384]{6,2,5,4,3,1,0:T(8,128)(2,1)}, u32[]{:S(2)}) copy-start(bf16[1,2,192,3,3,3,384]{6,2,5,4,3,1,0:T(8,128)(2,1)} %param.7) | copy-start | bytes 23887876
  10.4 0.7 copy-start.2
  11.0 0.7 copy-start.3
  11.7 7.5 %copy-start.1 = (bf16[1,2,192,3,3,3,384]{6,2,5,4,3,1,0:T(8,128)(2,1)S(1)}, bf16[1,2,192,3,3,3,384]{6,2,5,4,3,1,0:T(8,128)(2,1)}, u32[]{:S(2)}) copy-start(bf16[1,2,192,3,3,3,384]{6,2,5,4,3,1,0:T(8,128)(2,1)} %param.7) | copy-start | bytes 23887876
  16.3 2.9 %collective-permute-start.4 = (bf16[18,192,128]{2,1,0:T(8,128)(2,1)S(1)}, bf16[18,192,128]{2,1,0:T(8,128)(2,1)S(1)}, u32[]{:S(2)}, u32[]{:S(2)}) collective-permute-start(bf16[18,192,128]{2,1,0:T(8,128)(2,1)S(1)} %slice_dynamic-update-slice_fusion.refs_4_.refs_8_.refs_5_), channel_id=1, source_target_pairs={{0,1},{1,0},{2,3},{3,2},{4,5},{5,4},{6,7},{7,6},{8,9},{9,8},{10,11... | collective-permute-start | bytes 2654216 | tf_op jit(solution)/shard_map/ppermute | solution.py:282
  16.5 2.8 %collective-permute-start.5 = (bf16[6,192,128]{2,1,0:T(8,128)(2,1)S(1)}, bf16[6,192,128]{2,1,0:T(8,128)(2,1)S(1)}, u32[]{:S(2)}, u32[]{:S(2)}) collective-permute-start(bf16[6,192,128]{2,1,0:T(8,128)(2,1)S(1)} %pad_maximum_fusion.3.refs_6_.refs_10_.refs_9_), channel_id=1, source_target_pairs={{0,1},{1,0},{2,3},{3,2},{4,5},{5,4},{6,7},{7,6},{8,9},{9,8},{10,11... | collective-permute-start | bytes 884744 | tf_op jit(solution)/shard_map/ppermute | solution.py:282
  17.1 9.0 %collective-permute-start.2 = (bf16[6,192,128]{2,1,0:T(8,128)(2,1)S(1)}, bf16[6,192,128]{2,1,0:T(8,128)(2,1)S(1)}, u32[]{:S(2)}, u32[]{:S(2)}) collective-permute-start(bf16[6,192,128]{2,1,0:T(8,128)(2,1)S(1)} %pad_maximum_fusion.2), channel_id=1, source_target_pairs={{0,4},{4,0},{8,12},{12,8},{16,20},{20,16},{24,28},{28,24},{1,5},{5... | collective-permute-start | bytes 884744 | tf_op jit(solution)/shard_map/ppermute | solution.py:342
  26.1 1.6 %collective-permute-start.6 = (bf16[6,192,128]{2,1,0:T(8,128)(2,1)S(1)}, bf16[6,192,128]{2,1,0:T(8,128)(2,1)S(1)}, u32[]{:S(2)}, u32[]{:S(2)}) collective-permute-start(bf16[6,192,128]{2,1,0:T(8,128)(2,1)S(1)} %collective-permute-done.2.refs_0_.refs_2_.refs_7_), channel_id=1, source_target_pairs={{0,1},{1,0},{2,3},{3,2},{4,5},{5,4},{6,7},{7,6},{8,9},{9,8},{10,11... | collective-permute-start | bytes 884744 | tf_op jit(solution)/shard_map/ppermute | solution.py:282
  26.1 5.2 %collective-permute-start.8 = (bf16[2,192,128]{2,1,0:T(8,128)(2,1)S(1)}, bf16[2,192,128]{2,1,0:T(8,128)(2,1)S(1)}, u32[]{:S(2)}, u32[]{:S(2)}) collective-permute-start(bf16[2,192,128]{2,1,0:T(8,128)(2,1)S(1)} %get-tuple-element.60), channel_id=1, source_target_pairs={{0,4},{4,0},{8,12},{12,8},{16,20},{20,16},{24,28},{28,24},{1,5},{5... | collective-permute-start | bytes 294920 | tf_op jit(solution)/shard_map/ppermute | solution.py:358
  30.2 2.7 %collective-permute-start.7 = (bf16[12,192,128]{2,1,0:T(8,128)(2,1)S(1)}, bf16[12,192,128]{2,1,0:T(8,128)(2,1)S(1)}, u32[]{:S(2)}, u32[]{:S(2)}) collective-permute-start(bf16[12,192,128]{2,1,0:T(8,128)(2,1)S(1)} %far_row.2.refs_4_), channel_id=1, source_target_pairs={{0,1},{1,0},{2,3},{3,2},{4,5},{5,4},{6,7},{7,6},{8,9},{9,8},{10,11... | collective-permute-start | bytes 1769480 | tf_op jit(solution)/shard_map/ppermute | solution.py:282
  31.3 1.6 %collective-permute-start.9 = (bf16[6,192,128]{2,1,0:T(8,128)(2,1)S(1)}, bf16[6,192,128]{2,1,0:T(8,128)(2,1)S(1)}, u32[]{:S(2)}, u32[]{:S(2)}) collective-permute-start(bf16[6,192,128]{2,1,0:T(8,128)(2,1)S(1)} %constant_dynamic-update-slice_fusion.2.refs_8_.refs_3_), channel_id=1, source_target_pairs={{0,1},{1,0},{2,3},{3,2},{4,5},{5,4},{6,7},{7,6},{8,9},{9,8},{10,11... | collective-permute-start | bytes 884744 | tf_op jit(solution)/shard_map/ppermute | solution.py:282
  36.4 7.0 %collective-permute-start.10 = (bf16[4,192,128]{2,1,0:T(8,128)(2,1)S(1)}, bf16[4,192,128]{2,1,0:T(8,128)(2,1)S(1)}, u32[]{:S(2)}, u32[]{:S(2)}) collective-permute-start(bf16[4,192,128]{2,1,0:T(8,128)(2,1)S(1)} %get-tuple-element.61.refs_8_), channel_id=1, source_target_pairs={{0,2},{2,0},{1,3},{3,1},{4,6},{6,4},{5,7},{7,5},{8,10},{10,8},{9,1... | collective-permute-start | bytes 589832 | tf_op jit(solution)/shard_map/ppermute | solution.py:376
  43.4 6.3 %collective-permute-start.13 = (bf16[4,192,128]{2,1,0:T(8,128)(2,1)S(1)}, bf16[4,192,128]{2,1,0:T(8,128)(2,1)S(1)}, u32[]{:S(2)}, u32[]{:S(2)}) collective-permute-start(bf16[4,192,128]{2,1,0:T(8,128)(2,1)S(1)} %collective-permute-done.10.refs_4_.refs_6_), channel_id=1, source_target_pairs={{0,1},{1,0},{2,3},{3,2},{4,5},{5,4},{6,7},{7,6},{8,9},{9,8},{10,11... | collective-permute-start | bytes 589832 | tf_op jit(solution)/shard_map/ppermute | solution.py:282
  43.4 9.7 %collective-permute-start.11 = (bf16[4,192,128]{2,1,0:T(8,128)(2,1)S(1)}, bf16[4,192,128]{2,1,0:T(8,128)(2,1)S(1)}, u32[]{:S(2)}, u32[]{:S(2)}) collective-permute-start(bf16[4,192,128]{2,1,0:T(8,128)(2,1)S(1)} %collective-permute-done.10.refs_4_.refs_6_), channel_id=1, source_target_pairs={{0,8},{4,12},{8,0},{12,4},{16,24},{20,28},{24,16},{28,20},{1,9},{5... | collective-permute-start | bytes 589832 | tf_op jit(solution)/shard_map/ppermute | solution.py:301
  47.5 5.6 %collective-permute-start.12 = (bf16[4,192,128]{2,1,0:T(8,128)(2,1)S(1)}, bf16[4,192,128]{2,1,0:T(8,128)(2,1)S(1)}, u32[]{:S(2)}, u32[]{:S(2)}) collective-permute-start(bf16[4,192,128]{2,1,0:T(8,128)(2,1)S(1)} %collective-permute-done.10.refs_4_.refs_6_), channel_id=1, source_target_pairs={{8,16},{12,20},{16,8},{20,12},{9,17},{13,21},{17,9},{21,13},{10,18... | collective-permute-start | bytes 589832 | tf_op jit(solution)/shard_map/ppermute | solution.py:301
  48.2 7.1 %collective-permute-start.15 = (bf16[4,192,128]{2,1,0:T(8,128)(2,1)S(1)}, bf16[4,192,128]{2,1,0:T(8,128)(2,1)S(1)}, u32[]{:S(2)}, u32[]{:S(2)}) collective-permute-start(bf16[4,192,128]{2,1,0:T(8,128)(2,1)S(1)} %collective-permute-done.10.refs_4_.refs_6_), channel_id=1, source_target_pairs={{0,4},{4,0},{8,12},{12,8},{16,20},{20,16},{24,28},{28,24},{1,5},{5... | collective-permute-start | bytes 589832 | tf_op jit(solution)/shard_map/ppermute | solution.py:302
  55.4 2.1 %collective-permute-start.16 = (bf16[12,192,128]{2,1,0:T(8,128)(2,1)S(1)}, bf16[12,192,128]{2,1,0:T(8,128)(2,1)S(1)}, u32[]{:S(2)}, u32[]{:S(2)}) collective-permute-start(bf16[12,192,128]{2,1,0:T(8,128)(2,1)S(1)} %pad_maximum_fusion.refs_0_), channel_id=1, source_target_pairs={{0,1},{1,0},{2,3},{3,2},{4,5},{5,4},{6,7},{7,6},{8,9},{9,8},{10,11... | collective-permute-start | bytes 1769480 | tf_op jit(solution)/shard_map/ppermute | solution.py:282
  55.5 7.3 %collective-permute-start.14 = (bf16[4,192,128]{2,1,0:T(8,128)(2,1)S(1)}, bf16[4,192,128]{2,1,0:T(8,128)(2,1)S(1)}, u32[]{:S(2)}, u32[]{:S(2)}) collective-permute-start(bf16[4,192,128]{2,1,0:T(8,128)(2,1)S(1)} %get-tuple-element.97), channel_id=1, source_target_pairs={{0,4},{4,0},{8,12},{12,8},{16,20},{20,16},{24,28},{28,24},{1,5},{5... | collective-permute-start | bytes 589832 | tf_op jit(solution)/shard_map/ppermute | solution.py:342
  62.8 1.4 %collective-permute-start.17 = (bf16[4,192,128]{2,1,0:T(8,128)(2,1)S(1)}, bf16[4,192,128]{2,1,0:T(8,128)(2,1)S(1)}, u32[]{:S(2)}, u32[]{:S(2)}) collective-permute-start(bf16[4,192,128]{2,1,0:T(8,128)(2,1)S(1)} %collective-permute-done.14.refs_0_), channel_id=1, source_target_pairs={{0,1},{1,0},{2,3},{3,2},{4,5},{5,4},{6,7},{7,6},{8,9},{9,8},{10,11... | collective-permute-start | bytes 589832 | tf_op jit(solution)/shard_map/ppermute | solution.py:282
  66.5 2.1 %collective-permute-start.18 = (bf16[12,192,128]{2,1,0:T(8,128)(2,1)S(1)}, bf16[12,192,128]{2,1,0:T(8,128)(2,1)S(1)}, u32[]{:S(2)}, u32[]{:S(2)}) collective-permute-start(bf16[12,192,128]{2,1,0:T(8,128)(2,1)S(1)} %far_row.3.refs_4_), channel_id=1, source_target_pairs={{0,1},{1,0},{2,3},{3,2},{4,5},{5,4},{6,7},{7,6},{8,9},{9,8},{10,11... | collective-permute-start | bytes 1769480 | tf_op jit(solution)/shard_map/ppermute | solution.py:282

commit v6 on v4

--- a/solution.py
+++ b/solution.py
@@ -14,6 +14,7 @@
 VMEM = pl.BlockSpec(memory_space=pltpu.VMEM)
 SMEM = pl.BlockSpec(memory_space=pltpu.SMEM)
 TAILS = 2
+FRAMES = 4
 
 
 def params(mib):
@@ -118,45 +119,14 @@
         return sums
 
 
-def near_kernel(frames, base, names, *refs):
-    ref = dict(zip(names, refs))
-    part = Part(0, ref)
-    half = frames // 2
-    bias = ref["biases"][0]
-    places = [("own", 0), ("beside", 0), ("beside", 1), ("beside", 2)]
-
-    def load(slot, first):
-        name, group = places[slot]
-        if first == 0:
-            part.cached(slot, "tails_" + name, group * ref["tails_own"].shape[0])
-        for f in range(first, first + half):
-            kept = part.activate(slot, f, name, group * (frames + base) + base + f)
-            if slot == 0 and f >= frames - 2:
-                ref["kept"][f - frames + 2] = kept
-
-    def store(q, slots, first):
-        for f, value in enumerate(part.product(slots, first, half), first):
-            ref["sums"][(q + 1) * frames + f] = value + bias
-
-    for first in (0, half):
-        load(0, first)
-        load(1, first)
-        store(0, [(1, 0), (0, 1)], first)
-        load(2, first)
-        store(-1, [(2, 0), (1, 1), (0, 2)], first)
-        load(3, first)
-        store(1, [(0, 0), (3, 2)], first)
-
-
 def cached_kernel(names, *refs):
     ref = dict(zip(names, refs))
     first, second = Part(0, ref), Part(1, ref)
-    tails = ref["tails_own"].shape[0]
     held = (True, False)
-    first.cached(0, "tails_own", 0)
-    for group in range(3):
-        first.cached(1 + group, "tails_beside", group * tails)
-    first.cached(4, "tails_diagonal", 0)
+    row = TAILS + FRAMES
+    places = (("own", 0), ("beside", 0), ("pairs", 0), ("pairs", row), ("diagonal", 0))
+    for slot, (name, tile) in enumerate(places):
+        first.cached(slot, name, tile)
     for q, slots in ((-1, [(2, 0), (1, 1), (0, 2)]), (0, [(1, 0), (0, 1), (4, 2)]), (1, [(0, 0), (4, 1), (3, 2)])):
         for f, value in enumerate(first.product(slots, 0, 2, held)):
             ref["cached_sums"][2 * (q + 1) + f] = value + ref["biases"][0]
@@ -166,32 +136,38 @@
         ref["cached_seconds"][f] = value + ref["biases"][1]
 
 
-def own_kernel(frames, names, *refs):
+def own_kernel(frames, base, names, *refs):
     ref = dict(zip(names, refs))
     part = Part(0, ref)
     half = frames // 2
+    if base:
+        part.cached(0, "own", 0)
     for first in (0, half):
         for f in range(first, first + half):
-            kept = part.activate(0, f, "own", f)
+            kept = part.activate(0, f, "own", base + f)
             if f >= frames - 2:
                 ref["kept"][f - frames + 2] = kept
         for q in (-1, 0, 1):
-            for f, value in enumerate(part.product([(0, 1 - q)], first, half, (False, True)), first):
-                before = ref["cached_sums"][2 * (q + 1) + f] if f < 2 else ref["biases"][0]
+            for f, value in enumerate(part.product([(0, 1 - q)], first, half, (base > 0, True)), first):
+                before = ref["biases"][0] if base or f >= 2 else ref["cached_sums"][2 * (q + 1) + f]
                 ref["sums"][(q + 1) * frames + f] = value + before
 
 
-def beside_kernel(frames, names, *refs):
+def beside_kernel(frames, base, names, *refs):
     ref = dict(zip(names, refs))
     part = Part(0, ref)
     half = frames // 2
+    places = (("beside", 0), ("pairs", 0), ("pairs", base + frames))
 
     def load(slot, first):
+        name, tile = places[slot]
+        if base and first == 0:
+            part.cached(slot, name, tile)
         for f in range(first, first + half):
-            part.activate(slot, f, "beside", slot * frames + f)
+            part.activate(slot, f, name, tile + base + f)
 
     def store(q, slots, first):
-        for f, value in enumerate(part.product(slots, first, half, (False, True)), first):
+        for f, value in enumerate(part.product(slots, first, half, (base > 0, True)), first):
             at = (q + 1) * frames + f
             ref["sums"][at] = ref["sums_before"][at] + value
 
@@ -210,7 +186,7 @@
     half = frames // 2
     out, sums = ref["out"], ref["sums"]
     if base:
-        part.cached(0, "tails_diagonal", 0)
+        part.cached(0, "diagonal", 0)
     for first in (0, half):
         for f in range(first, first + half):
             part.activate(0, f, "diagonal", base + f)
@@ -243,7 +219,7 @@
         sums = part.product([(1, 0), (0, 1), (2, 2)], first, last - first, (period == 0, True))
         for f, value in enumerate(sums, first):
             before = ref["cached_seconds"][f] if period and f < 2 else bias
-            result = (ref["source"][base + f].astype(F32) + (value + before)).astype(BF16)
+            result = (ref["own"][base + f].astype(F32) + (value + before)).astype(BF16)
             if "result" in ref:
                 ref["result"][f] = result
             ref["out"][f] = jnp.where(segment == period, result, ref["older"][f]) if period else result
@@ -263,8 +239,7 @@
 
 def call(kernel, name, arrays, outs, slots):
     depth = arrays["weight"].shape[-1]
-    frames = 4
-    scratch = {"window": pltpu.VMEM((slots, frames + 2, depth, LANES), BF16)}
+    scratch = {"window": pltpu.VMEM((slots, FRAMES + 2, depth, LANES), BF16)}
     names = [*arrays, *outs, *scratch]
     results = pl.pallas_call(
         functools.partial(kernel, names),
@@ -295,7 +270,7 @@
     even, odd = [], []
     for i in range(count):
         k = i // 2
-        for k_to, group in ((k ^ 1, even), (k + 1 if k % 2 else k - 1, odd)):
+        for k_to, group in ((k ^ 1, odd), (k + 1 if k % 2 else k - 1, even)):
             if 0 <= k_to < pairs:
                 group.append((i, 2 * k_to + i % 2))
     return [lax.ppermute(x, "rows", pairs) for pairs in (across(count), even, odd)]
@@ -316,49 +291,41 @@
     gains, biases = prepared(place, norm_gain[0], conv_bias[0], kernels, channels)
     source = jnp.concatenate([caches[0].reshape(2 * TAILS, channels, LANES), features[:, 0]], axis=0)
     sums_shape, kept_shape = tiles(3 * frames, channels, F32), tiles(2, channels)
-    near_first = kind == pair % 2
+    near_first = kind != pair % 2
     out = tails = cached_seconds = None
     for period in range(segments):
         base = 0 if period else TAILS
         beside, even, odd = exchanged(source, count)
         if period == 0:
-            beside, even, odd, gains, biases = lax.optimization_barrier((beside, even, odd, gains, biases))
+            even, odd, gains, biases = lax.optimization_barrier((even, odd, gains, biases))
             common = {"place": place, "gains": gains, "biases": biases, "weight": kernels}
-        else:
-            arrays = common | with_other("own", source) | {"cached_sums": cached_sums}
-            outs = {"sums": sums_shape, "kept": kept_shape}
-            first = call(functools.partial(own_kernel, frames), "own_row", arrays, outs, 1)
-            sums, kept = first["sums"], first["kept"]
-            even, odd, sums, kept = lax.optimization_barrier((even, odd, sums, kept))
         near, far = jnp.where(near_first, even, odd), jnp.where(near_first, odd, even)
         if period == 0:
             seconds = [x[TAILS : 2 * TAILS] for x in (source, beside, near)]
             source, beside, near, far = [
                 jnp.concatenate([x[:TAILS], x[2 * TAILS :]], axis=0) for x in (source, beside, near, far)
             ]
+        own = with_other("own", source)
         diagonal = lax.ppermute(near, "rows", across(count))
-        arrays = with_other("beside", jnp.concatenate([beside, near, far], axis=0))
+        pairs = jnp.concatenate([near, far], axis=0)
+        own["own_other"], beside, pairs = lax.optimization_barrier((own["own_other"], beside, pairs))
+        beside = with_other("beside", beside) | with_other("pairs", pairs)
+        arrays = common | own | ({"cached_sums": cached_sums} if period else {})
+        outs = {"sums": sums_shape, "kept": kept_shape}
+        first = call(functools.partial(own_kernel, frames, base), "own_row", arrays, outs, 1)
+        arrays = common | beside | {"sums_before": first["sums"]}
+        kernel = functools.partial(beside_kernel, frames, base)
+        sums = call(kernel, "beside_rows", arrays, {"sums": sums_shape}, 3)["sums"]
+        diagonal, sums = lax.optimization_barrier((diagonal, sums))
+        diagonal = with_other("diagonal", diagonal)
         if period == 0:
-            arrays |= with_other("own", source)
-            cached = {"tails_" + key: value for key, value in arrays.items()}
-            outs = {"sums": sums_shape, "kept": kept_shape}
-            first = call(functools.partial(near_kernel, frames, base), "near_rows", common | arrays | cached, outs, 4)
-            sums, kept = first["sums"], first["kept"]
-        else:
-            arrays |= common | {"sums_before": sums}
-            sums = call(functools.partial(beside_kernel, frames), "beside_rows", arrays, {"sums": sums_shape}, 3)["sums"]
-        diagonal, sums = lax.optimization_barrier((diagonal, sums))
-        arrays = with_other("diagonal", diagonal)
-        if period == 0:
-            away = {"tails_" + key: value for key, value in arrays.items()}
             seconds, sums = lax.optimization_barrier((seconds, sums))
             seconds[2] = lax.ppermute(seconds[2], "rows", across(count))
             seconds = with_other("seconds", jnp.concatenate(seconds, axis=0))
-            arrays |= away
-        arrays |= common | {"sums": sums}
+        arrays = common | diagonal | {"sums": sums}
         outs = {"out": tiles(3 * frames, channels)}
         middle = call(functools.partial(far_kernel, frames, base), "far_row", arrays, outs, 1)["out"]
-        arrays = common | with_other("middle", middle) | {"source": source, "kept": kept}
+        arrays = common | with_other("middle", middle) | {"own": own["own"], "kept": first["kept"]}
         outs = {"out": tiles(frames, channels), "tails": tiles(2 * TAILS, channels)}
         if period:
             arrays |= {"older": out, "older_tails": tails, "cached_seconds": cached_seconds}
@@ -372,7 +339,7 @@
             result = second["result"] if period else out
             source = lax.ppermute(result, "segment", [(i, (i + 1) % segments) for i in range(segments)])
             if period == 0:
-                arrays, result = lax.optimization_barrier((common | cached | away | seconds, result))
+                arrays, result = lax.optimization_barrier((common | own | beside | diagonal | seconds, result))
                 outs = {"cached_sums": tiles(6, channels, F32), "cached_seconds": tiles(2, channels, F32)}
                 sums = call(cached_kernel, "cached_rows", arrays, outs, 8)
                 cached_sums, cached_seconds = sums["cached_sums"], sums["cached_seconds"]

time: 73.5 us -> 71.9 us (0.978)
  waiting for transfers between devices: 20.4 us -> 17 us
  starting transfers between devices: 15 us -> 16.6 us
  Pallas kernels: 29.7 us -> 31.1 us
  local copies, waits for them, and re-layouts: 5.61 us -> 4.36 us
    ppermute x9 -> x11, waiting for transfers between devices: 8.99 us -> 5.65 us  [swapped(): return lax.ppermute(x, 'chan', [(0, 1), (1, 0)])]
    unnamed x17 -> x12, local copies, waits for them, and re-layouts: 5.5 us -> 3.3 us
    ppermute x6, waiting for transfers between devices: 6.23 us -> 8.03 us  [exchanged(): lax.ppermute(x, 'rows', pairs)]
    ppermute x2, waiting for transfers between devices: 2.75 us -> 1.01 us  [shards(): diagonal = lax.ppermute(near, 'rows', across(count))]
    pallas_call x8 -> x9, Pallas kernels: 28.9 us -> 30.2 us  [call(): pl.pallas_call(functools.partial(kernel, names), out_shape=list(outs.valu...]
    ppermute x9 -> x11, starting transfers between devices: 0.71 us -> 1.71 us  [swapped(): return lax.ppermute(x, 'chan', [(0, 1), (1, 0)])]
    slice x3, local copies, waits for them, and re-layouts: 0.07 us -> 0.99 us  [shards(): seconds = [x[TAILS:2 * TAILS] for x in (source, beside, near)]]
  transfers between devices with their start and end apart: 19 -> 21, of which waited for: 14 -> 10; matrix products, arithmetic and copies ran while one was open for 0% -> 2% of each run, Pallas kernels for 28% -> 30%
where the time goes in v6:
time: 71.9 us; the launch traced here: 71.4 us
  Pallas kernels  31.1 us (43%)
  waiting for transfers between devices  17 us (24%)
  starting transfers between devices  16.6 us (23%)
  local copies, waits for them, and re-layouts  4.36 us (6%)
  other arithmetic  1.47 us (2%)
  between operations  0.99 us (1%)
    pallas_call x9, Pallas kernels, call(): pl.pallas_call(functools.partial(kernel, names), out_shape=list(outs.valu...  30.2 us
    ppermute x6, starting transfers between devices, exchanged(): lax.ppermute(x, 'rows', pairs)  11.3 us
    ppermute x6, waiting for transfers between devices, exchanged(): lax.ppermute(x, 'rows', pairs)  8.03 us
    ppermute x11, waiting for transfers between devices, swapped(): return lax.ppermute(x, 'chan', [(0, 1), (1, 0)])  5.65 us
    unnamed x12, local copies, waits for them, and re-layouts  3.3 us
    ppermute x11, starting transfers between devices, swapped(): return lax.ppermute(x, 'chan', [(0, 1), (1, 0)])  1.71 us
    ppermute x1, starting transfers between devices, shards(): lax.ppermute(result, 'segment', [(i, (i + 1) % segments) for i in range(s...  1.58 us
    ppermute x1, waiting for transfers between devices, shards(): lax.ppermute(result, 'segment', [(i, (i + 1) % segments) for i in range(s...  1.44 us
  transfers between devices with their start and end apart: 21, of which 10 were waited for; matrix products, arithmetic and copies ran while one was open for 2% of the time, Pallas kernels for 30%

profile of v6, /device:TPU:0, one launch (start us, length us, event | category | flops | bytes accessed | tf_op | source)
XLA Modules:
  0.0 71.4 jit_solution(17078052303903555218)
XLA Ops:
  0.7 1.1 %pad_maximum_fusion.1 = bf16[8,192,128]{2,1,0:T(8,128)(2,1)S(1)} fusion(bf16[4,192,128]{2,1,0:T(8,128)(2,1)} %bitcast.38, bf16[4,192,128]{2,1,0:T(8,128)(2,1)} %bitcast.36), kind=kLoop, calls=%fused_computation.1 | loop fusion | flops 196608 | bytes 786432 | tf_op jit(solution)/shard_map/concatenate | solution.py:292
  1.8 3.0 %collective-permute-start.4 = (bf16[8,192,128]{2,1,0:T(8,128)(2,1)S(1)}, bf16[8,192,128]{2,1,0:T(8,128)(2,1)S(1)}, u32[]{:S(2)}, u32[]{:S(2)}) collective-permute-start(bf16[8,192,128]{2,1,0:T(8,128)(2,1)S(1)} %pad_maximum_fusion.1), channel_id=1, source_target_pairs={{0,4},{4,0},{8,12},{12,8},{16,20},{20,16},{24,28},{28,24},{1,5},{5... | collective-permute-start | bytes 1179656 | tf_op jit(solution)/shard_map/ppermute | solution.py:276
  4.8 1.6 %collective-permute-start.1 = (bf16[8,192,128]{2,1,0:T(8,128)(2,1)S(1)}, bf16[8,192,128]{2,1,0:T(8,128)(2,1)S(1)}, u32[]{:S(2)}, u32[]{:S(2)}) collective-permute-start(bf16[8,192,128]{2,1,0:T(8,128)(2,1)S(1)} %pad_maximum_fusion.1), channel_id=1, source_target_pairs={{0,8},{4,12},{8,0},{12,4},{16,24},{20,28},{24,16},{28,20},{1,9},{5... | collective-permute-start | bytes 1179656 | tf_op jit(solution)/shard_map/ppermute | solution.py:276
  7.0 1.0 %slice_bitcast_fusion = (bf16[2,192,128]{2,1,0:T(8,128)(2,1)S(1)}, bf16[2,192,128]{2,1,0:T(8,128)(2,1)S(1)}) fusion(bf16[1,2,2,1,192,128]{5,4,2,3,1,0:T(8,128)(2,1)} %bitcast.37), kind=kLoop, calls=%fused_computation.10 | loop fusion | bytes 393216 | tf_op jit(solution)/shard_map/slice | solution.py:304
  8.2 3.3 %copy-done = bf16[1,2,192,3,3,3,384]{6,2,5,4,3,1,0:T(8,128)(2,1)S(1)} copy-done((bf16[1,2,192,3,3,3,384]{6,2,5,4,3,1,0:T(8,128)(2,1)S(1)}, bf16[1,2,192,3,3,3,384]{6,2,5,4,3,1,0:T(8,128)(2,1)}, u32[]{:S(2)}) %copy-start) | copy-done | bytes 7962648
  12.3 3.0 %collective-permute-done.1 = bf16[8,192,128]{2,1,0:T(8,128)(2,1)S(1)} collective-permute-done((bf16[8,192,128]{2,1,0:T(8,128)(2,1)S(1)}, bf16[8,192,128]{2,1,0:T(8,128)(2,1)S(1)}, u32[]{:S(2)}, u32[]{:S(2)}) %collective-permute-start.1) | collective-permute-done | bytes 393248 | tf_op jit(solution)/shard_map/ppermute | solution.py:276
  16.7 3.3 %own_row.2 = (f32[12,192,128]{2,1,0:T(8,128)S(1)}, bf16[2,192,128]{2,1,0:T(8,128)(2,1)S(1)}) custom-call(s32[4]{0:T(128)S(1)} %pad_add_fusion.place_ref.refs_0_.refs_10_, f32[2,384,128]{2,1,0:T(8,128)S(1)} %get-tuple-element.72.refs_1_.refs_5_, f32[2,192,128]{2,1,0:T(8,128)S(1)} %get-tuple-element.69.refs_2_, bf16[2,9,576,384]{3,2,1,0:T(8,128)(2,1)S(1)} %bitcast.25, ...), custom_call_target="tpu_custom_call" | custom-call | tf_op jit(solution)/shard_map/own_row/pallas_call | solution.py:244
  20.1 4.3 %beside_rows.2.refs_6_ = f32[12,192,128]{2,1,0:T(8,128)S(1)} custom-call(s32[4]{0:T(128)S(1)} %pad_add_fusion.place_ref.refs_0_.refs_10_, f32[2,384,128]{2,1,0:T(8,128)S(1)} %get-tuple-element.72.refs_1_.refs_5_, f32[2,192,128]{2,1,0:T(8,128)S(1)} %get-tuple-element.69.refs_2_, bf16[2,9,576,384]{3,2,1,0:T(8,128)(2,1)S(1)} %bitcast.26, ...), custom_call_target="tpu_custom_call" | custom-call | tf_op jit(solution)/shard_map/beside_rows/pallas_call | solution.py:244
  24.3 1.0 %collective-permute-done.2.refs_4_.refs_3_ = bf16[6,192,128]{2,1,0:T(8,128)(2,1)S(1)} collective-permute-done((bf16[6,192,128]{2,1,0:T(8,128)(2,1)S(1)}, bf16[6,192,128]{2,1,0:T(8,128)(2,1)S(1)}, u32[]{:S(2)}, u32[]{:S(2)}) %collective-permute-start.2) | collective-permute-done | bytes 294944 | tf_op jit(solution)/shard_map/ppermute | solution.py:309
  26.9 2.5 %far_row.2.refs_4_ = bf16[12,192,128]{2,1,0:T(8,128)(2,1)S(1)} custom-call(s32[4]{0:T(128)S(1)} %pad_add_fusion.place_ref.refs_0_.refs_10_, f32[2,384,128]{2,1,0:T(8,128)S(1)} %get-tuple-element.72.refs_1_.refs_5_, f32[2,192,128]{2,1,0:T(8,128)S(1)} %get-tuple-element.69.refs_2_, bf16[2,9,576,384]{3,2,1,0:T(8,128)(2,1)S(1)} %bitcast.27, ...), custom_call_target="tpu_custom_call" | custom-call | tf_op jit(solution)/shard_map/far_row/pallas_call | solution.py:244
  30.7 1.6 %collective-permute-done.10.refs_9_.refs_12_ = bf16[6,192,128]{2,1,0:T(8,128)(2,1)S(1)} collective-permute-done((bf16[6,192,128]{2,1,0:T(8,128)(2,1)S(1)}, bf16[6,192,128]{2,1,0:T(8,128)(2,1)S(1)}, u32[]{:S(2)}, u32[]{:S(2)}) %collective-permute-start.10) | collective-permute-done | bytes 294944 | tf_op jit(solution)/shard_map/ppermute | solution.py:257
  32.2 3.4 %second.2 = (bf16[4,192,128]{2,1,0:T(8,128)(2,1)S(1)}, bf16[4,192,128]{2,1,0:T(8,128)(2,1)S(1)}) custom-call(s32[4]{0:T(128)S(1)} %pad_add_fusion.place_ref.refs_0_.refs_10_, f32[2,384,128]{2,1,0:T(8,128)S(1)} %get-tuple-element.72.refs_1_.refs_5_, f32[2,192,128]{2,1,0:T(8,128)S(1)} %get-tuple-element.69.refs_2_, bf16[2,9,576,384]{3,2,1,0:T(8,128)(2,1)S(1)} %bitcast.28, ...), custom_call_target="tpu_custom_call" | custom-call | tf_op jit(solution)/shard_map/second/pallas_call | solution.py:244
  35.7 1.6 %collective-permute-start.11 = (bf16[4,192,128]{2,1,0:T(8,128)(2,1)S(1)}, bf16[4,192,128]{2,1,0:T(8,128)(2,1)S(1)}, u32[]{:S(2)}, u32[]{:S(2)}) collective-permute-start(bf16[4,192,128]{2,1,0:T(8,128)(2,1)S(1)} %get-tuple-element.66.refs_8_), channel_id=1, source_target_pairs={{0,2},{2,0},{1,3},{3,1},{4,6},{6,4},{5,7},{7,5},{8,10},{10,8},{9,1... | collective-permute-start | bytes 589832 | tf_op jit(solution)/shard_map/ppermute | solution.py:340
  37.3 4.0 %cached_rows.1 = (f32[6,192,128]{2,1,0:T(8,128)S(1)}, f32[2,192,128]{2,1,0:T(8,128)S(1)}) custom-call(bf16[6,192,128]{2,1,0:T(8,128)(2,1)S(1)} %pad_maximum_fusion.5.refs_4_.refs_0_, bf16[6,192,128]{2,1,0:T(8,128)(2,1)S(1)} %collective-permute-done.5.refs_5_.refs_1_, f32[2,192,128]{2,1,0:T(8,128)S(1)} %get-tuple-element.69.refs_2_, ...), custom_call_target="tpu_custom_call" | custom-call | tf_op jit(solution)/shard_map/cached_rows/pallas_call | solution.py:244
  41.2 1.4 %collective-permute-done.11.refs_4_.refs_6_ = bf16[4,192,128]{2,1,0:T(8,128)(2,1)S(1)} collective-permute-done((bf16[4,192,128]{2,1,0:T(8,128)(2,1)S(1)}, bf16[4,192,128]{2,1,0:T(8,128)(2,1)S(1)}, u32[]{:S(2)}, u32[]{:S(2)}) %collective-permute-start.11) | collective-permute-done | bytes 196640 | tf_op jit(solution)/shard_map/ppermute | solution.py:340
  42.7 4.6 %collective-permute-start.13 = (bf16[4,192,128]{2,1,0:T(8,128)(2,1)S(1)}, bf16[4,192,128]{2,1,0:T(8,128)(2,1)S(1)}, u32[]{:S(2)}, u32[]{:S(2)}) collective-permute-start(bf16[4,192,128]{2,1,0:T(8,128)(2,1)S(1)} %collective-permute-done.11.refs_4_.refs_6_), channel_id=1, source_target_pairs={{0,8},{4,12},{8,0},{12,4},{16,24},{20,28},{24,16},{28,20},{1,9},{5... | collective-permute-start | bytes 589832 | tf_op jit(solution)/shard_map/ppermute | solution.py:276
  48.8 2.9 %collective-permute-done.13 = bf16[4,192,128]{2,1,0:T(8,128)(2,1)S(1)} collective-permute-done((bf16[4,192,128]{2,1,0:T(8,128)(2,1)S(1)}, bf16[4,192,128]{2,1,0:T(8,128)(2,1)S(1)}, u32[]{:S(2)}, u32[]{:S(2)}) %collective-permute-start.13) | collective-permute-done | bytes 196640 | tf_op jit(solution)/shard_map/ppermute | solution.py:276
  51.7 2.1 %collective-permute-done.16.refs_4_ = bf16[4,192,128]{2,1,0:T(8,128)(2,1)S(1)} collective-permute-done((bf16[4,192,128]{2,1,0:T(8,128)(2,1)S(1)}, bf16[4,192,128]{2,1,0:T(8,128)(2,1)S(1)}, u32[]{:S(2)}, u32[]{:S(2)}) %collective-permute-start.16) | collective-permute-done | bytes 196640 | tf_op jit(solution)/shard_map/ppermute | solution.py:276
  55.1 3.0 %own_row.3 = (f32[12,192,128]{2,1,0:T(8,128)S(1)}, bf16[2,192,128]{2,1,0:T(8,128)(2,1)S(1)}) custom-call(s32[4]{0:T(128)S(1)} %pad_add_fusion.place_ref.refs_0_.refs_10_, f32[2,384,128]{2,1,0:T(8,128)S(1)} %get-tuple-element.72.refs_1_.refs_5_, f32[2,192,128]{2,1,0:T(8,128)S(1)} %get-tuple-element.69.refs_2_, bf16[2,9,576,384]{3,2,1,0:T(8,128)(2,1)S(1)} %bitcast.30, ...), custom_call_target="tpu_custom_call" | custom-call | tf_op jit(solution)/shard_map/own_row/pallas_call | solution.py:244
  58.1 3.7 %beside_rows.3.refs_6_ = f32[12,192,128]{2,1,0:T(8,128)S(1)} custom-call(s32[4]{0:T(128)S(1)} %pad_add_fusion.place_ref.refs_0_.refs_10_, f32[2,384,128]{2,1,0:T(8,128)S(1)} %get-tuple-element.72.refs_1_.refs_5_, f32[2,192,128]{2,1,0:T(8,128)S(1)} %get-tuple-element.69.refs_2_, bf16[2,9,576,384]{3,2,1,0:T(8,128)(2,1)S(1)} %bitcast.31, ...), custom_call_target="tpu_custom_call" | custom-call | tf_op jit(solution)/shard_map/beside_rows/pallas_call | solution.py:244
  61.9 1.4 %collective-permute-done.19.refs_5_ = bf16[4,192,128]{2,1,0:T(8,128)(2,1)S(1)} collective-permute-done((bf16[4,192,128]{2,1,0:T(8,128)(2,1)S(1)}, bf16[4,192,128]{2,1,0:T(8,128)(2,1)S(1)}, u32[]{:S(2)}, u32[]{:S(2)}) %collective-permute-start.19) | collective-permute-done | bytes 196640 | tf_op jit(solution)/shard_map/ppermute | solution.py:257
  63.3 2.3 %far_row.3.refs_4_ = bf16[12,192,128]{2,1,0:T(8,128)(2,1)S(1)} custom-call(s32[4]{0:T(128)S(1)} %pad_add_fusion.place_ref.refs_0_.refs_10_, f32[2,384,128]{2,1,0:T(8,128)S(1)} %get-tuple-element.72.refs_1_.refs_5_, f32[2,192,128]{2,1,0:T(8,128)S(1)} %get-tuple-element.69.refs_2_, bf16[2,9,576,384]{3,2,1,0:T(8,128)(2,1)S(1)} %bitcast.32, ...), custom_call_target="tpu_custom_call" | custom-call | tf_op jit(solution)/shard_map/far_row/pallas_call | solution.py:244
  65.8 1.9 %collective-permute-done.20.refs_5_ = bf16[12,192,128]{2,1,0:T(8,128)(2,1)S(1)} collective-permute-done((bf16[12,192,128]{2,1,0:T(8,128)(2,1)S(1)}, bf16[12,192,128]{2,1,0:T(8,128)(2,1)S(1)}, u32[]{:S(2)}, u32[]{:S(2)}) %collective-permute-start.20) | collective-permute-done | bytes 589856 | tf_op jit(solution)/shard_map/ppermute | solution.py:257
  67.7 3.8 %second.3 = (bf16[4,192,128]{2,1,0:T(8,128)(2,1)}, bf16[4,192,128]{2,1,0:T(8,128)(2,1)}) custom-call(s32[4]{0:T(128)S(1)} %pad_add_fusion.place_ref.refs_0_.refs_10_, f32[2,384,128]{2,1,0:T(8,128)S(1)} %get-tuple-element.72.refs_1_.refs_5_, f32[2,192,128]{2,1,0:T(8,128)S(1)} %get-tuple-element.69.refs_2_, bf16[2,9,576,384]{3,2,1,0:T(8,128)(2,1)S(1)} %bitcast.33, ...), custom_call_target="tpu_custom_call" | custom-call | tf_op jit(solution)/shard_map/second/pallas_call | solution.py:244
  (57 shorter events, 8.8 us)
Async XLA Ops:
  0.6 7.4 %copy-start.4 = (bf16[4,1,192,128]{3,2,1,0:T(8,128)(2,1)S(1)}, bf16[4,1,192,128]{3,2,1,0:T(8,128)(2,1)}, u32[]{:S(2)}) copy-start(bf16[4,1,192,128]{3,2,1,0:T(8,128)(2,1)} %param.5) | copy-start | bytes 589828
  0.6 7.6 %copy-start.2 = (f32[1,2,384]{2,1,0:T(2,128)S(1)}, f32[1,2,384]{2,1,0:T(2,128)}, u32[]{:S(2)}) copy-start(f32[1,2,384]{2,1,0:T(2,128)} %param.9) | copy-start | bytes 9220
  0.6 7.6 %copy-start.3 = (f32[1,2,384]{2,1,0:T(2,128)S(1)}, f32[1,2,384]{2,1,0:T(2,128)}, u32[]{:S(2)}) copy-start(f32[1,2,384]{2,1,0:T(2,128)} %param.8) | copy-start | bytes 9220
  1.8 13.7 %collective-permute-start.4 = (bf16[8,192,128]{2,1,0:T(8,128)(2,1)S(1)}, bf16[8,192,128]{2,1,0:T(8,128)(2,1)S(1)}, u32[]{:S(2)}, u32[]{:S(2)}) collective-permute-start(bf16[8,192,128]{2,1,0:T(8,128)(2,1)S(1)} %pad_maximum_fusion.1), channel_id=1, source_target_pairs={{0,4},{4,0},{8,12},{12,8},{16,20},{20,16},{24,28},{28,24},{1,5},{5... | collective-permute-start | bytes 1179656 | tf_op jit(solution)/shard_map/ppermute | solution.py:276
  4.8 10.6 %collective-permute-start.1 = (bf16[8,192,128]{2,1,0:T(8,128)(2,1)S(1)}, bf16[8,192,128]{2,1,0:T(8,128)(2,1)S(1)}, u32[]{:S(2)}, u32[]{:S(2)}) collective-permute-start(bf16[8,192,128]{2,1,0:T(8,128)(2,1)S(1)} %pad_maximum_fusion.1), channel_id=1, source_target_pairs={{0,8},{4,12},{8,0},{12,4},{16,24},{20,28},{24,16},{28,20},{1,9},{5... | collective-permute-start | bytes 1179656 | tf_op jit(solution)/shard_map/ppermute | solution.py:276
  6.3 9.0 %collective-permute-start = (bf16[8,192,128]{2,1,0:T(8,128)(2,1)S(1)}, bf16[8,192,128]{2,1,0:T(8,128)(2,1)S(1)}, u32[]{:S(2)}, u32[]{:S(2)}) collective-permute-start(bf16[8,192,128]{2,1,0:T(8,128)(2,1)S(1)} %pad_maximum_fusion.1), channel_id=1, source_target_pairs={{8,16},{12,20},{16,8},{20,12},{9,17},{13,21},{17,9},{21,13},{10,18... | collective-permute-start | bytes 1179656 | tf_op jit(solution)/shard_map/ppermute | solution.py:276
  8.0 7.6 %collective-permute-start.3 = (bf16[6,192,128]{2,1,0:T(8,128)(2,1)S(1)}, bf16[6,192,128]{2,1,0:T(8,128)(2,1)S(1)}, u32[]{:S(2)}, u32[]{:S(2)}) collective-permute-start(bf16[6,192,128]{2,1,0:T(8,128)(2,1)S(1)} %pad_maximum_fusion.4.refs_4_.refs_6_), channel_id=1, source_target_pairs={{0,1},{1,0},{2,3},{3,2},{4,5},{5,4},{6,7},{7,6},{8,9},{9,8},{10,11... | collective-permute-start | bytes 884744 | tf_op jit(solution)/shard_map/ppermute | solution.py:257
  15.7 4.4 %collective-permute-start.6 = (bf16[12,192,128]{2,1,0:T(8,128)(2,1)S(1)}, bf16[12,192,128]{2,1,0:T(8,128)(2,1)S(1)}, u32[]{:S(2)}, u32[]{:S(2)}) collective-permute-start(bf16[12,192,128]{2,1,0:T(8,128)(2,1)S(1)} %pad_maximum_fusion.refs_6_.refs_8_), channel_id=1, source_target_pairs={{0,1},{1,0},{2,3},{3,2},{4,5},{5,4},{6,7},{7,6},{8,9},{9,8},{10,11... | collective-permute-start | bytes 1769480 | tf_op jit(solution)/shard_map/ppermute | solution.py:257
  15.8 4.3 %collective-permute-start.5 = (bf16[6,192,128]{2,1,0:T(8,128)(2,1)S(1)}, bf16[6,192,128]{2,1,0:T(8,128)(2,1)S(1)}, u32[]{:S(2)}, u32[]{:S(2)}) collective-permute-start(bf16[6,192,128]{2,1,0:T(8,128)(2,1)S(1)} %pad_maximum_fusion.5.refs_4_.refs_0_), channel_id=1, source_target_pairs={{0,1},{1,0},{2,3},{3,2},{4,5},{5,4},{6,7},{7,6},{8,9},{9,8},{10,11... | collective-permute-start | bytes 884744 | tf_op jit(solution)/shard_map/ppermute | solution.py:257
  16.3 9.1 %collective-permute-start.2 = (bf16[6,192,128]{2,1,0:T(8,128)(2,1)S(1)}, bf16[6,192,128]{2,1,0:T(8,128)(2,1)S(1)}, u32[]{:S(2)}, u32[]{:S(2)}) collective-permute-start(bf16[6,192,128]{2,1,0:T(8,128)(2,1)S(1)} %pad_maximum_fusion.3), channel_id=1, source_target_pairs={{0,4},{4,0},{8,12},{12,8},{16,20},{20,16},{24,28},{28,24},{1,5},{5... | collective-permute-start | bytes 884744 | tf_op jit(solution)/shard_map/ppermute | solution.py:309
  25.3 1.6 %collective-permute-start.7 = (bf16[6,192,128]{2,1,0:T(8,128)(2,1)S(1)}, bf16[6,192,128]{2,1,0:T(8,128)(2,1)S(1)}, u32[]{:S(2)}, u32[]{:S(2)}) collective-permute-start(bf16[6,192,128]{2,1,0:T(8,128)(2,1)S(1)} %collective-permute-done.2.refs_4_.refs_3_), channel_id=1, source_target_pairs={{0,1},{1,0},{2,3},{3,2},{4,5},{5,4},{6,7},{7,6},{8,9},{9,8},{10,11... | collective-permute-start | bytes 884744 | tf_op jit(solution)/shard_map/ppermute | solution.py:257
  25.3 5.2 %collective-permute-start.9 = (bf16[2,192,128]{2,1,0:T(8,128)(2,1)S(1)}, bf16[2,192,128]{2,1,0:T(8,128)(2,1)S(1)}, u32[]{:S(2)}, u32[]{:S(2)}) collective-permute-start(bf16[2,192,128]{2,1,0:T(8,128)(2,1)S(1)} %get-tuple-element.65), channel_id=1, source_target_pairs={{0,4},{4,0},{8,12},{12,8},{16,20},{20,16},{24,28},{28,24},{1,5},{5... | collective-permute-start | bytes 294920 | tf_op jit(solution)/shard_map/ppermute | solution.py:323
  29.5 2.7 %collective-permute-start.8 = (bf16[12,192,128]{2,1,0:T(8,128)(2,1)S(1)}, bf16[12,192,128]{2,1,0:T(8,128)(2,1)S(1)}, u32[]{:S(2)}, u32[]{:S(2)}) collective-permute-start(bf16[12,192,128]{2,1,0:T(8,128)(2,1)S(1)} %far_row.2.refs_4_), channel_id=1, source_target_pairs={{0,1},{1,0},{2,3},{3,2},{4,5},{5,4},{6,7},{7,6},{8,9},{9,8},{10,11... | collective-permute-start | bytes 1769480 | tf_op jit(solution)/shard_map/ppermute | solution.py:257
  30.6 1.6 %collective-permute-start.10 = (bf16[6,192,128]{2,1,0:T(8,128)(2,1)S(1)}, bf16[6,192,128]{2,1,0:T(8,128)(2,1)S(1)}, u32[]{:S(2)}, u32[]{:S(2)}) collective-permute-start(bf16[6,192,128]{2,1,0:T(8,128)(2,1)S(1)} %constant_dynamic-update-slice_fusion.refs_8_.refs_11_), channel_id=1, source_target_pairs={{0,1},{1,0},{2,3},{3,2},{4,5},{5,4},{6,7},{7,6},{8,9},{9,8},{10,11... | collective-permute-start | bytes 884744 | tf_op jit(solution)/shard_map/ppermute | solution.py:257
  35.7 7.0 %collective-permute-start.11 = (bf16[4,192,128]{2,1,0:T(8,128)(2,1)S(1)}, bf16[4,192,128]{2,1,0:T(8,128)(2,1)S(1)}, u32[]{:S(2)}, u32[]{:S(2)}) collective-permute-start(bf16[4,192,128]{2,1,0:T(8,128)(2,1)S(1)} %get-tuple-element.66.refs_8_), channel_id=1, source_target_pairs={{0,2},{2,0},{1,3},{3,1},{4,6},{6,4},{5,7},{7,5},{8,10},{10,8},{9,1... | collective-permute-start | bytes 589832 | tf_op jit(solution)/shard_map/ppermute | solution.py:340
  42.7 9.0 %collective-permute-start.13 = (bf16[4,192,128]{2,1,0:T(8,128)(2,1)S(1)}, bf16[4,192,128]{2,1,0:T(8,128)(2,1)S(1)}, u32[]{:S(2)}, u32[]{:S(2)}) collective-permute-start(bf16[4,192,128]{2,1,0:T(8,128)(2,1)S(1)} %collective-permute-done.11.refs_4_.refs_6_), channel_id=1, source_target_pairs={{0,8},{4,12},{8,0},{12,4},{16,24},{20,28},{24,16},{28,20},{1,9},{5... | collective-permute-start | bytes 589832 | tf_op jit(solution)/shard_map/ppermute | solution.py:276
  47.3 4.4 %collective-permute-start.12 = (bf16[4,192,128]{2,1,0:T(8,128)(2,1)S(1)}, bf16[4,192,128]{2,1,0:T(8,128)(2,1)S(1)}, u32[]{:S(2)}, u32[]{:S(2)}) collective-permute-start(bf16[4,192,128]{2,1,0:T(8,128)(2,1)S(1)} %collective-permute-done.11.refs_4_.refs_6_), channel_id=1, source_target_pairs={{8,16},{12,20},{16,8},{20,12},{9,17},{13,21},{17,9},{21,13},{10,18... | collective-permute-start | bytes 589832 | tf_op jit(solution)/shard_map/ppermute | solution.py:276
  47.9 5.9 %collective-permute-start.16 = (bf16[4,192,128]{2,1,0:T(8,128)(2,1)S(1)}, bf16[4,192,128]{2,1,0:T(8,128)(2,1)S(1)}, u32[]{:S(2)}, u32[]{:S(2)}) collective-permute-start(bf16[4,192,128]{2,1,0:T(8,128)(2,1)S(1)} %collective-permute-done.11.refs_4_.refs_6_), channel_id=1, source_target_pairs={{0,4},{4,0},{8,12},{12,8},{16,20},{20,16},{24,28},{28,24},{1,5},{5... | collective-permute-start | bytes 589832 | tf_op jit(solution)/shard_map/ppermute | solution.py:276
  48.8 5.1 %collective-permute-start.15 = (bf16[4,192,128]{2,1,0:T(8,128)(2,1)S(1)}, bf16[4,192,128]{2,1,0:T(8,128)(2,1)S(1)}, u32[]{:S(2)}, u32[]{:S(2)}) collective-permute-start(bf16[4,192,128]{2,1,0:T(8,128)(2,1)S(1)} %collective-permute-done.11.refs_4_.refs_6_), channel_id=1, source_target_pairs={{0,1},{1,0},{2,3},{3,2},{4,5},{5,4},{6,7},{7,6},{8,9},{9,8},{10,11... | collective-permute-start | bytes 589832 | tf_op jit(solution)/shard_map/ppermute | solution.py:257
  53.8 4.3 %collective-permute-start.18 = (bf16[8,192,128]{2,1,0:T(8,128)(2,1)S(1)}, bf16[8,192,128]{2,1,0:T(8,128)(2,1)S(1)}, u32[]{:S(2)}, u32[]{:S(2)}) collective-permute-start(bf16[8,192,128]{2,1,0:T(8,128)(2,1)S(1)} %pad_maximum_fusion.2.refs_6_), channel_id=1, source_target_pairs={{0,1},{1,0},{2,3},{3,2},{4,5},{5,4},{6,7},{7,6},{8,9},{9,8},{10,11... | collective-permute-start | bytes 1179656 | tf_op jit(solution)/shard_map/ppermute | solution.py:257
  53.8 4.2 %collective-permute-start.17 = (bf16[4,192,128]{2,1,0:T(8,128)(2,1)S(1)}, bf16[4,192,128]{2,1,0:T(8,128)(2,1)S(1)}, u32[]{:S(2)}, u32[]{:S(2)}) collective-permute-start(bf16[4,192,128]{2,1,0:T(8,128)(2,1)S(1)} %collective-permute-done.16.refs_4_), channel_id=1, source_target_pairs={{0,1},{1,0},{2,3},{3,2},{4,5},{5,4},{6,7},{7,6},{8,9},{9,8},{10,11... | collective-permute-start | bytes 589832 | tf_op jit(solution)/shard_map/ppermute | solution.py:257
  54.4 7.5 %collective-permute-start.14 = (bf16[4,192,128]{2,1,0:T(8,128)(2,1)S(1)}, bf16[4,192,128]{2,1,0:T(8,128)(2,1)S(1)}, u32[]{:S(2)}, u32[]{:S(2)}) collective-permute-start(bf16[4,192,128]{2,1,0:T(8,128)(2,1)S(1)} %get-tuple-element.101), channel_id=1, source_target_pairs={{0,4},{4,0},{8,12},{12,8},{16,20},{20,16},{24,28},{28,24},{1,5},{5... | collective-permute-start | bytes 589832 | tf_op jit(solution)/shard_map/ppermute | solution.py:309
  61.8 1.5 %collective-permute-start.19 = (bf16[4,192,128]{2,1,0:T(8,128)(2,1)S(1)}, bf16[4,192,128]{2,1,0:T(8,128)(2,1)S(1)}, u32[]{:S(2)}, u32[]{:S(2)}) collective-permute-start(bf16[4,192,128]{2,1,0:T(8,128)(2,1)S(1)} %collective-permute-done.14.refs_4_), channel_id=1, source_target_pairs={{0,1},{1,0},{2,3},{3,2},{4,5},{5,4},{6,7},{7,6},{8,9},{9,8},{10,11... | collective-permute-start | bytes 589832 | tf_op jit(solution)/shard_map/ppermute | solution.py:257
  65.6 2.1 %collective-permute-start.20 = (bf16[12,192,128]{2,1,0:T(8,128)(2,1)S(1)}, bf16[12,192,128]{2,1,0:T(8,128)(2,1)S(1)}, u32[]{:S(2)}, u32[]{:S(2)}) collective-permute-start(bf16[12,192,128]{2,1,0:T(8,128)(2,1)S(1)} %far_row.3.refs_4_), channel_id=1, source_target_pairs={{0,1},{1,0},{2,3},{3,2},{4,5},{5,4},{6,7},{7,6},{8,9},{9,8},{10,11... | collective-permute-start | bytes 1769480 | tf_op jit(solution)/shard_map/ppermute | solution.py:257
  (2 other events, 8.5 us)

commit v7 on v6

--- a/solution.py
+++ b/solution.py
@@ -96,11 +96,12 @@
     def product(self, slots, first, frames, held=(True, True)):
         block, weight = [], []
         nothing = jnp.zeros((self.depth, LANES), BF16)
-        for slot, tap in slots:
+        for slot, tap, *held_here in slots:
+            held_now = held_here[0] if held_here else held
             row_tap = 1 + self.side * (tap - 1)
             for a in range(3):
                 wanted = [first + f + a for f in range(frames)]
-                here = [held[0 if frame < 2 else 1] for frame in wanted]
+                here = [held_now[0 if frame < 2 else 1] for frame in wanted]
                 if any(here):
                     tile = [self.window[slot, frame] if h else nothing for frame, h in zip(wanted, here)]
                     weight.append(self.weight[self.conv, 3 * a + row_tap])
@@ -168,8 +169,11 @@
 
     def store(q, slots, first):
         for f, value in enumerate(part.product(slots, first, half, (base > 0, True)), first):
-            at = (q + 1) * frames + f
-            ref["sums"][at] = ref["sums_before"][at] + value
+            total = ref["sums_before"][(q + 1) * frames + f] + value
+            if q < 0:
+                ref["first"][f] = total.astype(BF16)
+            else:
+                ref["sums"][q * frames + f] = total
 
     for first in (0, half):
         load(0, first)
@@ -190,50 +194,54 @@
     for first in (0, half):
         for f in range(first, first + half):
             part.activate(0, f, "diagonal", base + f)
-            out[f] = sums[f].astype(BF16)
         for q, tap in ((0, 2), (1, 1)):
             for f, value in enumerate(part.product([(0, tap)], first, half, (base > 0, True)), first):
-                at = (q + 1) * frames + f
+                at = q * frames + f
                 out[at] = (sums[at] + value).astype(BF16)
 
 
+def inside(part, count, q):
+    at = part.ref["place"][2] + part.side * q
+    return jnp.broadcast_to(jnp.logical_and(at >= 0, at < count), (1, LANES))
+
+
+def second_ahead_kernel(frames, count, names, *refs):
+    ref = dict(zip(names, refs))
+    part = Part(1, ref)
+    half = frames // 2
+    for first in (0, half):
+        for f in range(first, first + half):
+            part.activate(0, f, "first", f, inside(part, count, -1))
+        for f, value in enumerate(part.product([(0, 0)], first, half, (False, True)), first):
+            ref["ahead"][f] = value
+
+
 def second_kernel(frames, base, period, count, names, *refs):
     ref = dict(zip(names, refs))
     part = Part(1, ref)
-    row, segment = ref["place"][2], ref["place"][3]
+    segment = ref["place"][3]
     bias = ref["biases"][1]
-    offsets = (0, -1, 1)
-
-    def load(first, last):
-        for slot, q in enumerate(offsets):
-            at = row + part.side * q
-            valid = None if q == 0 else jnp.broadcast_to(jnp.logical_and(at >= 0, at < count), (1, LANES))
-            for f in range(first, last):
-                kept = part.activate(slot, f, "middle", (q + 1) * frames + f, valid)
-                if slot == 0 and f >= frames - 2:
-                    new_tails[2 + f - frames + 2] = kept
-
-    new_tails = {f: ref["kept"][f] for f in range(2)}
-
-    def store(first, last):
-        sums = part.product([(1, 0), (0, 1), (2, 2)], first, last - first, (period == 0, True))
-        for f, value in enumerate(sums, first):
+    half = frames // 2
+    slots = [(0, 1), (1, 2)]
+    if period == 0:
+        for slot, place in enumerate((0, 2, 1)):
+            part.cached(slot, "seconds", TAILS * place)
+        slots.append((2, 0, (True, False)))
+    tails = {f: ref["kept"][f] for f in range(2)}
+    for first in (0, half):
+        for q in range(2):
+            for f in range(first, first + half):
+                kept = part.activate(q, f, "middle", q * frames + f, inside(part, count, q) if q else None)
+                if q == 0 and f >= frames - 2:
+                    tails[4 + f - frames] = kept
+        for f, value in enumerate(part.product(slots, first, half, (period == 0, True)), first):
             before = ref["cached_seconds"][f] if period and f < 2 else bias
-            result = (ref["own"][base + f].astype(F32) + (value + before)).astype(BF16)
+            total = value + ref["ahead"][f] + before
+            result = (ref["own"][base + f].astype(F32) + total).astype(BF16)
             if "result" in ref:
                 ref["result"][f] = result
             ref["out"][f] = jnp.where(segment == period, result, ref["older"][f]) if period else result
-
-    if period == 0:
-        for slot in range(len(offsets)):
-            part.cached(slot, "seconds", TAILS * slot)
-    half = frames // 2
-    load(0, half)
-    store(0, half)
-    load(half, frames)
-    store(half, frames)
-    for f in range(4):
-        tail = new_tails[f]
+    for f, tail in tails.items():
         ref["tails"][f] = jnp.where(segment == period, tail, ref["older_tails"][f]) if period else tail
 
 
@@ -315,7 +323,9 @@
         first = call(functools.partial(own_kernel, frames, base), "own_row", arrays, outs, 1)
         arrays = common | beside | {"sums_before": first["sums"]}
         kernel = functools.partial(beside_kernel, frames, base)
-        sums = call(kernel, "beside_rows", arrays, {"sums": sums_shape}, 3)["sums"]
+        outs = {"sums": tiles(2 * frames, channels, F32), "first": tiles(frames, channels)}
+        both = call(kernel, "beside_rows", arrays, outs, 3)
+        sums, ahead = both["sums"], with_other("first", both["first"])
         diagonal, sums = lax.optimization_barrier((diagonal, sums))
         diagonal = with_other("diagonal", diagonal)
         if period == 0:
@@ -323,9 +333,12 @@
             seconds[2] = lax.ppermute(seconds[2], "rows", across(count))
             seconds = with_other("seconds", jnp.concatenate(seconds, axis=0))
         arrays = common | diagonal | {"sums": sums}
-        outs = {"out": tiles(3 * frames, channels)}
+        outs = {"out": tiles(2 * frames, channels)}
         middle = call(functools.partial(far_kernel, frames, base), "far_row", arrays, outs, 1)["out"]
-        arrays = common | with_other("middle", middle) | {"own": own["own"], "kept": first["kept"]}
+        ahead, middle = lax.optimization_barrier((ahead, middle))
+        kernel = functools.partial(second_ahead_kernel, frames, count)
+        ahead = call(kernel, "second_ahead", common | ahead, {"ahead": tiles(frames, channels, F32)}, 1)
+        arrays = common | with_other("middle", middle) | ahead | {"own": own["own"], "kept": first["kept"]}
         outs = {"out": tiles(frames, channels), "tails": tiles(2 * TAILS, channels)}
         if period:
             arrays |= {"older": out, "older_tails": tails, "cached_seconds": cached_seconds}

time: 71.9 us -> 71.5 us (level)
  waiting for transfers between devices: 17 us -> 13.7 us
  Pallas kernels: 31.1 us -> 33 us
    ppermute x11 -> x13, waiting for transfers between devices: 5.65 us -> 1.55 us  [swapped(): return lax.ppermute(x, 'chan', [(0, 1), (1, 0)])]
    pallas_call x9 -> x11, Pallas kernels: 30.2 us -> 32.2 us  [call(): pl.pallas_call(functools.partial(kernel, names), out_shape=list(outs.valu...]
    ppermute x11 -> x13, starting transfers between devices: 1.71 us -> 2.37 us  [swapped(): return lax.ppermute(x, 'chan', [(0, 1), (1, 0)])]
  transfers between devices with their start and end apart: 21 -> 23, of which waited for: 10 -> 8; matrix products, arithmetic and copies ran while one was open for 2% -> 2% of each run, Pallas kernels for 30% -> 38%
where the time goes in v7:
time: 71.5 us; the launch traced here: 70.8 us
  Pallas kernels  33 us (46%)
  starting transfers between devices  17.2 us (24%)
  waiting for transfers between devices  13.7 us (19%)
  local copies, waits for them, and re-layouts  4.36 us (6%)
  other arithmetic  1.47 us (2%)
  between operations  1.04 us (1%)
    pallas_call x11, Pallas kernels, call(): pl.pallas_call(functools.partial(kernel, names), out_shape=list(outs.valu...  32.2 us
    ppermute x6, starting transfers between devices, exchanged(): lax.ppermute(x, 'rows', pairs)  11.3 us
    ppermute x6, waiting for transfers between devices, exchanged(): lax.ppermute(x, 'rows', pairs)  8.45 us
    unnamed x12, local copies, waits for them, and re-layouts  3.3 us
    ppermute x13, starting transfers between devices, swapped(): return lax.ppermute(x, 'chan', [(0, 1), (1, 0)])  2.37 us
    ppermute x1, waiting for transfers between devices, shards(): lax.ppermute(result, 'segment', [(i, (i + 1) % segments) for i in range(s...  1.8 us
    ppermute x1, starting transfers between devices, shards(): lax.ppermute(result, 'segment', [(i, (i + 1) % segments) for i in range(s...  1.58 us
    ppermute x13, waiting for transfers between devices, swapped(): return lax.ppermute(x, 'chan', [(0, 1), (1, 0)])  1.55 us
  transfers between devices with their start and end apart: 23, of which 8 were waited for; matrix products, arithmetic and copies ran while one was open for 2% of the time, Pallas kernels for 38%

profile of v7, /device:TPU:0, one launch (start us, length us, event | category | flops | bytes accessed | tf_op | source)
XLA Modules:
  0.0 70.8 jit_solution(17504905663786123384)
XLA Ops:
  0.7 1.1 %pad_maximum_fusion.1 = bf16[8,192,128]{2,1,0:T(8,128)(2,1)S(1)} fusion(bf16[4,192,128]{2,1,0:T(8,128)(2,1)} %bitcast.40, bf16[4,192,128]{2,1,0:T(8,128)(2,1)} %bitcast.38), kind=kLoop, calls=%fused_computation.1 | loop fusion | flops 196608 | bytes 786432 | tf_op jit(solution)/shard_map/concatenate | solution.py:300
  1.8 3.0 %collective-permute-start.3 = (bf16[8,192,128]{2,1,0:T(8,128)(2,1)S(1)}, bf16[8,192,128]{2,1,0:T(8,128)(2,1)S(1)}, u32[]{:S(2)}, u32[]{:S(2)}) collective-permute-start(bf16[8,192,128]{2,1,0:T(8,128)(2,1)S(1)} %pad_maximum_fusion.1), channel_id=1, source_target_pairs={{0,4},{4,0},{8,12},{12,8},{16,20},{20,16},{24,28},{28,24},{1,5},{5... | collective-permute-start | bytes 1179656 | tf_op jit(solution)/shard_map/ppermute | solution.py:284
  4.8 1.6 %collective-permute-start.1 = (bf16[8,192,128]{2,1,0:T(8,128)(2,1)S(1)}, bf16[8,192,128]{2,1,0:T(8,128)(2,1)S(1)}, u32[]{:S(2)}, u32[]{:S(2)}) collective-permute-start(bf16[8,192,128]{2,1,0:T(8,128)(2,1)S(1)} %pad_maximum_fusion.1), channel_id=1, source_target_pairs={{0,8},{4,12},{8,0},{12,4},{16,24},{20,28},{24,16},{28,20},{1,9},{5... | collective-permute-start | bytes 1179656 | tf_op jit(solution)/shard_map/ppermute | solution.py:284
  7.0 1.0 %slice_bitcast_fusion = (bf16[2,192,128]{2,1,0:T(8,128)(2,1)S(1)}, bf16[2,192,128]{2,1,0:T(8,128)(2,1)S(1)}) fusion(bf16[1,2,2,1,192,128]{5,4,2,3,1,0:T(8,128)(2,1)} %bitcast.39), kind=kLoop, calls=%fused_computation.10 | loop fusion | bytes 393216 | tf_op jit(solution)/shard_map/slice | solution.py:312
  8.2 3.3 %copy-done = bf16[1,2,192,3,3,3,384]{6,2,5,4,3,1,0:T(8,128)(2,1)S(1)} copy-done((bf16[1,2,192,3,3,3,384]{6,2,5,4,3,1,0:T(8,128)(2,1)S(1)}, bf16[1,2,192,3,3,3,384]{6,2,5,4,3,1,0:T(8,128)(2,1)}, u32[]{:S(2)}) %copy-start) | copy-done | bytes 7962648
  12.3 3.0 %collective-permute-done.1 = bf16[8,192,128]{2,1,0:T(8,128)(2,1)S(1)} collective-permute-done((bf16[8,192,128]{2,1,0:T(8,128)(2,1)S(1)}, bf16[8,192,128]{2,1,0:T(8,128)(2,1)S(1)}, u32[]{:S(2)}, u32[]{:S(2)}) %collective-permute-start.1) | collective-permute-done | bytes 393248 | tf_op jit(solution)/shard_map/ppermute | solution.py:284
  16.7 3.3 %own_row.2 = (f32[12,192,128]{2,1,0:T(8,128)S(1)}, bf16[2,192,128]{2,1,0:T(8,128)(2,1)S(1)}) custom-call(s32[4]{0:T(128)S(1)} %pad_add_fusion.place_ref.refs_0_.refs_10_, f32[2,384,128]{2,1,0:T(8,128)S(1)} %get-tuple-element.87.refs_1_.refs_5_, f32[2,192,128]{2,1,0:T(8,128)S(1)} %get-tuple-element.84.refs_2_, bf16[2,9,576,384]{3,2,1,0:T(8,128)(2,1)S(1)} %bitcast.25, ...), custom_call_target="tpu_custom_call" | custom-call | tf_op jit(solution)/shard_map/own_row/pallas_call | solution.py:252
  20.1 4.3 %beside_rows.2 = (f32[8,192,128]{2,1,0:T(8,128)S(1)}, bf16[4,192,128]{2,1,0:T(8,128)(2,1)S(1)}) custom-call(s32[4]{0:T(128)S(1)} %pad_add_fusion.place_ref.refs_0_.refs_10_, f32[2,384,128]{2,1,0:T(8,128)S(1)} %get-tuple-element.87.refs_1_.refs_5_, f32[2,192,128]{2,1,0:T(8,128)S(1)} %get-tuple-element.84.refs_2_, bf16[2,9,576,384]{3,2,1,0:T(8,128)(2,1)S(1)} %bitcast.26, ...), custom_call_target="tpu_custom_call" | custom-call | tf_op jit(solution)/shard_map/beside_rows/pallas_call | solution.py:252
  24.3 1.0 %collective-permute-done.7.refs_4_.refs_3_ = bf16[6,192,128]{2,1,0:T(8,128)(2,1)S(1)} collective-permute-done((bf16[6,192,128]{2,1,0:T(8,128)(2,1)S(1)}, bf16[6,192,128]{2,1,0:T(8,128)(2,1)S(1)}, u32[]{:S(2)}, u32[]{:S(2)}) %collective-permute-start.7) | collective-permute-done | bytes 294944 | tf_op jit(solution)/shard_map/ppermute | solution.py:317
  26.9 2.5 %far_row.2.refs_4_ = bf16[8,192,128]{2,1,0:T(8,128)(2,1)S(1)} custom-call(s32[4]{0:T(128)S(1)} %pad_add_fusion.place_ref.refs_0_.refs_10_, f32[2,384,128]{2,1,0:T(8,128)S(1)} %get-tuple-element.87.refs_1_.refs_5_, f32[2,192,128]{2,1,0:T(8,128)S(1)} %get-tuple-element.84.refs_2_, bf16[2,9,576,384]{3,2,1,0:T(8,128)(2,1)S(1)} %bitcast.27, ...), custom_call_target="tpu_custom_call" | custom-call | tf_op jit(solution)/shard_map/far_row/pallas_call | solution.py:252
  30.7 1.6 %second_ahead.2.refs_6_ = f32[4,192,128]{2,1,0:T(8,128)S(1)} custom-call(s32[4]{0:T(128)S(1)} %pad_add_fusion.place_ref.refs_0_.refs_10_, f32[2,384,128]{2,1,0:T(8,128)S(1)} %get-tuple-element.87.refs_1_.refs_5_, f32[2,192,128]{2,1,0:T(8,128)S(1)} %get-tuple-element.84.refs_2_, bf16[2,9,576,384]{3,2,1,0:T(8,128)(2,1)S(1)} %bitcast.28, ...), custom_call_target="tpu_custom_call" | custom-call | tf_op jit(solution)/shard_map/second_ahead/pallas_call | solution.py:252
  32.3 2.8 %second.2 = (bf16[4,192,128]{2,1,0:T(8,128)(2,1)S(1)}, bf16[4,192,128]{2,1,0:T(8,128)(2,1)S(1)}) custom-call(s32[4]{0:T(128)S(1)} %pad_add_fusion.place_ref.refs_0_.refs_10_, f32[2,384,128]{2,1,0:T(8,128)S(1)} %get-tuple-element.87.refs_1_.refs_5_, f32[2,192,128]{2,1,0:T(8,128)S(1)} %get-tuple-element.84.refs_2_, bf16[2,9,576,384]{3,2,1,0:T(8,128)(2,1)S(1)} %bitcast.29, ...), custom_call_target="tpu_custom_call" | custom-call | tf_op jit(solution)/shard_map/second/pallas_call | solution.py:252
  35.1 1.6 %collective-permute-start.12 = (bf16[4,192,128]{2,1,0:T(8,128)(2,1)S(1)}, bf16[4,192,128]{2,1,0:T(8,128)(2,1)S(1)}, u32[]{:S(2)}, u32[]{:S(2)}) collective-permute-start(bf16[4,192,128]{2,1,0:T(8,128)(2,1)S(1)} %get-tuple-element.81.refs_9_), channel_id=1, source_target_pairs={{0,2},{2,0},{1,3},{3,1},{4,6},{6,4},{5,7},{7,5},{8,10},{10,8},{9,1... | collective-permute-start | bytes 589832 | tf_op jit(solution)/shard_map/ppermute | solution.py:353
  36.7 4.0 %cached_rows.1 = (f32[6,192,128]{2,1,0:T(8,128)S(1)}, f32[2,192,128]{2,1,0:T(8,128)S(1)}) custom-call(bf16[6,192,128]{2,1,0:T(8,128)(2,1)S(1)} %pad_maximum_fusion.4.refs_4_.refs_0_, bf16[6,192,128]{2,1,0:T(8,128)(2,1)S(1)} %collective-permute-done.4.refs_5_.refs_1_, f32[2,192,128]{2,1,0:T(8,128)S(1)} %get-tuple-element.84.refs_2_, ...), custom_call_target="tpu_custom_call" | custom-call | tf_op jit(solution)/shard_map/cached_rows/pallas_call | solution.py:252
  40.7 1.8 %collective-permute-done.12.refs_4_.refs_7_ = bf16[4,192,128]{2,1,0:T(8,128)(2,1)S(1)} collective-permute-done((bf16[4,192,128]{2,1,0:T(8,128)(2,1)S(1)}, bf16[4,192,128]{2,1,0:T(8,128)(2,1)S(1)}, u32[]{:S(2)}, u32[]{:S(2)}) %collective-permute-start.12) | collective-permute-done | bytes 196640 | tf_op jit(solution)/shard_map/ppermute | solution.py:353
  42.5 4.6 %collective-permute-start.16 = (bf16[4,192,128]{2,1,0:T(8,128)(2,1)S(1)}, bf16[4,192,128]{2,1,0:T(8,128)(2,1)S(1)}, u32[]{:S(2)}, u32[]{:S(2)}) collective-permute-start(bf16[4,192,128]{2,1,0:T(8,128)(2,1)S(1)} %collective-permute-done.12.refs_4_.refs_7_), channel_id=1, source_target_pairs={{0,8},{4,12},{8,0},{12,4},{16,24},{20,28},{24,16},{28,20},{1,9},{5... | collective-permute-start | bytes 589832 | tf_op jit(solution)/shard_map/ppermute | solution.py:284
  48.6 3.3 %collective-permute-done.16 = bf16[4,192,128]{2,1,0:T(8,128)(2,1)S(1)} collective-permute-done((bf16[4,192,128]{2,1,0:T(8,128)(2,1)S(1)}, bf16[4,192,128]{2,1,0:T(8,128)(2,1)S(1)}, u32[]{:S(2)}, u32[]{:S(2)}) %collective-permute-start.16) | collective-permute-done | bytes 196640 | tf_op jit(solution)/shard_map/ppermute | solution.py:284
  52.0 2.1 %collective-permute-done.14.refs_4_ = bf16[4,192,128]{2,1,0:T(8,128)(2,1)S(1)} collective-permute-done((bf16[4,192,128]{2,1,0:T(8,128)(2,1)S(1)}, bf16[4,192,128]{2,1,0:T(8,128)(2,1)S(1)}, u32[]{:S(2)}, u32[]{:S(2)}) %collective-permute-start.14) | collective-permute-done | bytes 196640 | tf_op jit(solution)/shard_map/ppermute | solution.py:284
  55.3 3.0 %own_row.3 = (f32[12,192,128]{2,1,0:T(8,128)S(1)}, bf16[2,192,128]{2,1,0:T(8,128)(2,1)S(1)}) custom-call(s32[4]{0:T(128)S(1)} %pad_add_fusion.place_ref.refs_0_.refs_10_, f32[2,384,128]{2,1,0:T(8,128)S(1)} %get-tuple-element.87.refs_1_.refs_5_, f32[2,192,128]{2,1,0:T(8,128)S(1)} %get-tuple-element.84.refs_2_, bf16[2,9,576,384]{3,2,1,0:T(8,128)(2,1)S(1)} %bitcast.31, ...), custom_call_target="tpu_custom_call" | custom-call | tf_op jit(solution)/shard_map/own_row/pallas_call | solution.py:252
  58.3 3.7 %beside_rows.3 = (f32[8,192,128]{2,1,0:T(8,128)S(1)}, bf16[4,192,128]{2,1,0:T(8,128)(2,1)S(1)}) custom-call(s32[4]{0:T(128)S(1)} %pad_add_fusion.place_ref.refs_0_.refs_10_, f32[2,384,128]{2,1,0:T(8,128)S(1)} %get-tuple-element.87.refs_1_.refs_5_, f32[2,192,128]{2,1,0:T(8,128)S(1)} %get-tuple-element.84.refs_2_, bf16[2,9,576,384]{3,2,1,0:T(8,128)(2,1)S(1)} %bitcast.32, ...), custom_call_target="tpu_custom_call" | custom-call | tf_op jit(solution)/shard_map/beside_rows/pallas_call | solution.py:252
  62.6 0.9 %collective-permute-done.21.refs_5_ = bf16[4,192,128]{2,1,0:T(8,128)(2,1)S(1)} collective-permute-done((bf16[4,192,128]{2,1,0:T(8,128)(2,1)S(1)}, bf16[4,192,128]{2,1,0:T(8,128)(2,1)S(1)}, u32[]{:S(2)}, u32[]{:S(2)}) %collective-permute-start.21) | collective-permute-done | bytes 196640 | tf_op jit(solution)/shard_map/ppermute | solution.py:265
  63.6 2.3 %far_row.3.refs_4_ = bf16[8,192,128]{2,1,0:T(8,128)(2,1)S(1)} custom-call(s32[4]{0:T(128)S(1)} %pad_add_fusion.place_ref.refs_0_.refs_10_, f32[2,384,128]{2,1,0:T(8,128)S(1)} %get-tuple-element.87.refs_1_.refs_5_, f32[2,192,128]{2,1,0:T(8,128)S(1)} %get-tuple-element.84.refs_2_, bf16[2,9,576,384]{3,2,1,0:T(8,128)(2,1)S(1)} %bitcast.33, ...), custom_call_target="tpu_custom_call" | custom-call | tf_op jit(solution)/shard_map/far_row/pallas_call | solution.py:252
  66.1 1.6 %second_ahead.3.refs_6_ = f32[4,192,128]{2,1,0:T(8,128)S(1)} custom-call(s32[4]{0:T(128)S(1)} %pad_add_fusion.place_ref.refs_0_.refs_10_, f32[2,384,128]{2,1,0:T(8,128)S(1)} %get-tuple-element.87.refs_1_.refs_5_, f32[2,192,128]{2,1,0:T(8,128)S(1)} %get-tuple-element.84.refs_2_, bf16[2,9,576,384]{3,2,1,0:T(8,128)(2,1)S(1)} %bitcast.34, ...), custom_call_target="tpu_custom_call" | custom-call | tf_op jit(solution)/shard_map/second_ahead/pallas_call | solution.py:252
  67.7 3.0 %second.3 = (bf16[4,192,128]{2,1,0:T(8,128)(2,1)}, bf16[4,192,128]{2,1,0:T(8,128)(2,1)}) custom-call(s32[4]{0:T(128)S(1)} %pad_add_fusion.place_ref.refs_0_.refs_10_, f32[2,384,128]{2,1,0:T(8,128)S(1)} %get-tuple-element.87.refs_1_.refs_5_, f32[2,192,128]{2,1,0:T(8,128)S(1)} %get-tuple-element.84.refs_2_, bf16[2,9,576,384]{3,2,1,0:T(8,128)(2,1)S(1)} %bitcast.35, ...), custom_call_target="tpu_custom_call" | custom-call | tf_op jit(solution)/shard_map/second/pallas_call | solution.py:252
  (63 shorter events, 9.3 us)
Async XLA Ops:
  0.6 7.6 %copy-start.2 = (f32[1,2,384]{2,1,0:T(2,128)S(1)}, f32[1,2,384]{2,1,0:T(2,128)}, u32[]{:S(2)}) copy-start(f32[1,2,384]{2,1,0:T(2,128)} %param.9) | copy-start | bytes 9220
  1.8 13.7 %collective-permute-start.3 = (bf16[8,192,128]{2,1,0:T(8,128)(2,1)S(1)}, bf16[8,192,128]{2,1,0:T(8,128)(2,1)S(1)}, u32[]{:S(2)}, u32[]{:S(2)}) collective-permute-start(bf16[8,192,128]{2,1,0:T(8,128)(2,1)S(1)} %pad_maximum_fusion.1), channel_id=1, source_target_pairs={{0,4},{4,0},{8,12},{12,8},{16,20},{20,16},{24,28},{28,24},{1,5},{5... | collective-permute-start | bytes 1179656 | tf_op jit(solution)/shard_map/ppermute | solution.py:284
  4.8 10.6 %collective-permute-start.1 = (bf16[8,192,128]{2,1,0:T(8,128)(2,1)S(1)}, bf16[8,192,128]{2,1,0:T(8,128)(2,1)S(1)}, u32[]{:S(2)}, u32[]{:S(2)}) collective-permute-start(bf16[8,192,128]{2,1,0:T(8,128)(2,1)S(1)} %pad_maximum_fusion.1), channel_id=1, source_target_pairs={{0,8},{4,12},{8,0},{12,4},{16,24},{20,28},{24,16},{28,20},{1,9},{5... | collective-permute-start | bytes 1179656 | tf_op jit(solution)/shard_map/ppermute | solution.py:284
  6.3 9.0 %collective-permute-start = (bf16[8,192,128]{2,1,0:T(8,128)(2,1)S(1)}, bf16[8,192,128]{2,1,0:T(8,128)(2,1)S(1)}, u32[]{:S(2)}, u32[]{:S(2)}) collective-permute-start(bf16[8,192,128]{2,1,0:T(8,128)(2,1)S(1)} %pad_maximum_fusion.1), channel_id=1, source_target_pairs={{8,16},{12,20},{16,8},{20,12},{9,17},{13,21},{17,9},{21,13},{10,18... | collective-permute-start | bytes 1179656 | tf_op jit(solution)/shard_map/ppermute | solution.py:284
  8.0 7.6 %collective-permute-start.2 = (bf16[6,192,128]{2,1,0:T(8,128)(2,1)S(1)}, bf16[6,192,128]{2,1,0:T(8,128)(2,1)S(1)}, u32[]{:S(2)}, u32[]{:S(2)}) collective-permute-start(bf16[6,192,128]{2,1,0:T(8,128)(2,1)S(1)} %pad_maximum_fusion.3.refs_4_.refs_7_.refs_6_), channel_id=1, source_target_pairs={{0,1},{1,0},{2,3},{3,2},{4,5},{5,4},{6,7},{7,6},{8,9},{9,8},{10,11... | collective-permute-start | bytes 884744 | tf_op jit(solution)/shard_map/ppermute | solution.py:265
  15.7 4.4 %collective-permute-start.5 = (bf16[12,192,128]{2,1,0:T(8,128)(2,1)S(1)}, bf16[12,192,128]{2,1,0:T(8,128)(2,1)S(1)}, u32[]{:S(2)}, u32[]{:S(2)}) collective-permute-start(bf16[12,192,128]{2,1,0:T(8,128)(2,1)S(1)} %pad_maximum_fusion.refs_6_.refs_8_), channel_id=1, source_target_pairs={{0,1},{1,0},{2,3},{3,2},{4,5},{5,4},{6,7},{7,6},{8,9},{9,8},{10,11... | collective-permute-start | bytes 1769480 | tf_op jit(solution)/shard_map/ppermute | solution.py:265
  15.8 4.3 %collective-permute-start.4 = (bf16[6,192,128]{2,1,0:T(8,128)(2,1)S(1)}, bf16[6,192,128]{2,1,0:T(8,128)(2,1)S(1)}, u32[]{:S(2)}, u32[]{:S(2)}) collective-permute-start(bf16[6,192,128]{2,1,0:T(8,128)(2,1)S(1)} %pad_maximum_fusion.4.refs_4_.refs_0_), channel_id=1, source_target_pairs={{0,1},{1,0},{2,3},{3,2},{4,5},{5,4},{6,7},{7,6},{8,9},{9,8},{10,11... | collective-permute-start | bytes 884744 | tf_op jit(solution)/shard_map/ppermute | solution.py:265
  16.3 9.1 %collective-permute-start.7 = (bf16[6,192,128]{2,1,0:T(8,128)(2,1)S(1)}, bf16[6,192,128]{2,1,0:T(8,128)(2,1)S(1)}, u32[]{:S(2)}, u32[]{:S(2)}) collective-permute-start(bf16[6,192,128]{2,1,0:T(8,128)(2,1)S(1)} %pad_maximum_fusion.5), channel_id=1, source_target_pairs={{0,4},{4,0},{8,12},{12,8},{16,20},{20,16},{24,28},{28,24},{1,5},{5... | collective-permute-start | bytes 884744 | tf_op jit(solution)/shard_map/ppermute | solution.py:317
  25.3 1.6 %collective-permute-start.8 = (bf16[6,192,128]{2,1,0:T(8,128)(2,1)S(1)}, bf16[6,192,128]{2,1,0:T(8,128)(2,1)S(1)}, u32[]{:S(2)}, u32[]{:S(2)}) collective-permute-start(bf16[6,192,128]{2,1,0:T(8,128)(2,1)S(1)} %collective-permute-done.7.refs_4_.refs_3_), channel_id=1, source_target_pairs={{0,1},{1,0},{2,3},{3,2},{4,5},{5,4},{6,7},{7,6},{8,9},{9,8},{10,11... | collective-permute-start | bytes 884744 | tf_op jit(solution)/shard_map/ppermute | solution.py:265
  25.3 5.2 %collective-permute-start.10 = (bf16[2,192,128]{2,1,0:T(8,128)(2,1)S(1)}, bf16[2,192,128]{2,1,0:T(8,128)(2,1)S(1)}, u32[]{:S(2)}, u32[]{:S(2)}) collective-permute-start(bf16[2,192,128]{2,1,0:T(8,128)(2,1)S(1)} %get-tuple-element.80), channel_id=1, source_target_pairs={{0,4},{4,0},{8,12},{12,8},{16,20},{20,16},{24,28},{28,24},{1,5},{5... | collective-permute-start | bytes 294920 | tf_op jit(solution)/shard_map/ppermute | solution.py:333
  26.1 3.3 %collective-permute-start.6 = (bf16[4,192,128]{2,1,0:T(8,128)(2,1)S(1)}, bf16[4,192,128]{2,1,0:T(8,128)(2,1)S(1)}, u32[]{:S(2)}, u32[]{:S(2)}) collective-permute-start(bf16[4,192,128]{2,1,0:T(8,128)(2,1)S(1)} %get-tuple-element.75.refs_4_), channel_id=1, source_target_pairs={{0,1},{1,0},{2,3},{3,2},{4,5},{5,4},{6,7},{7,6},{8,9},{9,8},{10,11... | collective-permute-start | bytes 589832 | tf_op jit(solution)/shard_map/ppermute | solution.py:265
  29.5 2.8 %collective-permute-start.9 = (bf16[8,192,128]{2,1,0:T(8,128)(2,1)S(1)}, bf16[8,192,128]{2,1,0:T(8,128)(2,1)S(1)}, u32[]{:S(2)}, u32[]{:S(2)}) collective-permute-start(bf16[8,192,128]{2,1,0:T(8,128)(2,1)S(1)} %far_row.2.refs_4_), channel_id=1, source_target_pairs={{0,1},{1,0},{2,3},{3,2},{4,5},{5,4},{6,7},{7,6},{8,9},{9,8},{10,11... | collective-permute-start | bytes 1179656 | tf_op jit(solution)/shard_map/ppermute | solution.py:265
  30.6 1.7 %collective-permute-start.11 = (bf16[6,192,128]{2,1,0:T(8,128)(2,1)S(1)}, bf16[6,192,128]{2,1,0:T(8,128)(2,1)S(1)}, u32[]{:S(2)}, u32[]{:S(2)}) collective-permute-start(bf16[6,192,128]{2,1,0:T(8,128)(2,1)S(1)} %constant_dynamic-update-slice_fusion.refs_9_.refs_11_), channel_id=1, source_target_pairs={{0,1},{1,0},{2,3},{3,2},{4,5},{5,4},{6,7},{7,6},{8,9},{9,8},{10,11... | collective-permute-start | bytes 884744 | tf_op jit(solution)/shard_map/ppermute | solution.py:265
  35.1 7.4 %collective-permute-start.12 = (bf16[4,192,128]{2,1,0:T(8,128)(2,1)S(1)}, bf16[4,192,128]{2,1,0:T(8,128)(2,1)S(1)}, u32[]{:S(2)}, u32[]{:S(2)}) collective-permute-start(bf16[4,192,128]{2,1,0:T(8,128)(2,1)S(1)} %get-tuple-element.81.refs_9_), channel_id=1, source_target_pairs={{0,2},{2,0},{1,3},{3,1},{4,6},{6,4},{5,7},{7,5},{8,10},{10,8},{9,1... | collective-permute-start | bytes 589832 | tf_op jit(solution)/shard_map/ppermute | solution.py:353
  42.5 9.4 %collective-permute-start.16 = (bf16[4,192,128]{2,1,0:T(8,128)(2,1)S(1)}, bf16[4,192,128]{2,1,0:T(8,128)(2,1)S(1)}, u32[]{:S(2)}, u32[]{:S(2)}) collective-permute-start(bf16[4,192,128]{2,1,0:T(8,128)(2,1)S(1)} %collective-permute-done.12.refs_4_.refs_7_), channel_id=1, source_target_pairs={{0,8},{4,12},{8,0},{12,4},{16,24},{20,28},{24,16},{28,20},{1,9},{5... | collective-permute-start | bytes 589832 | tf_op jit(solution)/shard_map/ppermute | solution.py:284
  47.1 4.8 %collective-permute-start.15 = (bf16[4,192,128]{2,1,0:T(8,128)(2,1)S(1)}, bf16[4,192,128]{2,1,0:T(8,128)(2,1)S(1)}, u32[]{:S(2)}, u32[]{:S(2)}) collective-permute-start(bf16[4,192,128]{2,1,0:T(8,128)(2,1)S(1)} %collective-permute-done.12.refs_4_.refs_7_), channel_id=1, source_target_pairs={{8,16},{12,20},{16,8},{20,12},{9,17},{13,21},{17,9},{21,13},{10,18... | collective-permute-start | bytes 589832 | tf_op jit(solution)/shard_map/ppermute | solution.py:284
  47.8 6.3 %collective-permute-start.14 = (bf16[4,192,128]{2,1,0:T(8,128)(2,1)S(1)}, bf16[4,192,128]{2,1,0:T(8,128)(2,1)S(1)}, u32[]{:S(2)}, u32[]{:S(2)}) collective-permute-start(bf16[4,192,128]{2,1,0:T(8,128)(2,1)S(1)} %collective-permute-done.12.refs_4_.refs_7_), channel_id=1, source_target_pairs={{0,4},{4,0},{8,12},{12,8},{16,20},{20,16},{24,28},{28,24},{1,5},{5... | collective-permute-start | bytes 589832 | tf_op jit(solution)/shard_map/ppermute | solution.py:284
  48.6 5.5 %collective-permute-start.13 = (bf16[4,192,128]{2,1,0:T(8,128)(2,1)S(1)}, bf16[4,192,128]{2,1,0:T(8,128)(2,1)S(1)}, u32[]{:S(2)}, u32[]{:S(2)}) collective-permute-start(bf16[4,192,128]{2,1,0:T(8,128)(2,1)S(1)} %collective-permute-done.12.refs_4_.refs_7_), channel_id=1, source_target_pairs={{0,1},{1,0},{2,3},{3,2},{4,5},{5,4},{6,7},{7,6},{8,9},{9,8},{10,11... | collective-permute-start | bytes 589832 | tf_op jit(solution)/shard_map/ppermute | solution.py:265
  54.1 4.2 %collective-permute-start.18 = (bf16[8,192,128]{2,1,0:T(8,128)(2,1)S(1)}, bf16[8,192,128]{2,1,0:T(8,128)(2,1)S(1)}, u32[]{:S(2)}, u32[]{:S(2)}) collective-permute-start(bf16[8,192,128]{2,1,0:T(8,128)(2,1)S(1)} %pad_maximum_fusion.2.refs_6_), channel_id=1, source_target_pairs={{0,1},{1,0},{2,3},{3,2},{4,5},{5,4},{6,7},{7,6},{8,9},{9,8},{10,11... | collective-permute-start | bytes 1179656 | tf_op jit(solution)/shard_map/ppermute | solution.py:265
  54.1 4.2 %collective-permute-start.17 = (bf16[4,192,128]{2,1,0:T(8,128)(2,1)S(1)}, bf16[4,192,128]{2,1,0:T(8,128)(2,1)S(1)}, u32[]{:S(2)}, u32[]{:S(2)}) collective-permute-start(bf16[4,192,128]{2,1,0:T(8,128)(2,1)S(1)} %collective-permute-done.14.refs_4_), channel_id=1, source_target_pairs={{0,1},{1,0},{2,3},{3,2},{4,5},{5,4},{6,7},{7,6},{8,9},{9,8},{10,11... | collective-permute-start | bytes 589832 | tf_op jit(solution)/shard_map/ppermute | solution.py:265
  54.6 7.5 %collective-permute-start.20 = (bf16[4,192,128]{2,1,0:T(8,128)(2,1)S(1)}, bf16[4,192,128]{2,1,0:T(8,128)(2,1)S(1)}, u32[]{:S(2)}, u32[]{:S(2)}) collective-permute-start(bf16[4,192,128]{2,1,0:T(8,128)(2,1)S(1)} %get-tuple-element.120), channel_id=1, source_target_pairs={{0,4},{4,0},{8,12},{12,8},{16,20},{20,16},{24,28},{28,24},{1,5},{5... | collective-permute-start | bytes 589832 | tf_op jit(solution)/shard_map/ppermute | solution.py:317
  62.1 1.5 %collective-permute-start.21 = (bf16[4,192,128]{2,1,0:T(8,128)(2,1)S(1)}, bf16[4,192,128]{2,1,0:T(8,128)(2,1)S(1)}, u32[]{:S(2)}, u32[]{:S(2)}) collective-permute-start(bf16[4,192,128]{2,1,0:T(8,128)(2,1)S(1)} %collective-permute-done.20.refs_4_), channel_id=1, source_target_pairs={{0,1},{1,0},{2,3},{3,2},{4,5},{5,4},{6,7},{7,6},{8,9},{9,8},{10,11... | collective-permute-start | bytes 589832 | tf_op jit(solution)/shard_map/ppermute | solution.py:265
  62.1 3.7 %collective-permute-start.19 = (bf16[4,192,128]{2,1,0:T(8,128)(2,1)S(1)}, bf16[4,192,128]{2,1,0:T(8,128)(2,1)S(1)}, u32[]{:S(2)}, u32[]{:S(2)}) collective-permute-start(bf16[4,192,128]{2,1,0:T(8,128)(2,1)S(1)} %get-tuple-element.109.refs_4_), channel_id=1, source_target_pairs={{0,1},{1,0},{2,3},{3,2},{4,5},{5,4},{6,7},{7,6},{8,9},{9,8},{10,11... | collective-permute-start | bytes 589832 | tf_op jit(solution)/shard_map/ppermute | solution.py:265
  65.9 1.9 %collective-permute-start.22 = (bf16[8,192,128]{2,1,0:T(8,128)(2,1)S(1)}, bf16[8,192,128]{2,1,0:T(8,128)(2,1)S(1)}, u32[]{:S(2)}, u32[]{:S(2)}) collective-permute-start(bf16[8,192,128]{2,1,0:T(8,128)(2,1)S(1)} %far_row.3.refs_4_), channel_id=1, source_target_pairs={{0,1},{1,0},{2,3},{3,2},{4,5},{5,4},{6,7},{7,6},{8,9},{9,8},{10,11... | collective-permute-start | bytes 1179656 | tf_op jit(solution)/shard_map/ppermute | solution.py:265
  (4 other events, 23.4 us)

commit v8 on v7

--- a/solution.py
+++ b/solution.py
@@ -245,6 +245,9 @@
         ref["tails"][f] = jnp.where(segment == period, tail, ref["older_tails"][f]) if period else tail
 
 
+TAKES = {"own_row": 3.0, "beside_rows": 3.7, "far_row": 2.3, "second_ahead": 1.6, "second": 3.0, "cached_rows": 4.0}
+
+
 def call(kernel, name, arrays, outs, slots):
     depth = arrays["weight"].shape[-1]
     scratch = {"window": pltpu.VMEM((slots, FRAMES + 2, depth, LANES), BF16)}
@@ -256,6 +259,7 @@
         out_specs=[VMEM] * len(outs),
         scratch_shapes=list(scratch.values()),
         compiler_params=params(16),
+        cost_estimate=pl.CostEstimate(flops=int(TAKES[name] * 1.15e+09), transcendentals=0, bytes_accessed=0),
         name=name,
     )(*arrays.values())
     return dict(zip(outs, results))

time: 71.5 us -> 71.2 us (level)
  no operation moved by 1% of the time
where the time goes in v8:
time: 71.2 us; the launch traced here: 70.7 us
  Pallas kernels  33 us (46%)
  starting transfers between devices  17.2 us (24%)
  waiting for transfers between devices  13.6 us (19%)
  local copies, waits for them, and re-layouts  4.36 us (6%)
  other arithmetic  1.47 us (2%)
  between operations  1.04 us (1%)
    pallas_call x11, Pallas kernels, call(): pl.pallas_call(functools.partial(kernel, names), out_shape=list(outs.valu...  32.2 us
    ppermute x6, starting transfers between devices, exchanged(): lax.ppermute(x, 'rows', pairs)  11.3 us
    ppermute x6, waiting for transfers between devices, exchanged(): lax.ppermute(x, 'rows', pairs)  8.41 us
    unnamed x12, local copies, waits for them, and re-layouts  3.3 us
    ppermute x13, starting transfers between devices, swapped(): return lax.ppermute(x, 'chan', [(0, 1), (1, 0)])  2.24 us
    ppermute x1, waiting for transfers between devices, shards(): lax.ppermute(result, 'segment', [(i, (i + 1) % segments) for i in range(s...  1.8 us
    ppermute x1, starting transfers between devices, shards(): lax.ppermute(result, 'segment', [(i, (i + 1) % segments) for i in range(s...  1.58 us
    ppermute x13, waiting for transfers between devices, swapped(): return lax.ppermute(x, 'chan', [(0, 1), (1, 0)])  1.52 us
  transfers between devices with their start and end apart: 23, of which 8 were waited for; matrix products, arithmetic and copies ran while one was open for 2% of the time, Pallas kernels for 38%

profile of v8, /device:TPU:0, one launch (start us, length us, event | category | flops | bytes accessed | tf_op | source)
XLA Modules:
  0.0 70.7 jit_solution(5231070464866092389)
XLA Ops:
  0.7 1.1 %pad_maximum_fusion.1 = bf16[8,192,128]{2,1,0:T(8,128)(2,1)S(1)} fusion(bf16[4,192,128]{2,1,0:T(8,128)(2,1)} %bitcast.40, bf16[4,192,128]{2,1,0:T(8,128)(2,1)} %bitcast.38), kind=kLoop, calls=%fused_computation.1 | loop fusion | flops 196608 | bytes 786432 | tf_op jit(solution)/shard_map/concatenate | solution.py:304
  1.8 3.0 %collective-permute-start.3 = (bf16[8,192,128]{2,1,0:T(8,128)(2,1)S(1)}, bf16[8,192,128]{2,1,0:T(8,128)(2,1)S(1)}, u32[]{:S(2)}, u32[]{:S(2)}) collective-permute-start(bf16[8,192,128]{2,1,0:T(8,128)(2,1)S(1)} %pad_maximum_fusion.1), channel_id=1, source_target_pairs={{0,4},{4,0},{8,12},{12,8},{16,20},{20,16},{24,28},{28,24},{1,5},{5... | collective-permute-start | bytes 1179656 | tf_op jit(solution)/shard_map/ppermute | solution.py:288
  4.8 1.6 %collective-permute-start.1 = (bf16[8,192,128]{2,1,0:T(8,128)(2,1)S(1)}, bf16[8,192,128]{2,1,0:T(8,128)(2,1)S(1)}, u32[]{:S(2)}, u32[]{:S(2)}) collective-permute-start(bf16[8,192,128]{2,1,0:T(8,128)(2,1)S(1)} %pad_maximum_fusion.1), channel_id=1, source_target_pairs={{0,8},{4,12},{8,0},{12,4},{16,24},{20,28},{24,16},{28,20},{1,9},{5... | collective-permute-start | bytes 1179656 | tf_op jit(solution)/shard_map/ppermute | solution.py:288
  7.0 1.0 %slice_bitcast_fusion = (bf16[2,192,128]{2,1,0:T(8,128)(2,1)S(1)}, bf16[2,192,128]{2,1,0:T(8,128)(2,1)S(1)}) fusion(bf16[1,2,2,1,192,128]{5,4,2,3,1,0:T(8,128)(2,1)} %bitcast.39), kind=kLoop, calls=%fused_computation.10 | loop fusion | bytes 393216 | tf_op jit(solution)/shard_map/slice | solution.py:316
  8.2 3.3 %copy-done = bf16[1,2,192,3,3,3,384]{6,2,5,4,3,1,0:T(8,128)(2,1)S(1)} copy-done((bf16[1,2,192,3,3,3,384]{6,2,5,4,3,1,0:T(8,128)(2,1)S(1)}, bf16[1,2,192,3,3,3,384]{6,2,5,4,3,1,0:T(8,128)(2,1)}, u32[]{:S(2)}) %copy-start) | copy-done | bytes 7962648
  12.3 3.0 %collective-permute-done.1 = bf16[8,192,128]{2,1,0:T(8,128)(2,1)S(1)} collective-permute-done((bf16[8,192,128]{2,1,0:T(8,128)(2,1)S(1)}, bf16[8,192,128]{2,1,0:T(8,128)(2,1)S(1)}, u32[]{:S(2)}, u32[]{:S(2)}) %collective-permute-start.1) | collective-permute-done | bytes 393248 | tf_op jit(solution)/shard_map/ppermute | solution.py:288
  16.7 3.3 %own_row.2 = (f32[12,192,128]{2,1,0:T(8,128)S(1)}, bf16[2,192,128]{2,1,0:T(8,128)(2,1)S(1)}) custom-call(s32[4]{0:T(128)S(1)} %pad_add_fusion.place_ref.refs_0_.refs_10_, f32[2,384,128]{2,1,0:T(8,128)S(1)} %get-tuple-element.87.refs_1_.refs_5_, f32[2,192,128]{2,1,0:T(8,128)S(1)} %get-tuple-element.84.refs_2_, bf16[2,9,576,384]{3,2,1,0:T(8,128)(2,1)S(1)} %bitcast.25, ...), custom_call_target="tpu_custom_call" | custom-call | flops 3449999872 | tf_op jit(solution)/shard_map/own_row/pallas_call | solution.py:255
  20.1 4.3 %beside_rows.2 = (f32[8,192,128]{2,1,0:T(8,128)S(1)}, bf16[4,192,128]{2,1,0:T(8,128)(2,1)S(1)}) custom-call(s32[4]{0:T(128)S(1)} %pad_add_fusion.place_ref.refs_0_.refs_10_, f32[2,384,128]{2,1,0:T(8,128)S(1)} %get-tuple-element.87.refs_1_.refs_5_, f32[2,192,128]{2,1,0:T(8,128)S(1)} %get-tuple-element.84.refs_2_, bf16[2,9,576,384]{3,2,1,0:T(8,128)(2,1)S(1)} %bitcast.26, ...), custom_call_target="tpu_custom_call" | custom-call | flops 4255000064 | tf_op jit(solution)/shard_map/beside_rows/pallas_call | solution.py:255
  24.4 1.0 %collective-permute-done.7.refs_4_.refs_3_ = bf16[6,192,128]{2,1,0:T(8,128)(2,1)S(1)} collective-permute-done((bf16[6,192,128]{2,1,0:T(8,128)(2,1)S(1)}, bf16[6,192,128]{2,1,0:T(8,128)(2,1)S(1)}, u32[]{:S(2)}, u32[]{:S(2)}) %collective-permute-start.7) | collective-permute-done | bytes 294944 | tf_op jit(solution)/shard_map/ppermute | solution.py:321
  26.9 2.5 %far_row.2.refs_4_ = bf16[8,192,128]{2,1,0:T(8,128)(2,1)S(1)} custom-call(s32[4]{0:T(128)S(1)} %pad_add_fusion.place_ref.refs_0_.refs_10_, f32[2,384,128]{2,1,0:T(8,128)S(1)} %get-tuple-element.87.refs_1_.refs_5_, f32[2,192,128]{2,1,0:T(8,128)S(1)} %get-tuple-element.84.refs_2_, bf16[2,9,576,384]{3,2,1,0:T(8,128)(2,1)S(1)} %bitcast.27, ...), custom_call_target="tpu_custom_call" | custom-call | flops 2644999936 | tf_op jit(solution)/shard_map/far_row/pallas_call | solution.py:255
  30.7 1.6 %second_ahead.2.refs_6_ = f32[4,192,128]{2,1,0:T(8,128)S(1)} custom-call(s32[4]{0:T(128)S(1)} %pad_add_fusion.place_ref.refs_0_.refs_10_, f32[2,384,128]{2,1,0:T(8,128)S(1)} %get-tuple-element.87.refs_1_.refs_5_, f32[2,192,128]{2,1,0:T(8,128)S(1)} %get-tuple-element.84.refs_2_, bf16[2,9,576,384]{3,2,1,0:T(8,128)(2,1)S(1)} %bitcast.28, ...), custom_call_target="tpu_custom_call" | custom-call | flops 1840000000 | tf_op jit(solution)/shard_map/second_ahead/pallas_call | solution.py:255
  32.3 2.8 %second.2 = (bf16[4,192,128]{2,1,0:T(8,128)(2,1)S(1)}, bf16[4,192,128]{2,1,0:T(8,128)(2,1)S(1)}) custom-call(s32[4]{0:T(128)S(1)} %pad_add_fusion.place_ref.refs_0_.refs_10_, f32[2,384,128]{2,1,0:T(8,128)S(1)} %get-tuple-element.87.refs_1_.refs_5_, f32[2,192,128]{2,1,0:T(8,128)S(1)} %get-tuple-element.84.refs_2_, bf16[2,9,576,384]{3,2,1,0:T(8,128)(2,1)S(1)} %bitcast.29, ...), custom_call_target="tpu_custom_call" | custom-call | flops 3449999872 | tf_op jit(solution)/shard_map/second/pallas_call | solution.py:255
  35.1 1.6 %collective-permute-start.12 = (bf16[4,192,128]{2,1,0:T(8,128)(2,1)S(1)}, bf16[4,192,128]{2,1,0:T(8,128)(2,1)S(1)}, u32[]{:S(2)}, u32[]{:S(2)}) collective-permute-start(bf16[4,192,128]{2,1,0:T(8,128)(2,1)S(1)} %get-tuple-element.81.refs_9_), channel_id=1, source_target_pairs={{0,2},{2,0},{1,3},{3,1},{4,6},{6,4},{5,7},{7,5},{8,10},{10,8},{9,1... | collective-permute-start | bytes 589832 | tf_op jit(solution)/shard_map/ppermute | solution.py:357
  36.7 4.0 %cached_rows.1 = (f32[6,192,128]{2,1,0:T(8,128)S(1)}, f32[2,192,128]{2,1,0:T(8,128)S(1)}) custom-call(bf16[6,192,128]{2,1,0:T(8,128)(2,1)S(1)} %pad_maximum_fusion.4.refs_4_.refs_0_, bf16[6,192,128]{2,1,0:T(8,128)(2,1)S(1)} %collective-permute-done.4.refs_5_.refs_1_, f32[2,192,128]{2,1,0:T(8,128)S(1)} %get-tuple-element.84.refs_2_, ...), custom_call_target="tpu_custom_call" | custom-call | flops 4600000000 | tf_op jit(solution)/shard_map/cached_rows/pallas_call | solution.py:255
  40.7 1.8 %collective-permute-done.12.refs_4_.refs_7_ = bf16[4,192,128]{2,1,0:T(8,128)(2,1)S(1)} collective-permute-done((bf16[4,192,128]{2,1,0:T(8,128)(2,1)S(1)}, bf16[4,192,128]{2,1,0:T(8,128)(2,1)S(1)}, u32[]{:S(2)}, u32[]{:S(2)}) %collective-permute-start.12) | collective-permute-done | bytes 196640 | tf_op jit(solution)/shard_map/ppermute | solution.py:357
  42.5 4.6 %collective-permute-start.16 = (bf16[4,192,128]{2,1,0:T(8,128)(2,1)S(1)}, bf16[4,192,128]{2,1,0:T(8,128)(2,1)S(1)}, u32[]{:S(2)}, u32[]{:S(2)}) collective-permute-start(bf16[4,192,128]{2,1,0:T(8,128)(2,1)S(1)} %collective-permute-done.12.refs_4_.refs_7_), channel_id=1, source_target_pairs={{0,8},{4,12},{8,0},{12,4},{16,24},{20,28},{24,16},{28,20},{1,9},{5... | collective-permute-start | bytes 589832 | tf_op jit(solution)/shard_map/ppermute | solution.py:288
  48.6 3.3 %collective-permute-done.16 = bf16[4,192,128]{2,1,0:T(8,128)(2,1)S(1)} collective-permute-done((bf16[4,192,128]{2,1,0:T(8,128)(2,1)S(1)}, bf16[4,192,128]{2,1,0:T(8,128)(2,1)S(1)}, u32[]{:S(2)}, u32[]{:S(2)}) %collective-permute-start.16) | collective-permute-done | bytes 196640 | tf_op jit(solution)/shard_map/ppermute | solution.py:288
  52.0 2.1 %collective-permute-done.14.refs_4_ = bf16[4,192,128]{2,1,0:T(8,128)(2,1)S(1)} collective-permute-done((bf16[4,192,128]{2,1,0:T(8,128)(2,1)S(1)}, bf16[4,192,128]{2,1,0:T(8,128)(2,1)S(1)}, u32[]{:S(2)}, u32[]{:S(2)}) %collective-permute-start.14) | collective-permute-done | bytes 196640 | tf_op jit(solution)/shard_map/ppermute | solution.py:288
  55.1 3.0 %own_row.3 = (f32[12,192,128]{2,1,0:T(8,128)S(1)}, bf16[2,192,128]{2,1,0:T(8,128)(2,1)S(1)}) custom-call(s32[4]{0:T(128)S(1)} %pad_add_fusion.place_ref.refs_0_.refs_10_, f32[2,384,128]{2,1,0:T(8,128)S(1)} %get-tuple-element.87.refs_1_.refs_5_, f32[2,192,128]{2,1,0:T(8,128)S(1)} %get-tuple-element.84.refs_2_, bf16[2,9,576,384]{3,2,1,0:T(8,128)(2,1)S(1)} %bitcast.31, ...), custom_call_target="tpu_custom_call" | custom-call | flops 3449999872 | tf_op jit(solution)/shard_map/own_row/pallas_call | solution.py:255
  58.1 3.7 %beside_rows.3 = (f32[8,192,128]{2,1,0:T(8,128)S(1)}, bf16[4,192,128]{2,1,0:T(8,128)(2,1)S(1)}) custom-call(s32[4]{0:T(128)S(1)} %pad_add_fusion.place_ref.refs_0_.refs_10_, f32[2,384,128]{2,1,0:T(8,128)S(1)} %get-tuple-element.87.refs_1_.refs_5_, f32[2,192,128]{2,1,0:T(8,128)S(1)} %get-tuple-element.84.refs_2_, bf16[2,9,576,384]{3,2,1,0:T(8,128)(2,1)S(1)} %bitcast.32, ...), custom_call_target="tpu_custom_call" | custom-call | flops 4255000064 | tf_op jit(solution)/shard_map/beside_rows/pallas_call | solution.py:255
  62.4 0.9 %collective-permute-done.21.refs_5_ = bf16[4,192,128]{2,1,0:T(8,128)(2,1)S(1)} collective-permute-done((bf16[4,192,128]{2,1,0:T(8,128)(2,1)S(1)}, bf16[4,192,128]{2,1,0:T(8,128)(2,1)S(1)}, u32[]{:S(2)}, u32[]{:S(2)}) %collective-permute-start.21) | collective-permute-done | bytes 196640 | tf_op jit(solution)/shard_map/ppermute | solution.py:269
  63.3 2.3 %far_row.3.refs_4_ = bf16[8,192,128]{2,1,0:T(8,128)(2,1)S(1)} custom-call(s32[4]{0:T(128)S(1)} %pad_add_fusion.place_ref.refs_0_.refs_10_, f32[2,384,128]{2,1,0:T(8,128)S(1)} %get-tuple-element.87.refs_1_.refs_5_, f32[2,192,128]{2,1,0:T(8,128)S(1)} %get-tuple-element.84.refs_2_, bf16[2,9,576,384]{3,2,1,0:T(8,128)(2,1)S(1)} %bitcast.33, ...), custom_call_target="tpu_custom_call" | custom-call | flops 2644999936 | tf_op jit(solution)/shard_map/far_row/pallas_call | solution.py:255
  65.9 1.6 %second_ahead.3.refs_6_ = f32[4,192,128]{2,1,0:T(8,128)S(1)} custom-call(s32[4]{0:T(128)S(1)} %pad_add_fusion.place_ref.refs_0_.refs_10_, f32[2,384,128]{2,1,0:T(8,128)S(1)} %get-tuple-element.87.refs_1_.refs_5_, f32[2,192,128]{2,1,0:T(8,128)S(1)} %get-tuple-element.84.refs_2_, bf16[2,9,576,384]{3,2,1,0:T(8,128)(2,1)S(1)} %bitcast.34, ...), custom_call_target="tpu_custom_call" | custom-call | flops 1840000000 | tf_op jit(solution)/shard_map/second_ahead/pallas_call | solution.py:255
  67.6 3.1 %second.3 = (bf16[4,192,128]{2,1,0:T(8,128)(2,1)}, bf16[4,192,128]{2,1,0:T(8,128)(2,1)}) custom-call(s32[4]{0:T(128)S(1)} %pad_add_fusion.place_ref.refs_0_.refs_10_, f32[2,384,128]{2,1,0:T(8,128)S(1)} %get-tuple-element.87.refs_1_.refs_5_, f32[2,192,128]{2,1,0:T(8,128)S(1)} %get-tuple-element.84.refs_2_, bf16[2,9,576,384]{3,2,1,0:T(8,128)(2,1)S(1)} %bitcast.35, ...), custom_call_target="tpu_custom_call" | custom-call | flops 3449999872 | tf_op jit(solution)/shard_map/second/pallas_call | solution.py:255
  (63 shorter events, 9.2 us)
Async XLA Ops:
  0.6 7.6 %copy-start.2 = (f32[1,2,384]{2,1,0:T(2,128)S(1)}, f32[1,2,384]{2,1,0:T(2,128)}, u32[]{:S(2)}) copy-start(f32[1,2,384]{2,1,0:T(2,128)} %param.9) | copy-start | bytes 9220
  1.8 13.7 %collective-permute-start.3 = (bf16[8,192,128]{2,1,0:T(8,128)(2,1)S(1)}, bf16[8,192,128]{2,1,0:T(8,128)(2,1)S(1)}, u32[]{:S(2)}, u32[]{:S(2)}) collective-permute-start(bf16[8,192,128]{2,1,0:T(8,128)(2,1)S(1)} %pad_maximum_fusion.1), channel_id=1, source_target_pairs={{0,4},{4,0},{8,12},{12,8},{16,20},{20,16},{24,28},{28,24},{1,5},{5... | collective-permute-start | bytes 1179656 | tf_op jit(solution)/shard_map/ppermute | solution.py:288
  4.8 10.6 %collective-permute-start.1 = (bf16[8,192,128]{2,1,0:T(8,128)(2,1)S(1)}, bf16[8,192,128]{2,1,0:T(8,128)(2,1)S(1)}, u32[]{:S(2)}, u32[]{:S(2)}) collective-permute-start(bf16[8,192,128]{2,1,0:T(8,128)(2,1)S(1)} %pad_maximum_fusion.1), channel_id=1, source_target_pairs={{0,8},{4,12},{8,0},{12,4},{16,24},{20,28},{24,16},{28,20},{1,9},{5... | collective-permute-start | bytes 1179656 | tf_op jit(solution)/shard_map/ppermute | solution.py:288
  6.3 9.0 %collective-permute-start = (bf16[8,192,128]{2,1,0:T(8,128)(2,1)S(1)}, bf16[8,192,128]{2,1,0:T(8,128)(2,1)S(1)}, u32[]{:S(2)}, u32[]{:S(2)}) collective-permute-start(bf16[8,192,128]{2,1,0:T(8,128)(2,1)S(1)} %pad_maximum_fusion.1), channel_id=1, source_target_pairs={{8,16},{12,20},{16,8},{20,12},{9,17},{13,21},{17,9},{21,13},{10,18... | collective-permute-start | bytes 1179656 | tf_op jit(solution)/shard_map/ppermute | solution.py:288
  8.0 7.6 %collective-permute-start.2 = (bf16[6,192,128]{2,1,0:T(8,128)(2,1)S(1)}, bf16[6,192,128]{2,1,0:T(8,128)(2,1)S(1)}, u32[]{:S(2)}, u32[]{:S(2)}) collective-permute-start(bf16[6,192,128]{2,1,0:T(8,128)(2,1)S(1)} %pad_maximum_fusion.3.refs_4_.refs_7_.refs_6_), channel_id=1, source_target_pairs={{0,1},{1,0},{2,3},{3,2},{4,5},{5,4},{6,7},{7,6},{8,9},{9,8},{10,11... | collective-permute-start | bytes 884744 | tf_op jit(solution)/shard_map/ppermute | solution.py:269
  15.7 4.4 %collective-permute-start.5 = (bf16[12,192,128]{2,1,0:T(8,128)(2,1)S(1)}, bf16[12,192,128]{2,1,0:T(8,128)(2,1)S(1)}, u32[]{:S(2)}, u32[]{:S(2)}) collective-permute-start(bf16[12,192,128]{2,1,0:T(8,128)(2,1)S(1)} %pad_maximum_fusion.refs_6_.refs_8_), channel_id=1, source_target_pairs={{0,1},{1,0},{2,3},{3,2},{4,5},{5,4},{6,7},{7,6},{8,9},{9,8},{10,11... | collective-permute-start | bytes 1769480 | tf_op jit(solution)/shard_map/ppermute | solution.py:269
  15.8 4.3 %collective-permute-start.4 = (bf16[6,192,128]{2,1,0:T(8,128)(2,1)S(1)}, bf16[6,192,128]{2,1,0:T(8,128)(2,1)S(1)}, u32[]{:S(2)}, u32[]{:S(2)}) collective-permute-start(bf16[6,192,128]{2,1,0:T(8,128)(2,1)S(1)} %pad_maximum_fusion.4.refs_4_.refs_0_), channel_id=1, source_target_pairs={{0,1},{1,0},{2,3},{3,2},{4,5},{5,4},{6,7},{7,6},{8,9},{9,8},{10,11... | collective-permute-start | bytes 884744 | tf_op jit(solution)/shard_map/ppermute | solution.py:269
  16.3 9.1 %collective-permute-start.7 = (bf16[6,192,128]{2,1,0:T(8,128)(2,1)S(1)}, bf16[6,192,128]{2,1,0:T(8,128)(2,1)S(1)}, u32[]{:S(2)}, u32[]{:S(2)}) collective-permute-start(bf16[6,192,128]{2,1,0:T(8,128)(2,1)S(1)} %pad_maximum_fusion.5), channel_id=1, source_target_pairs={{0,4},{4,0},{8,12},{12,8},{16,20},{20,16},{24,28},{28,24},{1,5},{5... | collective-permute-start | bytes 884744 | tf_op jit(solution)/shard_map/ppermute | solution.py:321
  25.3 1.6 %collective-permute-start.8 = (bf16[6,192,128]{2,1,0:T(8,128)(2,1)S(1)}, bf16[6,192,128]{2,1,0:T(8,128)(2,1)S(1)}, u32[]{:S(2)}, u32[]{:S(2)}) collective-permute-start(bf16[6,192,128]{2,1,0:T(8,128)(2,1)S(1)} %collective-permute-done.7.refs_4_.refs_3_), channel_id=1, source_target_pairs={{0,1},{1,0},{2,3},{3,2},{4,5},{5,4},{6,7},{7,6},{8,9},{9,8},{10,11... | collective-permute-start | bytes 884744 | tf_op jit(solution)/shard_map/ppermute | solution.py:269
  25.3 5.2 %collective-permute-start.10 = (bf16[2,192,128]{2,1,0:T(8,128)(2,1)S(1)}, bf16[2,192,128]{2,1,0:T(8,128)(2,1)S(1)}, u32[]{:S(2)}, u32[]{:S(2)}) collective-permute-start(bf16[2,192,128]{2,1,0:T(8,128)(2,1)S(1)} %get-tuple-element.80), channel_id=1, source_target_pairs={{0,4},{4,0},{8,12},{12,8},{16,20},{20,16},{24,28},{28,24},{1,5},{5... | collective-permute-start | bytes 294920 | tf_op jit(solution)/shard_map/ppermute | solution.py:337
  26.2 3.3 %collective-permute-start.6 = (bf16[4,192,128]{2,1,0:T(8,128)(2,1)S(1)}, bf16[4,192,128]{2,1,0:T(8,128)(2,1)S(1)}, u32[]{:S(2)}, u32[]{:S(2)}) collective-permute-start(bf16[4,192,128]{2,1,0:T(8,128)(2,1)S(1)} %get-tuple-element.75.refs_4_), channel_id=1, source_target_pairs={{0,1},{1,0},{2,3},{3,2},{4,5},{5,4},{6,7},{7,6},{8,9},{9,8},{10,11... | collective-permute-start | bytes 589832 | tf_op jit(solution)/shard_map/ppermute | solution.py:269
  29.5 2.9 %collective-permute-start.9 = (bf16[8,192,128]{2,1,0:T(8,128)(2,1)S(1)}, bf16[8,192,128]{2,1,0:T(8,128)(2,1)S(1)}, u32[]{:S(2)}, u32[]{:S(2)}) collective-permute-start(bf16[8,192,128]{2,1,0:T(8,128)(2,1)S(1)} %far_row.2.refs_4_), channel_id=1, source_target_pairs={{0,1},{1,0},{2,3},{3,2},{4,5},{5,4},{6,7},{7,6},{8,9},{9,8},{10,11... | collective-permute-start | bytes 1179656 | tf_op jit(solution)/shard_map/ppermute | solution.py:269
  30.6 1.7 %collective-permute-start.11 = (bf16[6,192,128]{2,1,0:T(8,128)(2,1)S(1)}, bf16[6,192,128]{2,1,0:T(8,128)(2,1)S(1)}, u32[]{:S(2)}, u32[]{:S(2)}) collective-permute-start(bf16[6,192,128]{2,1,0:T(8,128)(2,1)S(1)} %constant_dynamic-update-slice_fusion.refs_9_.refs_11_), channel_id=1, source_target_pairs={{0,1},{1,0},{2,3},{3,2},{4,5},{5,4},{6,7},{7,6},{8,9},{9,8},{10,11... | collective-permute-start | bytes 884744 | tf_op jit(solution)/shard_map/ppermute | solution.py:269
  35.1 7.4 %collective-permute-start.12 = (bf16[4,192,128]{2,1,0:T(8,128)(2,1)S(1)}, bf16[4,192,128]{2,1,0:T(8,128)(2,1)S(1)}, u32[]{:S(2)}, u32[]{:S(2)}) collective-permute-start(bf16[4,192,128]{2,1,0:T(8,128)(2,1)S(1)} %get-tuple-element.81.refs_9_), channel_id=1, source_target_pairs={{0,2},{2,0},{1,3},{3,1},{4,6},{6,4},{5,7},{7,5},{8,10},{10,8},{9,1... | collective-permute-start | bytes 589832 | tf_op jit(solution)/shard_map/ppermute | solution.py:357
  42.5 9.4 %collective-permute-start.16 = (bf16[4,192,128]{2,1,0:T(8,128)(2,1)S(1)}, bf16[4,192,128]{2,1,0:T(8,128)(2,1)S(1)}, u32[]{:S(2)}, u32[]{:S(2)}) collective-permute-start(bf16[4,192,128]{2,1,0:T(8,128)(2,1)S(1)} %collective-permute-done.12.refs_4_.refs_7_), channel_id=1, source_target_pairs={{0,8},{4,12},{8,0},{12,4},{16,24},{20,28},{24,16},{28,20},{1,9},{5... | collective-permute-start | bytes 589832 | tf_op jit(solution)/shard_map/ppermute | solution.py:288
  47.1 4.8 %collective-permute-start.15 = (bf16[4,192,128]{2,1,0:T(8,128)(2,1)S(1)}, bf16[4,192,128]{2,1,0:T(8,128)(2,1)S(1)}, u32[]{:S(2)}, u32[]{:S(2)}) collective-permute-start(bf16[4,192,128]{2,1,0:T(8,128)(2,1)S(1)} %collective-permute-done.12.refs_4_.refs_7_), channel_id=1, source_target_pairs={{8,16},{12,20},{16,8},{20,12},{9,17},{13,21},{17,9},{21,13},{10,18... | collective-permute-start | bytes 589832 | tf_op jit(solution)/shard_map/ppermute | solution.py:288
  47.8 6.3 %collective-permute-start.14 = (bf16[4,192,128]{2,1,0:T(8,128)(2,1)S(1)}, bf16[4,192,128]{2,1,0:T(8,128)(2,1)S(1)}, u32[]{:S(2)}, u32[]{:S(2)}) collective-permute-start(bf16[4,192,128]{2,1,0:T(8,128)(2,1)S(1)} %collective-permute-done.12.refs_4_.refs_7_), channel_id=1, source_target_pairs={{0,4},{4,0},{8,12},{12,8},{16,20},{20,16},{24,28},{28,24},{1,5},{5... | collective-permute-start | bytes 589832 | tf_op jit(solution)/shard_map/ppermute | solution.py:288
  48.6 5.5 %collective-permute-start.13 = (bf16[4,192,128]{2,1,0:T(8,128)(2,1)S(1)}, bf16[4,192,128]{2,1,0:T(8,128)(2,1)S(1)}, u32[]{:S(2)}, u32[]{:S(2)}) collective-permute-start(bf16[4,192,128]{2,1,0:T(8,128)(2,1)S(1)} %collective-permute-done.12.refs_4_.refs_7_), channel_id=1, source_target_pairs={{0,1},{1,0},{2,3},{3,2},{4,5},{5,4},{6,7},{7,6},{8,9},{9,8},{10,11... | collective-permute-start | bytes 589832 | tf_op jit(solution)/shard_map/ppermute | solution.py:269
  54.1 4.0 %collective-permute-start.18 = (bf16[8,192,128]{2,1,0:T(8,128)(2,1)S(1)}, bf16[8,192,128]{2,1,0:T(8,128)(2,1)S(1)}, u32[]{:S(2)}, u32[]{:S(2)}) collective-permute-start(bf16[8,192,128]{2,1,0:T(8,128)(2,1)S(1)} %pad_maximum_fusion.2.refs_6_), channel_id=1, source_target_pairs={{0,1},{1,0},{2,3},{3,2},{4,5},{5,4},{6,7},{7,6},{8,9},{9,8},{10,11... | collective-permute-start | bytes 1179656 | tf_op jit(solution)/shard_map/ppermute | solution.py:269
  54.1 7.7 %collective-permute-start.20 = (bf16[4,192,128]{2,1,0:T(8,128)(2,1)S(1)}, bf16[4,192,128]{2,1,0:T(8,128)(2,1)S(1)}, u32[]{:S(2)}, u32[]{:S(2)}) collective-permute-start(bf16[4,192,128]{2,1,0:T(8,128)(2,1)S(1)} %get-tuple-element.120), channel_id=1, source_target_pairs={{0,4},{4,0},{8,12},{12,8},{16,20},{20,16},{24,28},{28,24},{1,5},{5... | collective-permute-start | bytes 589832 | tf_op jit(solution)/shard_map/ppermute | solution.py:321
  54.9 3.2 %collective-permute-start.17 = (bf16[4,192,128]{2,1,0:T(8,128)(2,1)S(1)}, bf16[4,192,128]{2,1,0:T(8,128)(2,1)S(1)}, u32[]{:S(2)}, u32[]{:S(2)}) collective-permute-start(bf16[4,192,128]{2,1,0:T(8,128)(2,1)S(1)} %collective-permute-done.14.refs_4_), channel_id=1, source_target_pairs={{0,1},{1,0},{2,3},{3,2},{4,5},{5,4},{6,7},{7,6},{8,9},{9,8},{10,11... | collective-permute-start | bytes 589832 | tf_op jit(solution)/shard_map/ppermute | solution.py:269
  61.8 1.5 %collective-permute-start.21 = (bf16[4,192,128]{2,1,0:T(8,128)(2,1)S(1)}, bf16[4,192,128]{2,1,0:T(8,128)(2,1)S(1)}, u32[]{:S(2)}, u32[]{:S(2)}) collective-permute-start(bf16[4,192,128]{2,1,0:T(8,128)(2,1)S(1)} %collective-permute-done.20.refs_4_), channel_id=1, source_target_pairs={{0,1},{1,0},{2,3},{3,2},{4,5},{5,4},{6,7},{7,6},{8,9},{9,8},{10,11... | collective-permute-start | bytes 589832 | tf_op jit(solution)/shard_map/ppermute | solution.py:269
  62.2 3.4 %collective-permute-start.19 = (bf16[4,192,128]{2,1,0:T(8,128)(2,1)S(1)}, bf16[4,192,128]{2,1,0:T(8,128)(2,1)S(1)}, u32[]{:S(2)}, u32[]{:S(2)}) collective-permute-start(bf16[4,192,128]{2,1,0:T(8,128)(2,1)S(1)} %get-tuple-element.109.refs_4_), channel_id=1, source_target_pairs={{0,1},{1,0},{2,3},{3,2},{4,5},{5,4},{6,7},{7,6},{8,9},{9,8},{10,11... | collective-permute-start | bytes 589832 | tf_op jit(solution)/shard_map/ppermute | solution.py:269
  65.6 2.0 %collective-permute-start.22 = (bf16[8,192,128]{2,1,0:T(8,128)(2,1)S(1)}, bf16[8,192,128]{2,1,0:T(8,128)(2,1)S(1)}, u32[]{:S(2)}, u32[]{:S(2)}) collective-permute-start(bf16[8,192,128]{2,1,0:T(8,128)(2,1)S(1)} %far_row.3.refs_4_), channel_id=1, source_target_pairs={{0,1},{1,0},{2,3},{3,2},{4,5},{5,4},{6,7},{7,6},{8,9},{9,8},{10,11... | collective-permute-start | bytes 1179656 | tf_op jit(solution)/shard_map/ppermute | solution.py:269
  (4 other events, 23.4 us)
